TPU v7x, 32 devices: a whole 2x2x4 slice. The times are simulated.
32 devices in a mesh: ctx: 8 (over z, y), fsdp: 4 (over x, core).
Axes of the slice: x: 2, y: 2, z: 4, core: 2. Of those that a mesh axis runs over, the one named last changes fastest.
Arguments:
- tokens: bfloat16 [4, 2048, 768], P('fsdp', 'ctx'), may hold values from -6 to 6
- cotangent: bfloat16 [4, 2048, 768], P('fsdp', 'ctx'), may hold values from -6 to 6
- lengths: int32 [4], P('fsdp'), may hold values from 512 to 2048, as said below
- pairing: int32 [16], replicated, may hold values from 0 to 15, as said below
- w_qkv: bfloat16 [768, 2304], P('fsdp'), may hold values from -0.21875 to 0.21875
- bias_q: bfloat16 [768], P('fsdp'), may hold values from -3 to 3
- bias_v: bfloat16 [768], P('fsdp'), may hold values from -3 to 3
- w_out: bfloat16 [768, 768], P('fsdp'), may hold values from -6 to 6
- bias_out: bfloat16 [768], P('fsdp'), may hold values from -3 to 3
- ln1_gain: bfloat16 [768], P('fsdp'), may hold values from 0.099609375 to 1.8984375
- ln1_bias: bfloat16 [768], P('fsdp'), may hold values from -3 to 3
- w_in: bfloat16 [768, 3072], P('fsdp'), may hold values from -0.21875 to 0.21875
- bias_in: bfloat16 [3072], P('fsdp'), may hold values from -3 to 3
- w_back: bfloat16 [3072, 768], P('fsdp'), may hold values from -0.109375 to 0.109375
- bias_back: bfloat16 [768], P('fsdp'), may hold values from -3 to 3
- ln2_gain: bfloat16 [768], P('fsdp'), may hold values from 0.099609375 to 1.8984375
- ln2_bias: bfloat16 [768], P('fsdp'), may hold values from -3 to 3
Outputs:
- output: float32 [4, 2048, 768], P('fsdp', 'ctx')
- token_grad: float32 [4, 2048, 768], P('fsdp', 'ctx')
- w_qkv_grad: float32 [768, 2304], P('fsdp')
- bias_q_grad: float32 [768], P('fsdp')
- bias_v_grad: float32 [768], P('fsdp')
- w_out_grad: float32 [768, 768], P('fsdp')
- bias_out_grad: float32 [768], P('fsdp')
- ln1_gain_grad: float32 [768], P('fsdp')
- ln1_bias_grad: float32 [768], P('fsdp')
- w_in_grad: float32 [768, 3072], P('fsdp')
- bias_in_grad: float32 [3072], P('fsdp')
- w_back_grad: float32 [3072, 768], P('fsdp')
- bias_back_grad: float32 [768], P('fsdp')
- ln2_gain_grad: float32 [768], P('fsdp')
- ln2_bias_grad: float32 [768], P('fsdp')
Inputs may be any that keep to these rules, and one draw needn't show every extreme that they name: `lengths`: every draw has a sequence that fills all 2048 slots. `pairing`: ctx index i stores storage blocks 2i and 2i + 1, which are the sequence's blocks t and 15 - t for some t; each block appears once.
All inputs are finite; a program needn't handle non-finite values.
Results may differ from a plain program's by a relative error of at most 0.02.
Values may be sent and summed in bfloat16 or wider, within the bound.
A program may use at most 192 MiB of HBM per device.

v0:
```python
import math

import jax
import jax.numpy as jnp
from jax import lax
from jax.sharding import PartitionSpec as P

HEADS = 12
HEAD_DIM = 64
NMEM = 10


eps = 1e-12
neg_big = -1e30


def layer_norm(value, gain, shift):
    mean = jnp.mean(value, axis=-1, keepdims=True)
    centred = value - mean
    variance = jnp.mean(centred * centred, axis=-1, keepdims=True)
    return centred * lax.rsqrt(variance + eps) * gain + shift


def norm_back(value, gain, grad):
    mean = jnp.mean(value, axis=-1, keepdims=True)
    centred = value - mean
    scale = lax.rsqrt(jnp.mean(centred * centred, axis=-1, keepdims=True) + eps)
    unit = centred * scale
    scaled = grad * gain
    inner = (
        scaled
        - jnp.mean(scaled, axis=-1, keepdims=True)
        - unit * jnp.mean(scaled * unit, axis=-1, keepdims=True)
    )
    return (scale * inner, jnp.sum(grad * unit, axis=0), jnp.sum(grad, axis=0))


def block_width(count):
    return math.gcd(count, 512)


def places(pairing, start, count, half):
    rows = start + jnp.arange(count, dtype=jnp.int32)
    owners = rows // half
    spots = jnp.arange(pairing.shape[0], dtype=jnp.int32)
    picked = jnp.sum(jnp.where(owners[:, None] == spots[None, :], pairing[None, :], 0), axis=1)
    return picked * half + rows % half


def allowed_pairs(query_place, key_place, length):
    before = (key_place[None, :] <= query_place[:, None]) | (key_place[None, :] < NMEM)
    return (key_place[None, :] < length) & before


def heads_of(value):
    return value.reshape(value.shape[0], HEADS, HEAD_DIM)


def forward_fold(query_heads, query_place, pairing, length, half):

    def fold(carry, piece, start):
        keys, values = piece
        count = keys.shape[0]
        width = block_width(count)
        key_place = places(pairing, start, count, half)

        def step(index, state):
            top, total, summed = state
            offset = index * width
            key_heads = heads_of(lax.dynamic_slice_in_dim(keys, offset, width, 0))
            value_heads = heads_of(lax.dynamic_slice_in_dim(values, offset, width, 0))
            mask = allowed_pairs(
                query_place, lax.dynamic_slice_in_dim(key_place, offset, width, 0), length
            )[None]
            scores = (
                jnp.einsum(
                    "qhd,khd->hqk", query_heads, key_heads, preferred_element_type=jnp.float32
                )
                * 0.125
            )
            scores = jnp.where(mask, scores, neg_big)
            new_top = jnp.maximum(top, jnp.max(scores, axis=2))
            shrink = jnp.exp(top - new_top)
            probs = jnp.where(mask, jnp.exp(scores - new_top[:, :, None]), 0.0)
            total = total * shrink + jnp.sum(probs, axis=2)
            update = jnp.einsum(
                "hqk,khd->qhd",
                probs.astype(jnp.bfloat16),
                value_heads,
                preferred_element_type=jnp.float32,
            )
            summed = summed * jnp.transpose(shrink)[:, :, None] + update
            return (new_top, total, summed)

        return lax.fori_loop(0, count // width, step, carry)

    return fold


def query_grad_fold(query_heads, grad_heads, top_sum, delta, query_place, pairing, length, half):

    def fold(carry, piece, start):
        keys, values = piece
        count = keys.shape[0]
        width = block_width(count)
        key_place = places(pairing, start, count, half)

        def step(index, summed):
            offset = index * width
            key_heads = heads_of(lax.dynamic_slice_in_dim(keys, offset, width, 0))
            value_heads = heads_of(lax.dynamic_slice_in_dim(values, offset, width, 0))
            mask = allowed_pairs(
                query_place, lax.dynamic_slice_in_dim(key_place, offset, width, 0), length
            )[None]
            scores = (
                jnp.einsum(
                    "qhd,khd->hqk", query_heads, key_heads, preferred_element_type=jnp.float32
                )
                * 0.125
            )
            probs = jnp.where(mask, jnp.exp(scores - top_sum[:, :, None]), 0.0)
            prob_grad = jnp.einsum(
                "qhd,khd->hqk", grad_heads, value_heads, preferred_element_type=jnp.float32
            )
            score_grad = (probs * (prob_grad - delta[:, :, None])).astype(jnp.bfloat16)
            return (
                summed
                + jnp.einsum(
                    "hqk,khd->qhd", score_grad, key_heads, preferred_element_type=jnp.float32
                )
                * 0.125
            )

        return lax.fori_loop(0, count // width, step, carry)

    return fold


def key_terms(
    key_heads, value_heads, key_place, query_heads, grad_heads, top_sum, delta, query_place, length
):
    scores = (
        jnp.einsum("qhd,khd->hqk", query_heads, key_heads, preferred_element_type=jnp.float32)
        * 0.125
    )
    mask = allowed_pairs(query_place, key_place, length)[None]
    probs = jnp.where(mask, jnp.exp(scores - top_sum[:, :, None]), 0.0)
    prob_grad = jnp.einsum(
        "qhd,khd->hqk", grad_heads, value_heads, preferred_element_type=jnp.float32
    )
    score_grad = (probs * (prob_grad - delta[:, :, None])).astype(jnp.bfloat16)
    value_grad = jnp.einsum(
        "hqk,qhd->khd", probs.astype(jnp.bfloat16), grad_heads, preferred_element_type=jnp.float32
    )
    key_grad = (
        jnp.einsum("hqk,qhd->khd", score_grad, query_heads, preferred_element_type=jnp.float32)
        * 0.125
    )
    return (key_grad, value_grad)


def on_device(
    tokens,
    cotangent,
    lengths,
    pairing,
    w_qkv,
    bias_q,
    bias_v,
    w_out,
    bias_out,
    ln1_gain,
    ln1_bias,
    w_in,
    bias_in,
    w_back,
    bias_back,
    ln2_gain,
    ln2_bias,
):
    gathered = (
        lax.all_gather(w_qkv, "fsdp", axis=0, tiled=True),
        lax.all_gather(bias_q, "fsdp", axis=0, tiled=True),
        lax.all_gather(bias_v, "fsdp", axis=0, tiled=True),
        lax.all_gather(w_out, "fsdp", axis=0, tiled=True),
        lax.all_gather(bias_out, "fsdp", axis=0, tiled=True),
        lax.all_gather(ln1_gain, "fsdp", axis=0, tiled=True),
        lax.all_gather(ln1_bias, "fsdp", axis=0, tiled=True),
        lax.all_gather(w_in, "fsdp", axis=0, tiled=True),
        lax.all_gather(bias_in, "fsdp", axis=0, tiled=True),
        lax.all_gather(w_back, "fsdp", axis=0, tiled=True),
        lax.all_gather(bias_back, "fsdp", axis=0, tiled=True),
        lax.all_gather(ln2_gain, "fsdp", axis=0, tiled=True),
        lax.all_gather(ln2_bias, "fsdp", axis=0, tiled=True),
    )
    (
        qkv_all,
        query_bias,
        value_bias,
        out_all,
        out_bias,
        gain_one,
        shift_one,
        in_all,
        in_bias,
        back_all,
        back_bias,
        gain_two,
        shift_two,
    ) = gathered
    rows = tokens.shape[1]
    half = rows // 2
    width = tokens.shape[2]
    length = lengths[0]
    query_place = places(pairing, lax.axis_index("ctx") * rows, rows, half)
    valid = query_place < length
    inputs = tokens[0]
    proj = jnp.dot(inputs, qkv_all, preferred_element_type=jnp.float32)
    queries = (proj[:, :width] + query_bias.astype(jnp.float32)).astype(jnp.bfloat16)
    keys = proj[:, width : 2 * width].astype(jnp.bfloat16)
    values = (proj[:, 2 * width :] + value_bias.astype(jnp.float32)).astype(jnp.bfloat16)
    query_heads = heads_of(queries)
    start_state = (
        jnp.full((HEADS, rows), neg_big, jnp.float32),
        jnp.zeros((HEADS, rows), jnp.float32),
        jnp.zeros((rows, HEADS, HEAD_DIM), jnp.float32),
    )
    fold = forward_fold(query_heads, query_place, pairing, length, half)
    top, total, summed = fold(
        start_state,
        (
            lax.all_gather(keys, "ctx", axis=0, tiled=True),
            lax.all_gather(values, "ctx", axis=0, tiled=True),
        ),
        jnp.int32(0),
    )
    top_sum = top + jnp.log(total)
    attended = (summed / jnp.transpose(total)[:, :, None]).reshape(rows, width)
    attended_low = attended.astype(jnp.bfloat16)
    resid_one = (
        inputs.astype(jnp.float32)
        + jnp.dot(attended_low, out_all, preferred_element_type=jnp.float32)
        + out_bias.astype(jnp.float32)
    )
    hidden = layer_norm(resid_one, gain_one.astype(jnp.float32), shift_one.astype(jnp.float32))
    hidden_low = hidden.astype(jnp.bfloat16)
    upper = jnp.dot(hidden_low, in_all, preferred_element_type=jnp.float32) + in_bias.astype(
        jnp.float32
    )
    active, gelu_back = jax.vjp(lambda value: jax.nn.gelu(value, approximate=False), upper)
    active_low = active.astype(jnp.bfloat16)
    resid_two = (
        hidden
        + jnp.dot(active_low, back_all, preferred_element_type=jnp.float32)
        + back_bias.astype(jnp.float32)
    )
    normed = layer_norm(resid_two, gain_two.astype(jnp.float32), shift_two.astype(jnp.float32))
    output = jnp.where(valid[:, None], normed, 0.0)
    qkv_back, out_back, gain_one_back, in_back, back_back, gain_two_back = (
        qkv_all,
        out_all,
        gain_one,
        in_all,
        back_all,
        gain_two,
    )
    grad_y = jnp.where(valid[:, None], cotangent[0].astype(jnp.float32), 0.0)
    grad_resid_two, gain_two_grad, shift_two_grad = norm_back(
        resid_two, gain_two_back.astype(jnp.float32), grad_y
    )
    grad_mixed = grad_resid_two.astype(jnp.bfloat16)
    back_grad = jnp.einsum("tf,td->fd", active_low, grad_mixed, preferred_element_type=jnp.float32)
    back_bias_grad = jnp.sum(grad_mixed.astype(jnp.float32), axis=0)
    grad_active = jnp.einsum("td,fd->tf", grad_mixed, back_back, preferred_element_type=jnp.float32)
    (grad_upper,) = gelu_back(grad_active)
    grad_upper_low = grad_upper.astype(jnp.bfloat16)
    in_grad = jnp.einsum(
        "td,tf->df", hidden_low, grad_upper_low, preferred_element_type=jnp.float32
    )
    in_bias_grad = jnp.sum(grad_upper_low.astype(jnp.float32), axis=0)
    grad_hidden = grad_resid_two + jnp.einsum(
        "tf,df->td", grad_upper_low, in_back, preferred_element_type=jnp.float32
    )
    grad_resid_one, gain_one_grad, shift_one_grad = norm_back(
        resid_one, gain_one_back.astype(jnp.float32), grad_hidden
    )
    grad_branch = grad_resid_one.astype(jnp.bfloat16)
    out_grad = jnp.einsum(
        "tc,td->cd", attended_low, grad_branch, preferred_element_type=jnp.float32
    )
    out_bias_grad = jnp.sum(grad_branch.astype(jnp.float32), axis=0)
    grad_attended = jnp.einsum(
        "td,cd->tc", grad_branch, out_back, preferred_element_type=jnp.float32
    ).astype(jnp.bfloat16)
    grad_heads = heads_of(grad_attended)
    delta = jnp.transpose(jnp.sum(grad_heads.astype(jnp.float32) * heads_of(attended), axis=2))
    query_fold = query_grad_fold(
        query_heads, grad_heads, top_sum, delta, query_place, pairing, length, half
    )
    empty_heads = jnp.zeros((rows, HEADS, HEAD_DIM), jnp.float32)
    query_grad = query_fold(
        empty_heads,
        (
            lax.all_gather(keys, "ctx", axis=0, tiled=True),
            lax.all_gather(values, "ctx", axis=0, tiled=True),
        ),
        jnp.int32(0),
    )
    stats = jnp.concatenate([jnp.transpose(top_sum), jnp.transpose(delta)], axis=1)
    stats_all = lax.all_gather(stats, "ctx", axis=0, tiled=True)
    key_heads = heads_of(keys)
    value_heads = heads_of(values)
    query_in = lax.all_gather(queries, "ctx", axis=0, tiled=True)
    grad_in = lax.all_gather(grad_attended, "ctx", axis=0, tiled=True)
    count = query_in.shape[0]
    span = block_width(count)
    place_in = places(pairing, jnp.int32(0), count, half)

    def step(index, state):
        offset = index * span
        query_block = heads_of(lax.dynamic_slice_in_dim(query_in, offset, span, 0))
        grad_block = heads_of(lax.dynamic_slice_in_dim(grad_in, offset, span, 0))
        stats_block = lax.dynamic_slice_in_dim(stats_all, offset, span, 0)
        place_block = lax.dynamic_slice_in_dim(place_in, offset, span, 0)
        key_part, value_part = key_terms(
            key_heads,
            value_heads,
            query_place,
            query_block,
            grad_block,
            jnp.transpose(stats_block[:, :HEADS]),
            jnp.transpose(stats_block[:, HEADS:]),
            place_block,
            length,
        )
        return (state[0] + key_part, state[1] + value_part)

    key_sum, value_sum = lax.fori_loop(0, count // span, step, (empty_heads, empty_heads))
    key_grad = key_sum.reshape(rows, width)
    value_grad = value_sum.reshape(rows, width)
    grad_proj = jnp.concatenate(
        [
            query_grad.reshape(rows, width).astype(jnp.bfloat16),
            key_grad.astype(jnp.bfloat16),
            value_grad.astype(jnp.bfloat16),
        ],
        axis=1,
    )
    qkv_grad = jnp.einsum("td,tf->df", inputs, grad_proj, preferred_element_type=jnp.float32)
    query_bias_grad = jnp.sum(grad_proj[:, :width].astype(jnp.float32), axis=0)
    value_bias_grad = jnp.sum(grad_proj[:, 2 * width :].astype(jnp.float32), axis=0)
    token_grad = grad_resid_one + jnp.einsum(
        "tf,df->td", grad_proj, qkv_back, preferred_element_type=jnp.float32
    )
    grads = (
        qkv_grad,
        query_bias_grad,
        value_bias_grad,
        out_grad,
        out_bias_grad,
        gain_one_grad,
        shift_one_grad,
        in_grad,
        in_bias_grad,
        back_grad,
        back_bias_grad,
        gain_two_grad,
        shift_two_grad,
    )
    shards = (
        lax.psum_scatter(
            grads[0].astype(jnp.bfloat16), "fsdp", scatter_dimension=0, tiled=True
        ).astype(jnp.float32),
        lax.psum_scatter(
            grads[1].astype(jnp.bfloat16), "fsdp", scatter_dimension=0, tiled=True
        ).astype(jnp.float32),
        lax.psum_scatter(
            grads[2].astype(jnp.bfloat16), "fsdp", scatter_dimension=0, tiled=True
        ).astype(jnp.float32),
        lax.psum_scatter(
            grads[3].astype(jnp.bfloat16), "fsdp", scatter_dimension=0, tiled=True
        ).astype(jnp.float32),
        lax.psum_scatter(
            grads[4].astype(jnp.bfloat16), "fsdp", scatter_dimension=0, tiled=True
        ).astype(jnp.float32),
        lax.psum_scatter(
            grads[5].astype(jnp.bfloat16), "fsdp", scatter_dimension=0, tiled=True
        ).astype(jnp.float32),
        lax.psum_scatter(
            grads[6].astype(jnp.bfloat16), "fsdp", scatter_dimension=0, tiled=True
        ).astype(jnp.float32),
        lax.psum_scatter(
            grads[7].astype(jnp.bfloat16), "fsdp", scatter_dimension=0, tiled=True
        ).astype(jnp.float32),
        lax.psum_scatter(
            grads[8].astype(jnp.bfloat16), "fsdp", scatter_dimension=0, tiled=True
        ).astype(jnp.float32),
        lax.psum_scatter(
            grads[9].astype(jnp.bfloat16), "fsdp", scatter_dimension=0, tiled=True
        ).astype(jnp.float32),
        lax.psum_scatter(
            grads[10].astype(jnp.bfloat16), "fsdp", scatter_dimension=0, tiled=True
        ).astype(jnp.float32),
        lax.psum_scatter(
            grads[11].astype(jnp.bfloat16), "fsdp", scatter_dimension=0, tiled=True
        ).astype(jnp.float32),
        lax.psum_scatter(
            grads[12].astype(jnp.bfloat16), "fsdp", scatter_dimension=0, tiled=True
        ).astype(jnp.float32),
    )
    totals = (
        lax.psum(shards[0].astype(jnp.bfloat16), "ctx").astype(jnp.float32),
        lax.psum(shards[1].astype(jnp.bfloat16), "ctx").astype(jnp.float32),
        lax.psum(shards[2].astype(jnp.bfloat16), "ctx").astype(jnp.float32),
        lax.psum(shards[3].astype(jnp.bfloat16), "ctx").astype(jnp.float32),
        lax.psum(shards[4].astype(jnp.bfloat16), "ctx").astype(jnp.float32),
        lax.psum(shards[5].astype(jnp.bfloat16), "ctx").astype(jnp.float32),
        lax.psum(shards[6].astype(jnp.bfloat16), "ctx").astype(jnp.float32),
        lax.psum(shards[7].astype(jnp.bfloat16), "ctx").astype(jnp.float32),
        lax.psum(shards[8].astype(jnp.bfloat16), "ctx").astype(jnp.float32),
        lax.psum(shards[9].astype(jnp.bfloat16), "ctx").astype(jnp.float32),
        lax.psum(shards[10].astype(jnp.bfloat16), "ctx").astype(jnp.float32),
        lax.psum(shards[11].astype(jnp.bfloat16), "ctx").astype(jnp.float32),
        lax.psum(shards[12].astype(jnp.bfloat16), "ctx").astype(jnp.float32),
    )
    return (output[None], token_grad[None]) + tuple(totals)


def solution(mesh):
    return jax.shard_map(
        on_device,
        mesh=mesh,
        in_specs=(
            P("fsdp", "ctx", None),
            P("fsdp", "ctx", None),
            P("fsdp"),
            P(),
            P("fsdp", None),
            P("fsdp"),
            P("fsdp"),
            P("fsdp", None),
            P("fsdp"),
            P("fsdp"),
            P("fsdp"),
            P("fsdp", None),
            P("fsdp"),
            P("fsdp", None),
            P("fsdp"),
            P("fsdp"),
            P("fsdp"),
        ),
        out_specs=(
            P("fsdp", "ctx", None),
            P("fsdp", "ctx", None),
            P("fsdp", None),
            P("fsdp"),
            P("fsdp"),
            P("fsdp", None),
            P("fsdp"),
            P("fsdp"),
            P("fsdp"),
            P("fsdp", None),
            P("fsdp"),
            P("fsdp", None),
            P("fsdp"),
            P("fsdp"),
            P("fsdp"),
        ),
        check_vma=False,
    )
```

profile of v0, /device:TPU:0, one launch (start us, length us, event | category | flops | bytes accessed | tf_op | source)
XLA Modules:
  0.0 828.1 jit_solution(17585066011576581938)
XLA Ops:
  15.8 13.4 %all-reduce.20 = (bf16[768]{0:T(1024)(128)(2,1)S(1)}, bf16[768]{0:T(1024)(128)(2,1)S(1)}, bf16[768]{0:T(1024)(128)(2,1)S(1)}, bf16[768]{0:T(1024)(128)(2,1)S(1)}...) all-reduce(bf16[768]{0:T(1024)(128)(2,1)S(1)} %dynamic-update-slice, ...), channel_id=1, replica_groups=mesh['ctx'=8,'fsdp'=4] {'fsdp'}, use_global_device_ids=true, to_apply=%add | all-reduce | flops 5376 | bytes 21504
  29.2 14.1 %all-gather.10.cloned.1.call-done = bf16[768,2304]{1,0:T(8,128)(2,1)} async-done(((bf16[192,2304]{1,0:T(8,128)(2,1)}), bf16[768,2304]{1,0:T(8,128)(2,1)}) %all-gather.10.cloned.1.call-update) | async-done | bytes 3538960 | tf_op jit(solution)/shard_map/all_gather | solution.py:182
  50.8 5.2 all-gather
  58.2 49.9 %all-gather.14.cloned.1.call-done = bf16[2048,768]{1,0:T(8,128)(2,1)} async-done(((bf16[256,768]{1,0:T(8,128)(2,1)}), bf16[2048,768]{1,0:T(8,128)(2,1)}) %all-gather.14.cloned.1.call-update) | async-done | bytes 3145744 | tf_op jit(solution)/shard_map/all_gather | solution.py:233
  108.1 4.8 copy.75
  112.8 57.1 %all-gather.12.cloned.1.call-done = bf16[2048,768]{1,0:T(8,128)(2,1)} async-done(((bf16[256,768]{1,0:T(8,128)(2,1)}), bf16[2048,768]{1,0:T(8,128)(2,1)}) %all-gather.12.cloned.1.call-update) | async-done | bytes 3145744 | tf_op jit(solution)/shard_map/all_gather | solution.py:232
  170.0 4.7 copy.74
  174.6 52.1 %while.48 = (s32[]{:T(128)}, f32[12,256]{1,0:T(8,128)S(1)}, f32[12,256]{1,0:T(8,128)S(1)}, f32[256,12,64]{0,2,1:T(8,128)S(1)}, s32[2048]{0:T(1024)S(1)}, /*index...) while((s32[]{:T(128)}, f32[12,256]{1,0:T(8,128)S(1)}, ...), condition=%wide.region_5.6_spmd.clone, body=%wide.region_2.5_spmd.clone.sunk | while | flops 424102912 | bytes 51457252 | solution.py:95
  177.2 3.9 fusion.173
  181.1 4.7 fusion.177
  189.9 3.8 fusion.173
  193.7 5.3 fusion.177
  203.9 3.8 fusion.173
  207.8 4.7 fusion.177
  216.6 3.8 fusion.173
  220.4 4.7 fusion.177
  229.4 11.7 %multiply_convert_fusion.8 = (bf16[256,3072]{1,0:T(8,128)(2,1)}, f32[256,3072]{1,0:T(8,128)}, f32[256,3072]{1,0:T(8,128)}) fusion(f32[3072]{0:T(1024)S(1)} %bitcast.216, bf16[768,3072]{1,0:T(8,128)(2,1)} %all-gather.18.cloned.1.call-done, f32[256,768]{1,0:T(8,128)S(1)} %get-tuple-element.991, f32[768]{0:T(1024)S(1)} %convert_element_type.231, ...), kind=kOutput, calls=%fused_computation.71 | convolution fusion | flops 1260847104 | bytes 13389824 | tf_op jit(solution)/shard_map/dot_general | solution.py:247
  241.2 24.1 %all-gather.20.cloned.1.call-done = bf16[3072,768]{1,0:T(8,128)(2,1)} async-done(((bf16[768,768]{1,0:T(8,128)(2,1)}), bf16[3072,768]{1,0:T(8,128)(2,1)}) %all-gather.20.cloned.1.call-update) | async-done | bytes 4718608 | tf_op jit(solution)/shard_map/all_gather | solution.py:191
  265.3 4.5 fusion.110
  283.4 33.5 %all_gather.72 = f32[2048,24]{0,1:T(8,128)} all-gather(f32[256,24]{0,1:T(8,128)S(1)} %pad_maximum_fusion.3), channel_id=1, replica_groups=mesh['ctx'=8,'fsdp'=4] {'ctx'}, dimensions={0}, use_global_device_ids=true | all-gather | bytes 221184 | tf_op jit(solution)/shard_map/all_gather | solution.py:310
  317.0 56.3 %while.49 = (s32[]{:T(128)}, f32[256,12,64]{0,2,1:T(8,128)}, bf16[2048,768]{0,1:T(8,128)(2,1)}, s32[2048]{0:T(1024)}, s32[]{:T(128)}, /*index=5*/s32[256]{0:T(25...) while((s32[]{:T(128)}, f32[256,12,64]{0,2,1:T(8,128)}, ...), condition=%wide.region_16.17_spmd.clone, body=%wide.region_15.16_spmd.clone.sunk | while | flops 614401024 | bytes 20745424 | solution.py:134
  324.8 6.3 fusion.185
  338.7 6.6 fusion.185
  352.9 6.4 fusion.185
  363.1 3.7 fusion.184
  366.8 6.4 fusion.185
  373.3 18.7 %all-gather.24.cloned.1.call-done = bf16[2048,768]{1,0:T(8,128)(2,1)} async-done(((bf16[256,768]{1,0:T(8,128)(2,1)}), bf16[2048,768]{1,0:T(8,128)(2,1)}) %all-gather.24.cloned.1.call-update) | async-done | bytes 3145744 | tf_op jit(solution)/shard_map/all_gather | solution.py:314
  391.9 87.7 %while.50 = (s32[]{:T(128)}, f32[256,12,64]{0,2,1:T(8,128)}, f32[256,12,64]{0,2,1:T(8,128)}, bf16[2048,768]{1,0:T(8,128)(2,1)}, s32[]{:T(128)}, /*index=5*/s32[2...) while((s32[]{:T(128)}, f32[256,12,64]{0,2,1:T(8,128)}, ...), condition=%wide.region_18.19_spmd.clone, body=%wide.region_17.18_spmd.clone.sunk | while | flops 822411776 | bytes 34915620 | solution.py:338
  397.3 3.7 fusion.193
  402.2 5.1 fusion.195
  407.3 6.4 fusion.194
  424.0 5.1 fusion.195
  429.1 6.6 fusion.194
  446.0 5.1 fusion.195
  451.1 6.6 fusion.194
  468.0 5.1 fusion.195
  473.1 6.6 fusion.194
  486.3 5.8 copy.86
  495.2 5.5 convolution_convert_fusion
  501.4 5.2 convolution_convert_fusion.1
  506.9 24.5 %reduce-scatter.13.cloned.1.call-done = bf16[192,2304]{1,0:T(8,128)(2,1)} async-done(((bf16[768,2304]{1,0:T(8,128)(2,1)}), bf16[192,2304]{1,0:T(8,128)(2,1)}) %reduce-scatter.13.cloned.1.call-update) | async-done | bytes 884752
  533.7 26.6 %reduce-scatter.7.cloned.1.call-done = bf16[192,768]{1,0:T(8,128)(2,1)} async-done(((bf16[768,768]{1,0:T(8,128)(2,1)}), bf16[192,768]{1,0:T(8,128)(2,1)}) %reduce-scatter.7.cloned.1.call-update) | async-done | bytes 294928 | tf_op jit(solution)/shard_map/reduce_scatter | solution.py:380
  560.3 50.4 %reduce-scatter.11.cloned.1.call-done = bf16[768,768]{1,0:T(8,128)(2,1)} async-done(((bf16[3072,768]{1,0:T(8,128)(2,1)}), bf16[768,768]{1,0:T(8,128)(2,1)}) %reduce-scatter.11.cloned.1.call-update) | async-done | bytes 1179664 | tf_op jit(solution)/shard_map/reduce_scatter | solution.py:398
  610.7 50.4 %reduce-scatter.9.cloned.1.call-done = bf16[192,3072]{1,0:T(8,128)(2,1)} async-done(((bf16[768,3072]{1,0:T(8,128)(2,1)}), bf16[192,3072]{1,0:T(8,128)(2,1)}) %reduce-scatter.9.cloned.1.call-update) | async-done | bytes 1179664 | tf_op jit(solution)/shard_map/reduce_scatter | solution.py:392
  662.9 10.3 %all-reduce.19 = (bf16[768]{0:T(1024)(128)(2,1)S(1)}, bf16[768]{0:T(1024)(128)(2,1)S(1)}, bf16[768]{0:T(1024)(128)(2,1)S(1)}, bf16[768]{0:T(1024)(128)(2,1)S(1)}...) all-reduce(bf16[768]{0:T(1024)(128)(2,1)S(1)} %dynamic-update-slice, ...), channel_id=1, replica_groups=mesh['ctx'=8,'fsdp'=4] {'fsdp'}, use_global_device_ids=true, to_apply=%add.7 | all-reduce | flops 9984 | bytes 39936
  673.8 23.0 %all-reduce.17 = (bf16[192]{0:T(256)(128)(2,1)S(1)}, bf16[192]{0:T(256)(128)(2,1)S(1)}, bf16[192]{0:T(256)(128)(2,1)S(1)}, bf16[192]{0:T(256)(128)(2,1)S(1)}, bf...) all-reduce(bf16[192]{0:T(256)(128)(2,1)S(1)} %dynamic-slice.9, ...), channel_id=1, replica_groups=mesh['ctx'=8,'fsdp'=4] {'ctx'}, use_global_device_ids=true, to_apply=%region_23.24 | all-reduce | flops 2304 | bytes 9216 | tf_op jit(solution)/shard_map/psum | solution.py:413
  703.2 4.1 fusion.63
  707.2 107.0 %all-reduce.23.cloned.1.call-done = (bf16[192,2304]{0,1:T(8,128)(2,1)}, bf16[192,768]{1,0:T(8,128)(2,1)}, bf16[192,3072]{1,0:T(8,128)(2,1)}, bf16[768,768]{1,0:T(8,128)(2,1)}) async-done(((bf16[192,2304]{0,1:T(8,128)(2,1)}, bf16[192,768]{1,0:T(8,128)(2,1)}, bf16[192,3072]{1,0:T(8,128)(2,1)}, bf16[768,768]{1,0:T(8,128)(2,1)}), (bf16[192,2304]{0,1:T(8,128)(2,1)}, bf16[192,768]{1,0:T(8,128)(2,1)}, ...) | async-done | bytes 3538960 | tf_op jit(solution)/shard_map/psum | solution.py:412
  (356 shorter events, 140.9 us)
Async XLA Ops:
  7.2 36.1 %all-gather.10.cloned.1.call-start = ((), (), s32[]{:S(2)}) async-start(), calls=%async_computation.4 | async-start | bytes 4423680 | tf_op jit(solution)/shard_map/all_gather | solution.py:182
  7.9 100.2 %all-gather.14.cloned.1.call-start = ((), (), s32[]{:S(2)}) async-start(), calls=%async_computation.6 | async-start | bytes 3538944 | tf_op jit(solution)/shard_map/all_gather | solution.py:233
  46.5 9.6 %copy-start.55 = (s32[16]{0:T(128)S(1)}, s32[16]{0:T(128)}, u32[]{:S(2)}) copy-start(s32[16]{0:T(128)} %param.26) | copy-start | bytes 196
  47.4 10.2 %copy-start.6 = (bf16[256,768]{1,0:T(8,128)(2,1)}, bf16[256,768]{1,0:T(8,128)(2,1)S(1)}, u32[]{:S(2)}) copy-start(bf16[256,768]{1,0:T(8,128)(2,1)S(1)} %get-tuple-element.987) | copy-start | bytes 1179652
  47.4 9.0 %copy-start.9 = (bf16[256,768]{1,0:T(8,128)(2,1)S(1)}, bf16[256,768]{1,0:T(8,128)(2,1)}, u32[]{:S(2)}) copy-start(bf16[256,768]{1,0:T(8,128)(2,1)} %get-tuple-element.986) | copy-start | bytes 1179652
  47.4 122.6 %all-gather.12.cloned.1.call-start = ((), (), s32[]{:S(2)}) async-start(), calls=%async_computation.5 | async-start | bytes 3538944 | tf_op jit(solution)/shard_map/all_gather | solution.py:232
  48.2 9.0 %copy-start.10 = (bf16[256,768]{1,0:T(8,128)(2,1)S(1)}, bf16[256,768]{1,0:T(8,128)(2,1)}, u32[]{:S(2)}) copy-start(bf16[256,768]{1,0:T(8,128)(2,1)} %slice.39) | copy-start | bytes 1179652
  48.2 178.6 %all-gather.16.cloned.1.call-start = ((), (), s32[]{:S(2)}) async-start(), calls=%async_computation.7 | async-start | bytes 1474560 | tf_op jit(solution)/shard_map/all_gather | solution.py:185
  48.8 180.6 %all-gather.18.cloned.1.call-start = ((), (), s32[]{:S(2)}) async-start(), calls=%async_computation.8 | async-start | bytes 5898240 | tf_op jit(solution)/shard_map/all_gather | solution.py:189
  49.4 215.9 %all-gather.20.cloned.1.call-start = ((), (), s32[]{:S(2)}) async-start(), calls=%async_computation.9 | async-start | bytes 5898240 | tf_op jit(solution)/shard_map/all_gather | solution.py:191
  50.0 323.3 %all-gather.22.cloned.1.call-start = ((), (), s32[]{:S(2)}) async-start(), calls=%async_computation.10 | async-start | bytes 3538944 | tf_op jit(solution)/shard_map/all_gather | solution.py:313
  50.8 214.5 %copy-start.29 = (f32[768]{0:T(1024)}, f32[768]{0:T(1024)S(1)}, u32[]{:S(2)}) copy-start(f32[768]{0:T(1024)S(1)} %convert_element_type.230) | copy-start | bytes 9220
  50.8 214.5 %copy-start.32 = (f32[768]{0:T(1024)}, f32[768]{0:T(1024)S(1)}, u32[]{:S(2)}) copy-start(f32[768]{0:T(1024)S(1)} %convert_element_type.231) | copy-start | bytes 9220
  56.0 215.1 %copy-start.34 = (f32[768]{0:T(1024)}, f32[768]{0:T(1024)S(1)}, u32[]{:S(2)}) copy-start(f32[768]{0:T(1024)S(1)} %convert_element_type.236) | copy-start | bytes 9220
  56.3 214.8 %copy-start.46 = (pred[256]{0:T(512)(128)(4,1)}, pred[256]{0:T(512)(128)(4,1)S(1)}, u32[]{:S(2)}) copy-start(pred[256]{0:T(512)(128)(4,1)S(1)} %get-tuple-element.970) | copy-start | bytes 772
  57.6 334.3 %all-gather.24.cloned.1.call-start = ((), (), s32[]{:S(2)}) async-start(), calls=%async_computation.11 | async-start | bytes 3538944 | tf_op jit(solution)/shard_map/all_gather | solution.py:314
  193.7 6.2 copy-start
  226.7 14.4 %copy-start.14 = (f32[256,12,64]{0,2,1:T(8,128)}, f32[256,12,64]{0,2,1:T(8,128)S(1)}, u32[]{:S(2)}) copy-start(f32[256,12,64]{0,2,1:T(8,128)S(1)} %get-tuple-element.555) | copy-start | bytes 2359300
  226.7 14.4 %copy-start.20 = (f32[12,256]{1,0:T(8,128)}, f32[12,256]{1,0:T(8,128)S(1)}, u32[]{:S(2)}) copy-start(f32[12,256]{1,0:T(8,128)S(1)} %get-tuple-element.556) | copy-start | bytes 36868
  226.7 14.4 %copy-start.21 = (s32[256]{0:T(256)}, s32[256]{0:T(256)S(1)}, u32[]{:S(2)}) copy-start(s32[256]{0:T(256)S(1)} %get-tuple-element.1426) | copy-start | bytes 3076
  226.8 14.4 %copy-start.28 = (s32[2048]{0:T(1024)}, s32[2048]{0:T(1024)S(1)}, u32[]{:S(2)}) copy-start(s32[2048]{0:T(1024)S(1)} %get-tuple-element.1433) | copy-start | bytes 24580
  226.8 14.3 %copy-start.7 = (bf16[256,12,64]{0,2,1:T(8,128)(2,1)}, bf16[256,12,64]{0,2,1:T(8,128)(2,1)S(1)}, u32[]{:S(2)}) copy-start(bf16[256,12,64]{0,2,1:T(8,128)(2,1)S(1)} %fusion.81) | copy-start | bytes 1179652
  229.1 36.2 %copy-start.38 = (f32[256]{0:T(256)}, f32[256]{0:T(256)S(1)}, u32[]{:S(2)}) copy-start(f32[256]{0:T(256)S(1)} %broadcast_multiply_fusion.5) | copy-start | bytes 3076
  229.4 35.9 %copy-start.43 = (f32[256]{0:T(256)}, f32[256]{0:T(256)S(1)}, u32[]{:S(2)}) copy-start(f32[256]{0:T(256)S(1)} %add_rsqrt_fusion.1) | copy-start | bytes 3076
  265.3 6.8 slice-start.2
  265.3 6.7 slice-start.3
  265.3 6.7 copy-start.59
  278.1 38.9 %copy-start.3 = (f32[256,768]{1,0:T(8,128)}, f32[256,768]{1,0:T(8,128)S(1)}, u32[]{:S(2)}) copy-start(f32[256,768]{1,0:T(8,128)S(1)} %get-tuple-element.965) | copy-start | bytes 2359300
  316.9 214.4 %reduce-scatter.13.cloned.1.call-start = ((), (), s32[]{:S(2)}) async-start(), calls=%async_computation.15 | async-start | bytes 4423680
  492.2 68.1 %reduce-scatter.7.cloned.1.call-start = ((), (), s32[]{:S(2)}) async-start(), calls=%async_computation.12 | async-start | bytes 1474560 | tf_op jit(solution)/shard_map/reduce_scatter | solution.py:380
  494.9 115.8 %reduce-scatter.11.cloned.1.call-start = ((), (), s32[]{:S(2)}) async-start(), calls=%async_computation.14 | async-start | bytes 5898240 | tf_op jit(solution)/shard_map/reduce_scatter | solution.py:398
  500.7 160.4 %reduce-scatter.9.cloned.1.call-start = ((), (), s32[]{:S(2)}) async-start(), calls=%async_computation.13 | async-start | bytes 5898240 | tf_op jit(solution)/shard_map/reduce_scatter | solution.py:392
  506.7 155.8 %copy-start.57 = (bf16[192]{0:T(256)(128)(2,1)S(1)}, bf16[192]{0:T(256)(128)(2,1)}, u32[]{:S(2)}) copy-start(bf16[192]{0:T(256)(128)(2,1)} %param.39) | copy-start | bytes 1156
  506.7 156.2 %copy-start.48 = (bf16[768]{0:T(1024)(128)(2,1)S(1)}, bf16[768]{0:T(1024)(128)(2,1)}, u32[]{:S(2)}) copy-start(bf16[768]{0:T(1024)(128)(2,1)} %get-tuple-element.856) | copy-start | bytes 4612
  506.7 156.2 %copy-start.49 = (bf16[768]{0:T(1024)(128)(2,1)S(1)}, bf16[768]{0:T(1024)(128)(2,1)}, u32[]{:S(2)}) copy-start(bf16[768]{0:T(1024)(128)(2,1)} %get-tuple-element.861) | copy-start | bytes 4612
  506.7 156.2 %copy-start.50 = (bf16[768]{0:T(1024)(128)(2,1)S(1)}, bf16[768]{0:T(1024)(128)(2,1)}, u32[]{:S(2)}) copy-start(bf16[768]{0:T(1024)(128)(2,1)} %get-tuple-element.962) | copy-start | bytes 4612
  506.7 156.2 %copy-start.51 = (bf16[768]{0:T(1024)(128)(2,1)S(1)}, bf16[768]{0:T(1024)(128)(2,1)}, u32[]{:S(2)}) copy-start(bf16[768]{0:T(1024)(128)(2,1)} %get-tuple-element.964) | copy-start | bytes 4612
  506.7 156.2 %copy-start.52 = (bf16[3072]{0:T(1024)(128)(2,1)S(1)}, bf16[3072]{0:T(1024)(128)(2,1)}, u32[]{:S(2)}) copy-start(bf16[3072]{0:T(1024)(128)(2,1)} %get-tuple-element.996) | copy-start | bytes 18436
  506.7 156.2 %copy-start.53 = (bf16[768]{0:T(1024)(128)(2,1)S(1)}, bf16[768]{0:T(1024)(128)(2,1)}, u32[]{:S(2)}) copy-start(bf16[768]{0:T(1024)(128)(2,1)} %get-tuple-element.854) | copy-start | bytes 4612
  506.7 156.2 %copy-start.54 = (bf16[768]{0:T(1024)(128)(2,1)S(1)}, bf16[768]{0:T(1024)(128)(2,1)}, u32[]{:S(2)}) copy-start(bf16[768]{0:T(1024)(128)(2,1)} %get-tuple-element.859) | copy-start | bytes 4612
  506.7 195.2 %copy-start.2 = (f32[256,768]{1,0:T(8,128)S(1)}, f32[256,768]{1,0:T(8,128)}, u32[]{:S(2)}) copy-start(f32[256,768]{1,0:T(8,128)} %copy-done.1) | copy-start | bytes 2359300
  506.8 195.2 %copy-start.35 = (f32[768]{0:T(1024)S(1)}, f32[768]{0:T(1024)}, u32[]{:S(2)}) copy-start(f32[768]{0:T(1024)} %copy-done.34) | copy-start | bytes 9220
  506.8 195.2 %copy-start.37 = (f32[256]{0:T(256)S(1)}, f32[256]{0:T(256)}, u32[]{:S(2)}) copy-start(f32[256]{0:T(256)} %copy-done.36) | copy-start | bytes 3076
  506.8 195.2 %copy-start.42 = (f32[256]{0:T(256)S(1)}, f32[256]{0:T(256)}, u32[]{:S(2)}) copy-start(f32[256]{0:T(256)} %copy-done.41) | copy-start | bytes 3076
  506.8 195.2 %copy-start.47 = (pred[256]{0:T(512)(128)(4,1)S(1)}, pred[256]{0:T(512)(128)(4,1)}, u32[]{:S(2)}) copy-start(pred[256]{0:T(512)(128)(4,1)} %copy-done.46) | copy-start | bytes 772
  506.8 307.5 %all-reduce.23.cloned.1.call-start = ((), (), s32[]{:S(2)}) async-start(), calls=%async_computation.16 | async-start | bytes 7667712 | tf_op jit(solution)/shard_map/psum | solution.py:412
  533.7 169.5 %copy-start.23 = (bf16[256,12,64]{0,2,1:T(8,128)(2,1)S(1)}, bf16[256,12,64]{0,2,1:T(8,128)(2,1)}, u32[]{:S(2)}) copy-start(bf16[256,12,64]{0,2,1:T(8,128)(2,1)} %copy-done.22) | copy-start | bytes 1179652
  533.7 169.5 %copy-start.26 = (bf16[256,12,64]{0,2,1:T(8,128)(2,1)S(1)}, bf16[256,12,64]{0,2,1:T(8,128)(2,1)}, u32[]{:S(2)}) copy-start(bf16[256,12,64]{0,2,1:T(8,128)(2,1)} %copy-done.25) | copy-start | bytes 1179652
  (38 other events, 129.9 us)
Sparse Core Ops, SparseCore 0:
  9.6 33.6 all-gather.9
  47.5 60.5 all-gather.13
  110.8 59.0 all-gather.11
  171.4 16.0 all-gather.15
  188.9 37.4 all-gather.17
  227.8 37.4 all-gather.19
  267.5 62.3 all-gather.21
  332.6 59.3 all-gather.23
  492.3 39.0 reduce-scatter.12
  534.5 25.7 reduce-scatter.6
  562.8 47.8 reduce-scatter.10
  613.2 47.8 reduce-scatter.8
  665.7 148.5 all-reduce.22
where the time goes:
time: 834 us; the launch traced here: 828 us
  waiting for transfers between devices  425 us (51%)
  matrix products  184 us (22%)
  blocking collectives  85.3 us (10%)
  local copies, waits for them, and re-layouts  62 us (7%)
  other arithmetic  52.2 us (6%)
  between operations  17.6 us (2%)
    psum x1, waiting for transfers between devices, on_device(): lax.psum(shards[0].astype(jnp.bfloat16), 'ctx').astype(jnp.float32)  107 us
    all_gather x1, waiting for transfers between devices, on_device(): lax.all_gather(keys, 'ctx', axis=0, tiled=True)  57.1 us
    reduce_scatter x1, waiting for transfers between devices, on_device(): lax.psum_scatter(grads[7].astype(jnp.bfloat16), 'fsdp', scatter_dimension...  50.4 us
    reduce_scatter x1, waiting for transfers between devices, on_device(): lax.psum_scatter(grads[9].astype(jnp.bfloat16), 'fsdp', scatter_dimension...  50.4 us
    all_gather x1, waiting for transfers between devices, on_device(): lax.all_gather(values, 'ctx', axis=0, tiled=True)  49.9 us
    all_gather x1, blocking collectives, on_device(): stats_all = lax.all_gather(stats, 'ctx', axis=0, tiled=True)  33.5 us
    dot_general x8, matrix products, step(): jnp.einsum('qhd,khd->hqk', query_heads, key_heads, preferred_element_type...  30.2 us
    unnamed x154, local copies, waits for them, and re-layouts  30.1 us
  transfers between devices with their start and end apart: 13, of which 10 were waited for; matrix products, arithmetic and copies ran while one was open for 22% of the time, Pallas kernels for 0%

commit v1 on v0

--- a/solution.py
+++ b/solution.py
@@ -1,13 +1,17 @@
+import functools
 import math
 
 import jax
 import jax.numpy as jnp
 from jax import lax
+from jax.experimental import pallas as pl
+from jax.experimental.pallas import tpu as pltpu
 from jax.sharding import PartitionSpec as P
 
 HEADS = 12
 HEAD_DIM = 64
 NMEM = 10
+BLK = 128
 
 
 eps = 1e-12
@@ -159,7 +163,7 @@
     return (key_grad, value_grad)
 
 
-def on_device(
+def on_device_any(
     tokens,
     cotangent,
     lengths,
@@ -426,9 +430,463 @@
     return (output[None], token_grad[None]) + tuple(totals)
 
 
+MESH = pl.DeviceIdType.MESH
+
+
+def exchange_kernel(n, in_ref, out_ref, sent, landed, own):
+    me = lax.axis_index("ctx")
+    barrier = pltpu.get_barrier_semaphore()
+    for k in range(1, n):
+        pl.semaphore_signal(
+            barrier, inc=1, device_id={"ctx": lax.rem(me + k, n)}, device_id_type=MESH
+        )
+    pl.semaphore_wait(barrier, n - 1)
+    copies = []
+    for k in range(1, n):
+        peer = lax.rem(me + k, n)
+        copy = pltpu.make_async_remote_copy(
+            src_ref=in_ref.at[peer],
+            dst_ref=out_ref.at[me],
+            send_sem=sent.at[k],
+            recv_sem=landed.at[k],
+            device_id={"ctx": peer},
+            device_id_type=MESH,
+        )
+        copy.start()
+        copies.append(copy)
+    local = pltpu.make_async_copy(in_ref.at[me], out_ref.at[me], own)
+    local.start()
+    local.wait()
+    for copy in copies:
+        copy.wait()
+
+
+def exchange(blocks, name):
+    n = blocks.shape[0]
+    return pl.pallas_call(
+        functools.partial(exchange_kernel, n),
+        out_shape=jax.ShapeDtypeStruct(blocks.shape, blocks.dtype),
+        in_specs=[vmem()],
+        out_specs=vmem(),
+        scratch_shapes=[
+            pltpu.SemaphoreType.DMA((n,)),
+            pltpu.SemaphoreType.DMA((n,)),
+            pltpu.SemaphoreType.DMA,
+        ],
+        compiler_params=pltpu.CompilerParams(
+            collective_id=name, has_side_effects=True, vmem_limit_bytes=16 << 20
+        ),
+        name="exchange",
+    )(blocks)
+
+
+def split_heads(value):
+    rows = value.shape[0]
+    trio = value.reshape(rows, HEADS // 3, 3, HEAD_DIM)
+    own = trio[:, :, :2]
+    shared = jnp.broadcast_to(trio[:, :, 2:], own.shape)
+    both = jnp.concatenate([own, shared], axis=-1)
+    return jnp.transpose(both.reshape(rows, -1, 2 * HEAD_DIM), (1, 0, 2))
+
+
+def send_blocks(queries, keys, values):
+    return jnp.concatenate([split_heads(queries), split_heads(keys), split_heads(values)], axis=2)
+
+
+def join_heads(blocks):
+    rows = blocks.shape[1]
+    pairs = blocks.reshape(HEADS // 3, 2, rows, 2, HEAD_DIM)
+    shared = pairs[:, 0, :, 1].astype(jnp.float32) + pairs[:, 1, :, 1].astype(jnp.float32)
+    trio = jnp.stack([pairs[:, 0, :, 0], pairs[:, 1, :, 0], shared.astype(blocks.dtype)], axis=2)
+    return jnp.transpose(trio, (1, 0, 2, 3)).reshape(rows, HEADS * HEAD_DIM)
+
+
+def join_parts(blocks):
+    parts = jnp.split(blocks, 3, axis=2)
+    return jnp.concatenate([join_heads(part) for part in parts], axis=1)
+
+
+BLK = 128
+
+
+def low_lanes(shape):
+    return lax.broadcasted_iota(jnp.int32, shape, 1) < 64
+
+
+def attend_kernel(chunks, pair_ref, len_ref, spot_ref, in_ref, out_ref, keep_ref, mix_ref, lse_ref):
+    length = len_ref[0]
+    spot = spot_ref[0]
+    blocks = 2 * chunks
+    for s in range(blocks):
+        keep_ref[pair_ref[s]] = in_ref[s]
+    left = low_lanes((256, BLK))
+    left_half = left[:BLK]
+    for c in range(chunks):
+        keys = 256 * (c + 1)
+        own = keep_ref[2 * c : 2 * c + 2, :, :BLK].reshape(256, BLK)
+        shared = keep_ref[2 * c + spot, :, :BLK]
+        zero = jnp.zeros((), jnp.bfloat16)
+        query = jnp.concatenate(
+            [jnp.where(left, own, zero), jnp.where(left_half, zero, shared)], axis=0
+        ) * jnp.bfloat16(0.125)
+        key = keep_ref[: 2 * c + 2, :, BLK : 2 * BLK].reshape(keys, BLK)
+        value = keep_ref[: 2 * c + 2, :, 2 * BLK :].reshape(keys, BLK)
+        scores = mask_scores(
+            lax.dot_general(key, query, (((1,), (1,)), ((), ())), preferred_element_type=jnp.float32),
+            c, spot, length,
+        )
+        top = jnp.max(scores, axis=0, keepdims=True)
+        probs = jnp.exp(scores - top)
+        total = jnp.sum(probs, axis=0, keepdims=True)
+        summed = lax.dot_general(
+            value, probs.astype(jnp.bfloat16), (((0,), (0,)), ((), ())),
+            preferred_element_type=jnp.float32,
+        ) / total
+        lse_ref[c] = top + jnp.log(total)
+        part = summed[64:, 256:]
+        none = jnp.zeros_like(part)
+        first = jnp.where(spot == 0, part, none)
+        second = jnp.where(spot == 0, none, part)
+        mixed = jnp.concatenate(
+            [summed[:64, :256], jnp.concatenate([first, second], axis=1)], axis=0
+        )
+        mix_ref[c] = mixed
+    for s in range(blocks):
+        place = pair_ref[s]
+        c = place // 2
+        piece = mix_ref[c, :, pl.ds(pl.multiple_of((place % 2) * BLK, BLK), BLK)]
+        out_ref[s] = jnp.transpose(piece).astype(jnp.bfloat16)
+
+
+def mask_scores(scores, c, spot, length):
+    keys, width = scores.shape
+    edge = 256 * c
+    row = lax.broadcasted_iota(jnp.int32, (keys, width), 0)
+    scores = jnp.where(row < length, scores, neg_big)
+    lane = lax.broadcasted_iota(jnp.int32, (256, width), 1)
+    query_place = edge + jnp.where(lane < 256, lane, lane - 256 + spot * BLK)
+    key_place = edge + lax.broadcasted_iota(jnp.int32, (256, width), 0)
+    seen = key_place <= query_place
+    if c == 0:
+        seen = seen | (key_place < NMEM)
+    tail = jnp.where(seen, scores[edge:], neg_big)
+    if c == 0:
+        return tail
+    return jnp.concatenate([scores[:edge], tail], axis=0)
+
+
+def attend_back_kernel(
+    chunks, pair_ref, len_ref, spot_ref, keep_ref, grad_ref, mix_ref, lse_ref, out_ref, g_ref,
+    q_sum, k_sum, v_sum
+):
+    length = len_ref[0]
+    spot = spot_ref[0]
+    blocks = 2 * chunks
+    for s in range(blocks):
+        g_ref[pair_ref[s]] = grad_ref[s]
+    k_sum[...] = jnp.zeros_like(k_sum)
+    v_sum[...] = jnp.zeros_like(v_sum)
+    left = low_lanes((256, BLK))
+    left_half = left[:BLK]
+    zero = jnp.zeros((), jnp.bfloat16)
+    for c in range(chunks):
+        keys = 256 * (c + 1)
+        own = keep_ref[2 * c : 2 * c + 2, :, :BLK].reshape(256, BLK)
+        shared = keep_ref[2 * c + spot, :, :BLK]
+        query = jnp.concatenate(
+            [jnp.where(left, own, zero), jnp.where(left_half, zero, shared)], axis=0
+        ) * jnp.bfloat16(0.125)
+        g_own = g_ref[2 * c : 2 * c + 2].reshape(256, BLK)
+        g_shared = g_ref[2 * c + spot]
+        grad = jnp.concatenate(
+            [jnp.where(left, g_own, zero), jnp.where(left_half, zero, g_shared)], axis=0
+        )
+        key = keep_ref[: 2 * c + 2, :, BLK : 2 * BLK].reshape(keys, BLK)
+        value = keep_ref[: 2 * c + 2, :, 2 * BLK :].reshape(keys, BLK)
+        turned = jnp.transpose(g_own.astype(jnp.float32)) * mix_ref[c]
+        delta_own = jnp.sum(turned[:64], axis=0, keepdims=True)
+        delta_pair = jnp.sum(turned[64:], axis=0, keepdims=True)
+        delta = jnp.concatenate(
+            [delta_own, jnp.where(spot == 0, delta_pair[:, :BLK], delta_pair[:, BLK:])], axis=1
+        )
+        nt = (((1,), (1,)), ((), ()))
+        scores = mask_scores(
+            lax.dot_general(key, query, nt, preferred_element_type=jnp.float32), c, spot, length
+        )
+        probs = jnp.exp(scores - lse_ref[c])
+        prob_grad = lax.dot_general(value, grad, nt, preferred_element_type=jnp.float32)
+        score_grad = (probs * (prob_grad - delta)).astype(jnp.bfloat16)
+        nn = (((1,), (0,)), ((), ()))
+        v_sum[:keys] += lax.dot_general(
+            probs.astype(jnp.bfloat16), grad, nn, preferred_element_type=jnp.float32
+        )
+        k_sum[:keys] += lax.dot_general(score_grad, query, nn, preferred_element_type=jnp.float32)
+        q_grad = lax.dot_general(
+            score_grad, key, (((0,), (0,)), ((), ())), preferred_element_type=jnp.float32
+        ) * 0.125
+        part = q_grad[256:]
+        none = jnp.zeros_like(part)
+        first = jnp.where(spot == 0, part, none)
+        second = jnp.where(spot == 0, none, part)
+        q_sum[256 * c : 256 * c + 256] = jnp.where(
+            left, q_grad[:256], jnp.concatenate([first, second], axis=0)
+        )
+    for s in range(blocks):
+        rows = pl.ds(pl.multiple_of(pair_ref[s] * BLK, BLK), BLK)
+        out_ref[s] = jnp.concatenate([q_sum[rows], k_sum[rows], v_sum[rows]], axis=1).astype(jnp.bfloat16)
+
+
+def smem():
+    return pl.BlockSpec(memory_space=pltpu.SMEM)
+
+
+def vmem():
+    return pl.BlockSpec(memory_space=pltpu.VMEM)
+
+
+def attend(pairing, lengths, spot, packed):
+    blocks = packed.shape[0]
+    chunks = blocks // 2
+    return pl.pallas_call(
+        functools.partial(attend_kernel, chunks),
+        out_shape=(
+            jax.ShapeDtypeStruct((blocks, BLK, BLK), jnp.bfloat16),
+            jax.ShapeDtypeStruct((blocks, BLK, 3 * BLK), jnp.bfloat16),
+            jax.ShapeDtypeStruct((chunks, BLK, 256), jnp.float32),
+            jax.ShapeDtypeStruct((chunks, 1, 384), jnp.float32),
+        ),
+        in_specs=[smem(), smem(), smem(), vmem()],
+        out_specs=(vmem(), vmem(), vmem(), vmem()),
+        compiler_params=pltpu.CompilerParams(vmem_limit_bytes=48 << 20),
+        name="attend",
+    )(pairing, lengths, spot, packed)
+
+
+def attend_back(pairing, lengths, spot, keep, grad, mix, lse):
+    blocks = keep.shape[0]
+    chunks = blocks // 2
+    return pl.pallas_call(
+        functools.partial(attend_back_kernel, chunks),
+        out_shape=jax.ShapeDtypeStruct((blocks, BLK, 3 * BLK), jnp.bfloat16),
+        in_specs=[smem(), smem(), smem(), vmem(), vmem(), vmem(), vmem()],
+        out_specs=vmem(),
+        scratch_shapes=[
+            pltpu.VMEM((blocks, BLK, BLK), jnp.bfloat16),
+            pltpu.VMEM((blocks * BLK, BLK), jnp.float32),
+            pltpu.VMEM((blocks * BLK, BLK), jnp.float32),
+            pltpu.VMEM((blocks * BLK, BLK), jnp.float32),
+        ],
+        compiler_params=pltpu.CompilerParams(vmem_limit_bytes=48 << 20),
+        name="attend_back",
+    )(pairing, lengths, spot, keep, grad, mix, lse)
+
+
+def on_device_spread(
+    tokens,
+    cotangent,
+    lengths,
+    pairing,
+    w_qkv,
+    bias_q,
+    bias_v,
+    w_out,
+    bias_out,
+    ln1_gain,
+    ln1_bias,
+    w_in,
+    bias_in,
+    w_back,
+    bias_back,
+    ln2_gain,
+    ln2_bias,
+):
+    gathered = (
+        lax.all_gather(w_qkv, "fsdp", axis=0, tiled=True),
+        lax.all_gather(bias_q, "fsdp", axis=0, tiled=True),
+        lax.all_gather(bias_v, "fsdp", axis=0, tiled=True),
+        lax.all_gather(w_out, "fsdp", axis=0, tiled=True),
+        lax.all_gather(bias_out, "fsdp", axis=0, tiled=True),
+        lax.all_gather(ln1_gain, "fsdp", axis=0, tiled=True),
+        lax.all_gather(ln1_bias, "fsdp", axis=0, tiled=True),
+        lax.all_gather(w_in, "fsdp", axis=0, tiled=True),
+        lax.all_gather(bias_in, "fsdp", axis=0, tiled=True),
+        lax.all_gather(w_back, "fsdp", axis=0, tiled=True),
+        lax.all_gather(bias_back, "fsdp", axis=0, tiled=True),
+        lax.all_gather(ln2_gain, "fsdp", axis=0, tiled=True),
+        lax.all_gather(ln2_bias, "fsdp", axis=0, tiled=True),
+    )
+    (
+        qkv_all,
+        query_bias,
+        value_bias,
+        out_all,
+        out_bias,
+        gain_one,
+        shift_one,
+        in_all,
+        in_bias,
+        back_all,
+        back_bias,
+        gain_two,
+        shift_two,
+    ) = gathered
+    rows = tokens.shape[1]
+    half = rows // 2
+    width = tokens.shape[2]
+    length = lengths[0]
+    query_place = places(pairing, lax.axis_index("ctx") * rows, rows, half)
+    valid = query_place < length
+    inputs = tokens[0]
+    proj = jnp.dot(inputs, qkv_all, preferred_element_type=jnp.float32)
+    queries = (proj[:, :width] + query_bias.astype(jnp.float32)).astype(jnp.bfloat16)
+    keys = proj[:, width : 2 * width].astype(jnp.bfloat16)
+    values = (proj[:, 2 * width :] + value_bias.astype(jnp.float32)).astype(jnp.bfloat16)
+    spot = lax.rem(lax.axis_index("ctx"), 2).astype(jnp.int32).reshape(1)
+    sent = send_blocks(queries, keys, values)
+    packed = exchange(sent, 0).reshape(-1, half, 6 * HEAD_DIM)
+    mixed_out, keep, mix, lse = attend(pairing, lengths, spot, packed)
+    attended_low = join_heads(exchange(mixed_out.reshape(-1, rows, 2 * HEAD_DIM), 1))
+    resid_one = (
+        inputs.astype(jnp.float32)
+        + jnp.dot(attended_low, out_all, preferred_element_type=jnp.float32)
+        + out_bias.astype(jnp.float32)
+    )
+    hidden = layer_norm(resid_one, gain_one.astype(jnp.float32), shift_one.astype(jnp.float32))
+    hidden_low = hidden.astype(jnp.bfloat16)
+    upper = jnp.dot(hidden_low, in_all, preferred_element_type=jnp.float32) + in_bias.astype(
+        jnp.float32
+    )
+    active, gelu_back = jax.vjp(lambda value: jax.nn.gelu(value, approximate=False), upper)
+    active_low = active.astype(jnp.bfloat16)
+    resid_two = (
+        hidden
+        + jnp.dot(active_low, back_all, preferred_element_type=jnp.float32)
+        + back_bias.astype(jnp.float32)
+    )
+    normed = layer_norm(resid_two, gain_two.astype(jnp.float32), shift_two.astype(jnp.float32))
+    output = jnp.where(valid[:, None], normed, 0.0)
+    qkv_back, out_back, gain_one_back, in_back, back_back, gain_two_back = (
+        qkv_all,
+        out_all,
+        gain_one,
+        in_all,
+        back_all,
+        gain_two,
+    )
+    grad_y = jnp.where(valid[:, None], cotangent[0].astype(jnp.float32), 0.0)
+    grad_resid_two, gain_two_grad, shift_two_grad = norm_back(
+        resid_two, gain_two_back.astype(jnp.float32), grad_y
+    )
+    grad_mixed = grad_resid_two.astype(jnp.bfloat16)
+    back_grad = jnp.einsum("tf,td->fd", active_low, grad_mixed, preferred_element_type=jnp.float32)
+    back_bias_grad = jnp.sum(grad_mixed.astype(jnp.float32), axis=0)
+    grad_active = jnp.einsum("td,fd->tf", grad_mixed, back_back, preferred_element_type=jnp.float32)
+    (grad_upper,) = gelu_back(grad_active)
+    grad_upper_low = grad_upper.astype(jnp.bfloat16)
+    in_grad = jnp.einsum(
+        "td,tf->df", hidden_low, grad_upper_low, preferred_element_type=jnp.float32
+    )
+    in_bias_grad = jnp.sum(grad_upper_low.astype(jnp.float32), axis=0)
+    grad_hidden = grad_resid_two + jnp.einsum(
+        "tf,df->td", grad_upper_low, in_back, preferred_element_type=jnp.float32
+    )
+    grad_resid_one, gain_one_grad, shift_one_grad = norm_back(
+        resid_one, gain_one_back.astype(jnp.float32), grad_hidden
+    )
+    grad_branch = grad_resid_one.astype(jnp.bfloat16)
+    out_grad = jnp.einsum(
+        "tc,td->cd", attended_low, grad_branch, preferred_element_type=jnp.float32
+    )
+    out_bias_grad = jnp.sum(grad_branch.astype(jnp.float32), axis=0)
+    grad_attended = jnp.einsum(
+        "td,cd->tc", grad_branch, out_back, preferred_element_type=jnp.float32
+    ).astype(jnp.bfloat16)
+    grad_in = exchange(split_heads(grad_attended), 2).reshape(-1, half, 2 * HEAD_DIM)
+    grad_blocks = attend_back(pairing, lengths, spot, keep, grad_in, mix, lse)
+    grad_proj = join_parts(exchange(grad_blocks.reshape(-1, rows, 6 * HEAD_DIM), 3))
+    qkv_grad = jnp.einsum("td,tf->df", inputs, grad_proj, preferred_element_type=jnp.float32)
+    query_bias_grad = jnp.sum(grad_proj[:, :width].astype(jnp.float32), axis=0)
+    value_bias_grad = jnp.sum(grad_proj[:, 2 * width :].astype(jnp.float32), axis=0)
+    token_grad = grad_resid_one + jnp.einsum(
+        "tf,df->td", grad_proj, qkv_back, preferred_element_type=jnp.float32
+    )
+    grads = (
+        qkv_grad,
+        query_bias_grad,
+        value_bias_grad,
+        out_grad,
+        out_bias_grad,
+        gain_one_grad,
+        shift_one_grad,
+        in_grad,
+        in_bias_grad,
+        back_grad,
+        back_bias_grad,
+        gain_two_grad,
+        shift_two_grad,
+    )
+    shards = (
+        lax.psum_scatter(
+            grads[0].astype(jnp.bfloat16), "fsdp", scatter_dimension=0, tiled=True
+        ).astype(jnp.float32),
+        lax.psum_scatter(
+            grads[1].astype(jnp.bfloat16), "fsdp", scatter_dimension=0, tiled=True
+        ).astype(jnp.float32),
+        lax.psum_scatter(
+            grads[2].astype(jnp.bfloat16), "fsdp", scatter_dimension=0, tiled=True
+        ).astype(jnp.float32),
+        lax.psum_scatter(
+            grads[3].astype(jnp.bfloat16), "fsdp", scatter_dimension=0, tiled=True
+        ).astype(jnp.float32),
+        lax.psum_scatter(
+            grads[4].astype(jnp.bfloat16), "fsdp", scatter_dimension=0, tiled=True
+        ).astype(jnp.float32),
+        lax.psum_scatter(
+            grads[5].astype(jnp.bfloat16), "fsdp", scatter_dimension=0, tiled=True
+        ).astype(jnp.float32),
+        lax.psum_scatter(
+            grads[6].astype(jnp.bfloat16), "fsdp", scatter_dimension=0, tiled=True
+        ).astype(jnp.float32),
+        lax.psum_scatter(
+            grads[7].astype(jnp.bfloat16), "fsdp", scatter_dimension=0, tiled=True
+        ).astype(jnp.float32),
+        lax.psum_scatter(
+            grads[8].astype(jnp.bfloat16), "fsdp", scatter_dimension=0, tiled=True
+        ).astype(jnp.float32),
+        lax.psum_scatter(
+            grads[9].astype(jnp.bfloat16), "fsdp", scatter_dimension=0, tiled=True
+        ).astype(jnp.float32),
+        lax.psum_scatter(
+            grads[10].astype(jnp.bfloat16), "fsdp", scatter_dimension=0, tiled=True
+        ).astype(jnp.float32),
+        lax.psum_scatter(
+            grads[11].astype(jnp.bfloat16), "fsdp", scatter_dimension=0, tiled=True
+        ).astype(jnp.float32),
+        lax.psum_scatter(
+            grads[12].astype(jnp.bfloat16), "fsdp", scatter_dimension=0, tiled=True
+        ).astype(jnp.float32),
+    )
+    totals = (
+        lax.psum(shards[0].astype(jnp.bfloat16), "ctx").astype(jnp.float32),
+        lax.psum(shards[1].astype(jnp.bfloat16), "ctx").astype(jnp.float32),
+        lax.psum(shards[2].astype(jnp.bfloat16), "ctx").astype(jnp.float32),
+        lax.psum(shards[3].astype(jnp.bfloat16), "ctx").astype(jnp.float32),
+        lax.psum(shards[4].astype(jnp.bfloat16), "ctx").astype(jnp.float32),
+        lax.psum(shards[5].astype(jnp.bfloat16), "ctx").astype(jnp.float32),
+        lax.psum(shards[6].astype(jnp.bfloat16), "ctx").astype(jnp.float32),
+        lax.psum(shards[7].astype(jnp.bfloat16), "ctx").astype(jnp.float32),
+        lax.psum(shards[8].astype(jnp.bfloat16), "ctx").astype(jnp.float32),
+        lax.psum(shards[9].astype(jnp.bfloat16), "ctx").astype(jnp.float32),
+        lax.psum(shards[10].astype(jnp.bfloat16), "ctx").astype(jnp.float32),
+        lax.psum(shards[11].astype(jnp.bfloat16), "ctx").astype(jnp.float32),
+        lax.psum(shards[12].astype(jnp.bfloat16), "ctx").astype(jnp.float32),
+    )
+    return (output[None], token_grad[None]) + tuple(totals)
+
+
 def solution(mesh):
     return jax.shard_map(
-        on_device,
+        on_device_spread if mesh.shape["ctx"] == 8 else on_device_any,
         mesh=mesh,
         in_specs=(
             P("fsdp", "ctx", None),

time: 834 us -> 571 us (0.68)
  matrix products: 184 us -> 41.9 us
  waiting for transfers between devices: 425 us -> 299 us
  Pallas kernels: 0 us -> 116 us
  local copies, waits for them, and re-layouts: 62 us -> 24.3 us
  other arithmetic: 52.2 us -> 17.2 us
  blocking collectives: 85.3 us -> 52.2 us
    dot_general x40 -> x12, matrix products: 184 us -> 41.9 us  [the longest x1 11.7 us: on_device_spread(): jnp.dot(hidden_low, in_all, preferred_element_type=jnp.float32)]
    all_gather x8 -> x4, waiting for transfers between devices: 164 us -> 24.8 us  [the longest x1 14.3 us: on_device_spread(): lax.all_gather(w_back, 'fsdp', axis=0, tiled=True)]
    pallas_call x0 -> x6, Pallas kernels: none -> 116 us  [the longest x4 96.8 us: exchange(): pl.pallas_call(functools.partial(exchange_kernel, n), out_shape=jax.Shape...]
    all_gather x2 -> x1, blocking collectives: 38.7 us -> 5.73 us  [on_device_spread(): lax.all_gather(bias_in, 'fsdp', axis=0, tiled=True)]
    dynamic_slice x24 -> x0, local copies, waits for them, and re-layouts: 23.1 us -> none  [the longest x8 12 us: step(): value_heads = heads_of(lax.dynamic_slice_in_dim(values, offset, width, 0))]
    lt x21 -> x1, other arithmetic: 13.9 us -> 0.02 us  [on_device_spread(): valid = query_place < length]
    unnamed x154 -> x144, local copies, waits for them, and re-layouts: 30.1 us -> 17 us
    unnamed x14 -> x10, waiting for transfers between devices: 26.9 us -> 39.1 us
  transfers between devices with their start and end apart: 13 -> 9, of which waited for: 10 -> 7; matrix products, arithmetic and copies ran while one was open for 22% -> 9% of each run, Pallas kernels for 0% -> 10%
where the time goes in v1:
time: 571 us; the launch traced here: 568 us
  waiting for transfers between devices  299 us (52%)
  Pallas kernels  116 us (20%)
  blocking collectives  52.2 us (9%)
  matrix products  41.9 us (7%)
  local copies, waits for them, and re-layouts  24.3 us (4%)
  between operations  17.7 us (3%)
  other arithmetic  17.2 us (3%)
    psum x1, waiting for transfers between devices, on_device_spread(): lax.psum(shards[0].astype(jnp.bfloat16), 'ctx').astype(jnp.float32)  107 us
    pallas_call x4, Pallas kernels, exchange(): pl.pallas_call(functools.partial(exchange_kernel, n), out_shape=jax.Shape...  96.8 us
    reduce_scatter x1, waiting for transfers between devices, on_device_spread(): lax.psum_scatter(grads[9].astype(jnp.bfloat16), 'fsdp', scatter_dimension...  50.6 us
    reduce_scatter x1, waiting for transfers between devices, on_device_spread(): lax.psum_scatter(grads[7].astype(jnp.bfloat16), 'fsdp', scatter_dimension...  50.4 us
    unnamed x10, waiting for transfers between devices  39.1 us
    reduce_scatter x1, waiting for transfers between devices, on_device_spread(): lax.psum_scatter(grads[3].astype(jnp.bfloat16), 'fsdp', scatter_dimension...  26.6 us
    unnamed x2, blocking collectives  23.4 us
    psum x1, blocking collectives, on_device_spread(): lax.psum(shards[1].astype(jnp.bfloat16), 'ctx').astype(jnp.float32)  23 us
  transfers between devices with their start and end apart: 9, of which 7 were waited for; matrix products, arithmetic and copies ran while one was open for 9% of the time, Pallas kernels for 10%

profile of v1, /device:TPU:0, one launch (start us, length us, event | category | flops | bytes accessed | tf_op | source)
XLA Modules:
  0.0 568.0 jit_solution(13399610130923106978)
XLA Ops:
  13.1 13.2 %all-reduce.20 = (bf16[768]{0:T(1024)(128)(2,1)S(1)}, bf16[768]{0:T(1024)(128)(2,1)S(1)}, bf16[768]{0:T(1024)(128)(2,1)S(1)}, bf16[768]{0:T(1024)(128)(2,1)S(1)}...) all-reduce(bf16[768]{0:T(1024)(128)(2,1)S(1)} %dynamic-update-slice, ...), channel_id=1, replica_groups=mesh['ctx'=8,'fsdp'=4] {'fsdp'}, use_global_device_ids=true, to_apply=%add.1 | all-reduce | flops 5376 | bytes 21504
  26.3 5.7 %all-gather = bf16[4,1,768]{2,1,0:T(2,128)(2,1)S(1)} all-gather(bf16[1,1,768]{2,1,0:T(2,128)(2,1)S(1)} %reshape.350), channel_id=1, replica_groups=mesh['ctx'=8,'fsdp'=4] {'fsdp'}, dimensions={0}, use_global_device_ids=true | all-gather | bytes 7680 | tf_op jit(solution)/shard_map/all_gather | solution.py:712
  32.9 10.5 %all-gather.6.cloned.1.call-done = bf16[768,2304]{1,0:T(8,128)(2,1)} async-done(((bf16[192,2304]{1,0:T(8,128)(2,1)}), bf16[768,2304]{1,0:T(8,128)(2,1)}) %all-gather.6.cloned.1.call-update) | async-done | bytes 3538960 | tf_op jit(solution)/shard_map/all_gather | solution.py:704
  43.3 3.1 fusion.24
  48.6 30.1 %exchange.4 = bf16[8,256,384]{2,1,0:T(8,128)(2,1)S(1)} custom-call(bf16[8,256,384]{2,1,0:T(8,128)(2,1)S(1)} %pad_maximum_fusion.in_ref), custom_call_target="tpu_custom_call" | custom-call | tf_op jit(solution)/shard_map/exchange/pallas_call | solution.py:466
  78.8 7.5 %attend.1 = (bf16[16,128,128]{2,1,0:T(8,128)(2,1)S(1)}, bf16[16,128,384]{2,1,0:T(8,128)(2,1)S(1)}, f32[8,128,256]{2,1,0:T(8,128)S(1)}, f32[8,1,384]{2,1,0:T(1,128)S(1)}) custom-call(s32[16]{0:T(128)S(1)} %copy-done, s32[1]{0:T(128)} %copy.146.len_ref, s32[1]{0:T(128)} %bitcast.2.spot_ref, bf16[16,128,384]{2,1,0:T(8,128)(2,1)S(1)} %bitcast.127), custom_call_target="tpu_custom_call" | custom-call | tf_op jit(solution)/shard_map/attend/pallas_call | solution.py:650
  86.3 21.3 %exchange.5 = bf16[8,256,128]{2,1,0:T(8,128)(2,1)S(1)} custom-call(bf16[8,256,128]{2,1,0:T(8,128)(2,1)S(1)} %bitcast.131), custom_call_target="tpu_custom_call" | custom-call | tf_op jit(solution)/shard_map/exchange/pallas_call | solution.py:466
  107.7 1.0 copy.107
  108.7 1.0 fusion.26
  109.7 1.0 slice_bitcast_fusion.8
  110.8 0.8 copy.110
  111.6 2.4 fusion.50
  114.3 11.7 %multiply_convert_fusion = (bf16[256,3072]{1,0:T(8,128)(2,1)}, f32[256,3072]{1,0:T(8,128)}, f32[256,3072]{1,0:T(8,128)}) fusion(f32[3072]{0:T(1024)S(1)} %bitcast.159, bf16[768,3072]{1,0:T(8,128)(2,1)} %all-gather.10.cloned.1.call-done, f32[256,768]{1,0:T(8,128)S(1)} %get-tuple-element.147, f32[768]{0:T(1024)S(1)} %convert_element_type.316, ...), kind=kOutput, calls=%fused_computation.8 | convolution fusion | flops 1260847104 | bytes 13389824 | tf_op jit(solution)/shard_map/dot_general | solution.py:756
  126.1 14.3 %all-gather.12.cloned.1.call-done = bf16[3072,768]{1,0:T(8,128)(2,1)} async-done(((bf16[768,768]{1,0:T(8,128)(2,1)}), bf16[3072,768]{1,0:T(8,128)(2,1)}) %all-gather.12.cloned.1.call-update) | async-done | bytes 4718608 | tf_op jit(solution)/shard_map/all_gather | solution.py:713
  140.4 4.4 fusion.51
  145.1 1.0 fusion.21
  146.2 0.9 convert_reduce_fusion.1
  147.3 2.8 fusion.52
  150.1 2.2 multiply_reduce_fusion
  152.3 0.9 convert_reduce_fusion
  153.2 0.9 copy-done.5
  154.9 0.8 pad_maximum_fusion.5
  155.7 1.3 copy.112
  157.0 13.2 %exchange.6 = bf16[8,256,128]{2,1,0:T(8,128)(2,1)S(1)} custom-call(bf16[8,256,128]{2,1,0:T(8,128)(2,1)S(1)} %bitcast.130), custom_call_target="tpu_custom_call" | custom-call | tf_op jit(solution)/shard_map/exchange/pallas_call | solution.py:466
  170.3 11.4 %attend_back.1 = bf16[16,128,384]{2,1,0:T(8,128)(2,1)S(1)} custom-call(s32[16]{0:T(128)S(1)} %copy-done, s32[1]{0:T(128)} %copy.146.len_ref, s32[1]{0:T(128)} %bitcast.2.spot_ref, bf16[16,128,384]{2,1,0:T(8,128)(2,1)S(1)} %get-tuple-element.20.keep_ref, bf16[16,128,128]{2,1,0:T(8,128)(2,1)S(1)} %bitcast.129, f32[8,128,256]{2,1,0:T(8,128)S(1)} %get-tuple-element.21.mix_ref, ...), custom_call_target="tpu_custom_call" | custom-call | tf_op jit(solution)/shard_map/attend_back/pallas_call | solution.py:668
  181.7 32.1 %exchange.7 = bf16[8,256,384]{2,1,0:T(8,128)(2,1)S(1)} custom-call(bf16[8,256,384]{2,1,0:T(8,128)(2,1)S(1)} %bitcast.128), custom_call_target="tpu_custom_call" | custom-call | tf_op jit(solution)/shard_map/exchange/pallas_call | solution.py:466
  215.1 0.9 fusion.45
  217.1 1.1 fusion
  218.1 4.1 copy.128
  222.3 1.0 copy-done.6
  223.5 1.5 convolution_convert_fusion.3
  225.0 4.4 convolution_convert_fusion.1
  229.5 1.3 copy-done.8
  231.1 3.6 convolution_convert_fusion
  234.9 36.4 %reduce-scatter.13.cloned.1.call-done = bf16[192,2304]{1,0:T(8,128)(2,1)} async-done(((bf16[768,2304]{1,0:T(8,128)(2,1)}), bf16[192,2304]{1,0:T(8,128)(2,1)}) %reduce-scatter.13.cloned.1.call-update) | async-done | bytes 884752
  271.3 2.3 copy.129
  273.6 26.6 %reduce-scatter.7.cloned.1.call-done = bf16[192,768]{1,0:T(8,128)(2,1)} async-done(((bf16[768,768]{1,0:T(8,128)(2,1)}), bf16[192,768]{1,0:T(8,128)(2,1)}) %reduce-scatter.7.cloned.1.call-update) | async-done | bytes 294928 | tf_op jit(solution)/shard_map/reduce_scatter | solution.py:838
  300.2 50.4 %reduce-scatter.9.cloned.1.call-done = bf16[192,3072]{1,0:T(8,128)(2,1)} async-done(((bf16[768,3072]{1,0:T(8,128)(2,1)}), bf16[192,3072]{1,0:T(8,128)(2,1)}) %reduce-scatter.9.cloned.1.call-update) | async-done | bytes 1179664 | tf_op jit(solution)/shard_map/reduce_scatter | solution.py:850
  350.6 50.6 %reduce-scatter.11.cloned.1.call-done = bf16[768,768]{1,0:T(8,128)(2,1)} async-done(((bf16[3072,768]{1,0:T(8,128)(2,1)}), bf16[768,768]{1,0:T(8,128)(2,1)}) %reduce-scatter.11.cloned.1.call-update) | async-done | bytes 1179664 | tf_op jit(solution)/shard_map/reduce_scatter | solution.py:856
  403.0 10.3 %all-reduce.19 = (bf16[768]{0:T(1024)(128)(2,1)S(1)}, bf16[768]{0:T(1024)(128)(2,1)S(1)}, bf16[768]{0:T(1024)(128)(2,1)S(1)}, bf16[768]{0:T(1024)(128)(2,1)S(1)}...) all-reduce(bf16[768]{0:T(1024)(128)(2,1)S(1)} %dynamic-update-slice, ...), channel_id=1, replica_groups=mesh['ctx'=8,'fsdp'=4] {'fsdp'}, use_global_device_ids=true, to_apply=%add.7 | all-reduce | flops 9984 | bytes 39936
  414.0 23.0 %all-reduce.17 = (bf16[192]{0:T(256)(128)(2,1)S(1)}, bf16[192]{0:T(256)(128)(2,1)S(1)}, bf16[192]{0:T(256)(128)(2,1)S(1)}, bf16[192]{0:T(256)(128)(2,1)S(1)}, bf...) all-reduce(bf16[192]{0:T(256)(128)(2,1)S(1)} %dynamic-slice.9, ...), channel_id=1, replica_groups=mesh['ctx'=8,'fsdp'=4] {'ctx'}, use_global_device_ids=true, to_apply=%region_13.14 | all-reduce | flops 2304 | bytes 9216 | tf_op jit(solution)/shard_map/psum | solution.py:871
  442.1 1.2 select_bitcast_fusion
  443.3 4.1 fusion.8
  447.4 107.0 %all-reduce.23.cloned.1.call-done = (bf16[192,2304]{0,1:T(8,128)(2,1)}, bf16[192,768]{1,0:T(8,128)(2,1)}, bf16[192,3072]{1,0:T(8,128)(2,1)}, bf16[768,768]{1,0:T(8,128)(2,1)}) async-done(((bf16[192,2304]{0,1:T(8,128)(2,1)}, bf16[192,768]{1,0:T(8,128)(2,1)}, bf16[192,3072]{1,0:T(8,128)(2,1)}, bf16[768,768]{1,0:T(8,128)(2,1)}), (bf16[192,2304]{0,1:T(8,128)(2,1)}, bf16[192,768]{1,0:T(8,128)(2,1)}, ...) | async-done | bytes 3538960 | tf_op jit(solution)/shard_map/psum | solution.py:870
  554.4 2.6 copy.127
  557.1 0.9 convert_element_type.347
  557.9 1.7 convert_element_type.354
  559.6 1.6 convert_element_type.357
  (236 shorter events, 17.8 us)
Async XLA Ops:
  7.2 4.2 copy-start.43
  7.2 4.5 copy-start.44
  7.2 4.7 copy-start.45
  7.2 4.9 copy-start.46
  7.2 5.1 copy-start.47
  7.2 5.4 copy-start.48
  7.3 5.6 copy-start.49
  7.3 19.0 %copy-start.42 = (bf16[768]{0:T(1024)(128)(2,1)S(1)}, bf16[768]{0:T(1024)(128)(2,1)}, u32[]{:S(2)}) copy-start(bf16[768]{0:T(1024)(128)(2,1)} %param.29) | copy-start | bytes 4612
  7.3 25.5 %copy-start = (s32[16]{0:T(128)S(1)}, s32[16]{0:T(128)}, u32[]{:S(2)}) copy-start(s32[16]{0:T(128)} %pair_ref.3) | copy-start | bytes 196
  7.3 36.1 %copy-start.12 = (bf16[1,256,768]{2,1,0:T(8,128)(2,1)S(1)}, bf16[1,256,768]{2,1,0:T(8,128)(2,1)}, u32[]{:S(2)}) copy-start(bf16[1,256,768]{2,1,0:T(8,128)(2,1)} %param.17) | copy-start | bytes 1179652
  7.3 36.0 %all-gather.6.cloned.1.call-start = ((), (), s32[]{:S(2)}) async-start(), calls=%async_computation.4 | async-start | bytes 4423680 | tf_op jit(solution)/shard_map/all_gather | solution.py:704
  8.0 103.6 %all-gather.8.cloned.1.call-start = ((), (), s32[]{:S(2)}) async-start(), calls=%async_computation.5 | async-start | bytes 1474560 | tf_op jit(solution)/shard_map/all_gather | solution.py:707
  8.8 105.5 %all-gather.10.cloned.1.call-start = ((), (), s32[]{:S(2)}) async-start(), calls=%async_computation.6 | async-start | bytes 5898240 | tf_op jit(solution)/shard_map/all_gather | solution.py:711
  9.5 130.9 %all-gather.12.cloned.1.call-start = ((), (), s32[]{:S(2)}) async-start(), calls=%async_computation.7 | async-start | bytes 5898240 | tf_op jit(solution)/shard_map/all_gather | solution.py:713
  10.1 261.2 %reduce-scatter.13.cloned.1.call-start = ((), (), s32[]{:S(2)}) async-start(), calls=%async_computation.11 | async-start | bytes 4423680
  32.9 113.3 %copy-start.32 = (pred[256]{0:T(512)(128)(4,1)}, pred[256]{0:T(512)(128)(4,1)S(1)}, u32[]{:S(2)}) copy-start(pred[256]{0:T(512)(128)(4,1)S(1)} %fusion.32) | copy-start | bytes 772
  114.0 38.3 %copy-start.1 = (f32[256,768]{1,0:T(8,128)}, f32[256,768]{1,0:T(8,128)S(1)}, u32[]{:S(2)}) copy-start(f32[256,768]{1,0:T(8,128)S(1)} %get-tuple-element.147) | copy-start | bytes 2359300
  114.0 38.3 %copy-start.26 = (f32[256]{0:T(256)}, f32[256]{0:T(256)S(1)}, u32[]{:S(2)}) copy-start(f32[256]{0:T(256)S(1)} %broadcast_multiply_fusion.5) | copy-start | bytes 3076
  114.3 38.0 %copy-start.29 = (f32[256]{0:T(256)}, f32[256]{0:T(256)S(1)}, u32[]{:S(2)}) copy-start(f32[256]{0:T(256)S(1)} %add_rsqrt_fusion.1) | copy-start | bytes 3076
  140.4 6.7 %slice-start.2 = ((s8[4718592]{0:T(1024)(128)(4,1)}), s8[4194304]{0:T(1024)(128)(4,1)S(1)}, s32[]{:S(2)}) async-start(s8[4718592]{0:T(1024)(128)(4,1)} %bitcast.162), calls=%async_computation.15 | async-start | bytes 8388608
  140.4 4.7 copy-start.14
  140.4 6.7 %slice-start.3 = ((s8[4718592]{0:T(1024)(128)(4,1)}), s8[524288]{0:T(1024)(128)(4,1)S(1)}, s32[]{:S(2)}) async-start(s8[4718592]{0:T(1024)(128)(4,1)} %bitcast.162), calls=%async_computation.16 | async-start | bytes 1048576
  140.4 6.7 %copy-start.52 = (f32[256,3072]{1,0:T(8,128)S(1)}, f32[256,3072]{1,0:T(8,128)}, u32[]{:S(2)}) copy-start(f32[256,3072]{1,0:T(8,128)} %get-tuple-element.148) | copy-start | bytes 9437188
  145.1 4.9 copy-start.27
  146.1 3.9 slice-start
  150.0 4.1 copy-start.7
  222.3 78.0 %reduce-scatter.7.cloned.1.call-start = ((), (), s32[]{:S(2)}) async-start(), calls=%async_computation.8 | async-start | bytes 1474560 | tf_op jit(solution)/shard_map/reduce_scatter | solution.py:838
  225.0 125.7 %reduce-scatter.9.cloned.1.call-start = ((), (), s32[]{:S(2)}) async-start(), calls=%async_computation.9 | async-start | bytes 5898240 | tf_op jit(solution)/shard_map/reduce_scatter | solution.py:850
  229.5 171.7 %reduce-scatter.11.cloned.1.call-start = ((), (), s32[]{:S(2)}) async-start(), calls=%async_computation.10 | async-start | bytes 5898240 | tf_op jit(solution)/shard_map/reduce_scatter | solution.py:856
  234.7 167.9 %copy-start.50 = (bf16[192]{0:T(256)(128)(2,1)S(1)}, bf16[192]{0:T(256)(128)(2,1)}, u32[]{:S(2)}) copy-start(bf16[192]{0:T(256)(128)(2,1)} %param.33) | copy-start | bytes 1156
  234.7 168.1 %copy-start.31 = (bf16[4,3,64]{2,0,1:T(4,128)(2,1)S(1)}, bf16[4,3,64]{2,0,1:T(4,128)(2,1)}, u32[]{:S(2)}) copy-start(bf16[4,3,64]{2,0,1:T(4,128)(2,1)} %get-tuple-element.154) | copy-start | bytes 4612
  234.7 168.2 %copy-start.30 = (bf16[4,3,64]{2,0,1:T(4,128)(2,1)S(1)}, bf16[4,3,64]{2,0,1:T(4,128)(2,1)}, u32[]{:S(2)}) copy-start(bf16[4,3,64]{2,0,1:T(4,128)(2,1)} %get-tuple-element.125) | copy-start | bytes 4612
  234.7 168.3 %copy-start.34 = (bf16[768]{0:T(1024)(128)(2,1)S(1)}, bf16[768]{0:T(1024)(128)(2,1)}, u32[]{:S(2)}) copy-start(bf16[768]{0:T(1024)(128)(2,1)} %get-tuple-element.85) | copy-start | bytes 4612
  234.8 168.3 %copy-start.35 = (bf16[768]{0:T(1024)(128)(2,1)S(1)}, bf16[768]{0:T(1024)(128)(2,1)}, u32[]{:S(2)}) copy-start(bf16[768]{0:T(1024)(128)(2,1)} %get-tuple-element.90) | copy-start | bytes 4612
  234.8 168.2 %copy-start.36 = (bf16[768]{0:T(1024)(128)(2,1)S(1)}, bf16[768]{0:T(1024)(128)(2,1)}, u32[]{:S(2)}) copy-start(bf16[768]{0:T(1024)(128)(2,1)} %get-tuple-element.121) | copy-start | bytes 4612
  234.8 168.2 %copy-start.37 = (bf16[768]{0:T(1024)(128)(2,1)S(1)}, bf16[768]{0:T(1024)(128)(2,1)}, u32[]{:S(2)}) copy-start(bf16[768]{0:T(1024)(128)(2,1)} %get-tuple-element.123) | copy-start | bytes 4612
  234.8 168.2 %copy-start.38 = (bf16[3072]{0:T(1024)(128)(2,1)S(1)}, bf16[3072]{0:T(1024)(128)(2,1)}, u32[]{:S(2)}) copy-start(bf16[3072]{0:T(1024)(128)(2,1)} %get-tuple-element.152) | copy-start | bytes 18436
  234.8 168.2 %copy-start.39 = (bf16[768]{0:T(1024)(128)(2,1)S(1)}, bf16[768]{0:T(1024)(128)(2,1)}, u32[]{:S(2)}) copy-start(bf16[768]{0:T(1024)(128)(2,1)} %get-tuple-element.83) | copy-start | bytes 4612
  234.8 168.2 %copy-start.40 = (bf16[768]{0:T(1024)(128)(2,1)S(1)}, bf16[768]{0:T(1024)(128)(2,1)}, u32[]{:S(2)}) copy-start(bf16[768]{0:T(1024)(128)(2,1)} %get-tuple-element.88) | copy-start | bytes 4612
  234.8 207.3 %copy-start.4 = (f32[256,768]{1,0:T(8,128)S(1)}, f32[256,768]{1,0:T(8,128)}, u32[]{:S(2)}) copy-start(f32[256,768]{1,0:T(8,128)} %copy-done.3) | copy-start | bytes 2359300
  234.8 207.3 %copy-start.28 = (f32[256]{0:T(256)S(1)}, f32[256]{0:T(256)}, u32[]{:S(2)}) copy-start(f32[256]{0:T(256)} %copy-done.27) | copy-start | bytes 3076
  234.8 207.3 %copy-start.33 = (pred[256]{0:T(512)(128)(4,1)S(1)}, pred[256]{0:T(512)(128)(4,1)}, u32[]{:S(2)}) copy-start(pred[256]{0:T(512)(128)(4,1)} %copy-done.32) | copy-start | bytes 772
  234.8 319.6 %all-reduce.23.cloned.1.call-start = ((), (), s32[]{:S(2)}) async-start(), calls=%async_computation.12 | async-start | bytes 7667712 | tf_op jit(solution)/shard_map/psum | solution.py:870
  273.6 169.7 %copy-start.20 = (bf16[256,4,3,64]{0,3,2,1:T(8,128)(2,1)S(1)}, bf16[256,4,3,64]{0,3,2,1:T(8,128)(2,1)}, u32[]{:S(2)}) copy-start(bf16[256,4,3,64]{0,3,2,1:T(8,128)(2,1)} %copy-done.19) | copy-start | bytes 1179652
  273.6 169.7 %copy-start.22 = (bf16[256,4,3,64]{0,3,2,1:T(8,128)(2,1)S(1)}, bf16[256,4,3,64]{0,3,2,1:T(8,128)(2,1)}, u32[]{:S(2)}) copy-start(bf16[256,4,3,64]{0,3,2,1:T(8,128)(2,1)} %copy-done.21) | copy-start | bytes 1179652
  273.6 169.7 %copy-start.24 = (bf16[256,4,3,64]{0,3,2,1:T(8,128)(2,1)S(1)}, bf16[256,4,3,64]{0,3,2,1:T(8,128)(2,1)}, u32[]{:S(2)}) copy-start(bf16[256,4,3,64]{0,3,2,1:T(8,128)(2,1)} %copy-done.23) | copy-start | bytes 1179652
  554.4 3.5 copy-start.18
  554.4 5.2 copy-start.17
  (18 other events, 33.6 us)
Sparse Core Ops, SparseCore 0:
  9.7 33.6 all-gather.5
  44.9 17.4 all-gather.7
  64.0 37.4 all-gather.9
  102.9 37.4 all-gather.11
  222.4 48.8 reduce-scatter.12
  274.5 25.7 reduce-scatter.6
  302.8 47.8 reduce-scatter.8
  353.3 47.8 reduce-scatter.10
  405.8 148.5 all-reduce.22

commit v2 on v1

--- a/solution.py
+++ b/solution.py
@@ -681,6 +681,231 @@
     )(pairing, lengths, spot, keep, grad, mix, lse)
 
 
+PARTS = 12
+
+
+def sum_sources(chunk):
+    left = jnp.where(chunk < 4, 3 + chunk, jnp.where(chunk < 8, 2, jnp.where(chunk < 9, 1, 0)))
+    right = jnp.where(
+        chunk < 4, 8, jnp.where(chunk < 8, chunk, jnp.where(chunk < 9, 3, chunk - 9))
+    )
+    return left, right
+
+
+def sum_kernel(
+    left_ref, right_ref, small_ref, out_ref, small_out,
+    pair_out, pair_in, x_out, x_in, first_sum, y_out, y_in, half_sum, z_out, z_in,
+    s_pair, s_x_out, s_x, s_y_out, s_y, s_z_out, s_z,
+    pair_sem, x_sem, y_sem, z_sem, spread_sem, last_sem, s_sem,
+):
+    ctx = lax.axis_index("ctx")
+    fsdp = lax.axis_index("fsdp")
+    z, y = ctx // 2, lax.rem(ctx, 2)
+    x, core = fsdp // 2, lax.rem(fsdp, 2)
+    sibling = {"fsdp": 2 * x + 1 - core}
+    across = {"fsdp": 2 * (1 - x) + core}
+    beside = {"ctx": 2 * z + 1 - y}
+    along = [{"ctx": 2 * lax.rem(z + k, 4) + y} for k in (1, 2, 3)]
+    barrier = pltpu.get_barrier_semaphore()
+    for peer in [sibling, across, beside] + along:
+        pl.semaphore_signal(barrier, inc=1, device_id=peer, device_id_type=MESH)
+    pl.semaphore_wait(barrier, 6)
+
+    def copy(src, dst, sems, at, peer):
+        return pltpu.make_async_remote_copy(
+            src_ref=src, dst_ref=dst, send_sem=sems.at[(0,) + at], recv_sem=sems.at[(1,) + at],
+            device_id=peer, device_id_type=MESH,
+        )
+
+    def pair_copy(c):
+        return copy(pair_out.at[c], pair_in.at[c], pair_sem, (c,), sibling)
+
+    def x_copy(c):
+        return copy(x_out.at[c], x_in.at[c], x_sem, (c,), across)
+
+    def y_copy(c):
+        return copy(y_out.at[c], y_in.at[c], y_sem, (c,), beside)
+
+    def z_copy(c, k):
+        return copy(
+            z_out.at[c, lax.rem(z + k, 4)], z_in.at[c, k - 1], z_sem, (c, k - 1), along[k - 1]
+        )
+
+    def spread_copy(c, k):
+        piece = out_ref.at[c, y, z]
+        return copy(piece, piece, spread_sem, (c, k - 1), along[k - 1])
+
+    def last_copy(c):
+        return copy(out_ref.at[c, y], out_ref.at[c, y], last_sem, (c,), beside)
+
+    def partial(c, shard):
+        left, right = sum_sources(c)
+        return jnp.dot(left_ref[left, shard], right_ref[right], preferred_element_type=jnp.float32)
+
+    low = jnp.bfloat16
+
+    def stage_pair(c):
+        for side in range(2):
+            pair_out[c, side] = partial(c, 2 * side + 1 - core).astype(low)
+        pair_copy(c).start()
+
+    def stage_x(c):
+        pair_copy(c).wait_recv()
+        x_out[c] = (
+            partial(c, 2 * (1 - x) + core) + pair_in[c, 1 - x].astype(jnp.float32)
+        ).astype(low)
+        x_copy(c).start()
+        first_sum[lax.rem(c, 2)] = partial(c, 2 * x + core) + pair_in[c, x].astype(jnp.float32)
+
+    def stage_y(c):
+        x_copy(c).wait_recv()
+        total = first_sum[lax.rem(c, 2)] + x_in[c].astype(jnp.float32)
+        here, there = total[:, :384], total[:, 384:]
+        y_out[c] = jnp.where(y == 0, there, here).astype(low)
+        y_copy(c).start()
+        half_sum[lax.rem(c, 2)] = jnp.where(y == 0, here, there)
+
+    def stage_z(c):
+        y_copy(c).wait_recv()
+        total = half_sum[lax.rem(c, 2)] + y_in[c].astype(jnp.float32)
+        z_out[c] = total.astype(low).reshape(4, 48, 384)
+        for k in (1, 2, 3):
+            z_copy(c, k).start()
+        half_sum[lax.rem(c, 2)] = total
+
+    def stage_spread(c):
+        total = half_sum[lax.rem(c, 2), pl.ds(pl.multiple_of(48 * z, 48), 48)]
+        for k in (1, 2, 3):
+            z_copy(c, k).wait_recv()
+            total = total + z_in[c, k - 1].astype(jnp.float32)
+        out_ref[c, y, z] = total.astype(low)
+        for k in (1, 2, 3):
+            spread_copy(c, k).start()
+
+    def stage_last(c):
+        for k in (1, 2, 3):
+            spread_copy(c, k).wait_recv()
+        last_copy(c).start()
+
+    stages = [stage_pair, stage_x, stage_y, stage_z, stage_spread, stage_last]
+    order = [0, 1, 4, 2, 3, 5]
+
+    def small_step(t):
+        def s_copy(src, dst, k, peer):
+            return copy(src, dst, s_sem, (k,), peer)
+
+        send_pair = s_copy(s_pair.at[0], s_pair.at[1], 0, sibling)
+        send_x = s_copy(s_x_out, s_x, 1, across)
+        send_y = s_copy(s_y_out, s_y, 2, beside)
+        send_z = [s_copy(s_z_out, s_z.at[k], 3 + k, along[k]) for k in range(3)]
+
+        @pl.when(t == 0)
+        def _():
+            for side in range(2):
+                s_pair[0, side] = small_ref[2 * side + 1 - core]
+            send_pair.start()
+
+        @pl.when(t == 1)
+        def _():
+            send_pair.wait()
+            s_x_out[...] = small_ref[2 * (1 - x) + core] + s_pair[1, 1 - x]
+            send_x.start()
+
+        @pl.when(t == 2)
+        def _():
+            send_x.wait()
+            s_y_out[...] = small_ref[2 * x + core] + s_pair[1, x] + s_x[...]
+            send_y.start()
+
+        @pl.when(t == 3)
+        def _():
+            send_y.wait()
+            s_z_out[...] = s_y_out[...] + s_y[...]
+            for cp in send_z:
+                cp.start()
+
+        @pl.when(t == 4)
+        def _():
+            for cp in send_z:
+                cp.wait()
+            total = jnp.zeros_like(s_z_out)
+            for place in range(4):
+                k = lax.rem(place - z + 4, 4)
+                behind = 4 - k
+                other = s_z[jnp.where(k == 0, 0, behind - 1)]
+                total = total + jnp.where(k == 0, s_z_out[...], other)
+            small_out[...] = total
+
+    def slot(t, carry):
+        small_step(t)
+        for index in order:
+            c = t - index
+
+            @pl.when((c >= 0) & (c < PARTS))
+            def _():
+                stages[index](c)
+
+        return carry
+
+    lax.fori_loop(0, PARTS + 5, slot, 0)
+
+    def drain(c, carry):
+        pair_copy(c).wait_send()
+        x_copy(c).wait_send()
+        y_copy(c).wait_send()
+        for k in (1, 2, 3):
+            z_copy(c, k).wait_send()
+            spread_copy(c, k).wait_send()
+        last_copy(c).wait()
+        return carry
+
+    lax.fori_loop(0, PARTS, drain, 0)
+
+
+def sum_all(left, right, small, name):
+    low, wide = jnp.bfloat16, jnp.float32
+    dma = pltpu.SemaphoreType.DMA
+    return pl.pallas_call(
+        sum_kernel,
+        out_shape=(
+            jax.ShapeDtypeStruct((PARTS, 2, 4, 48, 384), low),
+            jax.ShapeDtypeStruct(small.shape[1:], wide),
+        ),
+        in_specs=[vmem(), vmem(), vmem()],
+        out_specs=(vmem(), vmem()),
+        scratch_shapes=[
+            pltpu.VMEM((PARTS, 2, 192, 768), low),
+            pltpu.VMEM((PARTS, 2, 192, 768), low),
+            pltpu.VMEM((PARTS, 192, 768), low),
+            pltpu.VMEM((PARTS, 192, 768), low),
+            pltpu.VMEM((2, 192, 768), wide),
+            pltpu.VMEM((PARTS, 192, 384), low),
+            pltpu.VMEM((PARTS, 192, 384), low),
+            pltpu.VMEM((2, 192, 384), wide),
+            pltpu.VMEM((PARTS, 4, 48, 384), low),
+            pltpu.VMEM((PARTS, 3, 48, 384), low),
+            pltpu.VMEM((2, 2) + small.shape[1:], wide),
+            pltpu.VMEM(small.shape[1:], wide),
+            pltpu.VMEM(small.shape[1:], wide),
+            pltpu.VMEM(small.shape[1:], wide),
+            pltpu.VMEM(small.shape[1:], wide),
+            pltpu.VMEM(small.shape[1:], wide),
+            pltpu.VMEM((3,) + small.shape[1:], wide),
+            dma((2, PARTS)),
+            dma((2, PARTS)),
+            dma((2, PARTS)),
+            dma((2, PARTS, 3)),
+            dma((2, PARTS, 3)),
+            dma((2, PARTS)),
+            dma((2, 6)),
+        ],
+        compiler_params=pltpu.CompilerParams(
+            collective_id=name, has_side_effects=True, vmem_limit_bytes=58 << 20
+        ),
+        name="sum_all",
+    )(left, right, small)
+
+
 def on_device_spread(
     tokens,
     cotangent,
@@ -778,14 +1003,10 @@
         resid_two, gain_two_back.astype(jnp.float32), grad_y
     )
     grad_mixed = grad_resid_two.astype(jnp.bfloat16)
-    back_grad = jnp.einsum("tf,td->fd", active_low, grad_mixed, preferred_element_type=jnp.float32)
     back_bias_grad = jnp.sum(grad_mixed.astype(jnp.float32), axis=0)
     grad_active = jnp.einsum("td,fd->tf", grad_mixed, back_back, preferred_element_type=jnp.float32)
     (grad_upper,) = gelu_back(grad_active)
     grad_upper_low = grad_upper.astype(jnp.bfloat16)
-    in_grad = jnp.einsum(
-        "td,tf->df", hidden_low, grad_upper_low, preferred_element_type=jnp.float32
-    )
     in_bias_grad = jnp.sum(grad_upper_low.astype(jnp.float32), axis=0)
     grad_hidden = grad_resid_two + jnp.einsum(
         "tf,df->td", grad_upper_low, in_back, preferred_element_type=jnp.float32
@@ -794,9 +1015,6 @@
         resid_one, gain_one_back.astype(jnp.float32), grad_hidden
     )
     grad_branch = grad_resid_one.astype(jnp.bfloat16)
-    out_grad = jnp.einsum(
-        "tc,td->cd", attended_low, grad_branch, preferred_element_type=jnp.float32
-    )
     out_bias_grad = jnp.sum(grad_branch.astype(jnp.float32), axis=0)
     grad_attended = jnp.einsum(
         "td,cd->tc", grad_branch, out_back, preferred_element_type=jnp.float32
@@ -804,84 +1022,57 @@
     grad_in = exchange(split_heads(grad_attended), 2).reshape(-1, half, 2 * HEAD_DIM)
     grad_blocks = attend_back(pairing, lengths, spot, keep, grad_in, mix, lse)
     grad_proj = join_parts(exchange(grad_blocks.reshape(-1, rows, 6 * HEAD_DIM), 3))
-    qkv_grad = jnp.einsum("td,tf->df", inputs, grad_proj, preferred_element_type=jnp.float32)
     query_bias_grad = jnp.sum(grad_proj[:, :width].astype(jnp.float32), axis=0)
     value_bias_grad = jnp.sum(grad_proj[:, 2 * width :].astype(jnp.float32), axis=0)
     token_grad = grad_resid_one + jnp.einsum(
         "tf,df->td", grad_proj, qkv_back, preferred_element_type=jnp.float32
     )
-    grads = (
-        qkv_grad,
-        query_bias_grad,
-        value_bias_grad,
-        out_grad,
-        out_bias_grad,
-        gain_one_grad,
-        shift_one_grad,
-        in_grad,
-        in_bias_grad,
-        back_grad,
-        back_bias_grad,
-        gain_two_grad,
-        shift_two_grad,
-    )
-    shards = (
-        lax.psum_scatter(
-            grads[0].astype(jnp.bfloat16), "fsdp", scatter_dimension=0, tiled=True
-        ).astype(jnp.float32),
-        lax.psum_scatter(
-            grads[1].astype(jnp.bfloat16), "fsdp", scatter_dimension=0, tiled=True
-        ).astype(jnp.float32),
-        lax.psum_scatter(
-            grads[2].astype(jnp.bfloat16), "fsdp", scatter_dimension=0, tiled=True
-        ).astype(jnp.float32),
-        lax.psum_scatter(
-            grads[3].astype(jnp.bfloat16), "fsdp", scatter_dimension=0, tiled=True
-        ).astype(jnp.float32),
-        lax.psum_scatter(
-            grads[4].astype(jnp.bfloat16), "fsdp", scatter_dimension=0, tiled=True
-        ).astype(jnp.float32),
-        lax.psum_scatter(
-            grads[5].astype(jnp.bfloat16), "fsdp", scatter_dimension=0, tiled=True
-        ).astype(jnp.float32),
-        lax.psum_scatter(
-            grads[6].astype(jnp.bfloat16), "fsdp", scatter_dimension=0, tiled=True
-        ).astype(jnp.float32),
-        lax.psum_scatter(
-            grads[7].astype(jnp.bfloat16), "fsdp", scatter_dimension=0, tiled=True
-        ).astype(jnp.float32),
-        lax.psum_scatter(
-            grads[8].astype(jnp.bfloat16), "fsdp", scatter_dimension=0, tiled=True
-        ).astype(jnp.float32),
-        lax.psum_scatter(
-            grads[9].astype(jnp.bfloat16), "fsdp", scatter_dimension=0, tiled=True
-        ).astype(jnp.float32),
-        lax.psum_scatter(
-            grads[10].astype(jnp.bfloat16), "fsdp", scatter_dimension=0, tiled=True
-        ).astype(jnp.float32),
-        lax.psum_scatter(
-            grads[11].astype(jnp.bfloat16), "fsdp", scatter_dimension=0, tiled=True
-        ).astype(jnp.float32),
-        lax.psum_scatter(
-            grads[12].astype(jnp.bfloat16), "fsdp", scatter_dimension=0, tiled=True
-        ).astype(jnp.float32),
-    )
-    totals = (
-        lax.psum(shards[0].astype(jnp.bfloat16), "ctx").astype(jnp.float32),
-        lax.psum(shards[1].astype(jnp.bfloat16), "ctx").astype(jnp.float32),
-        lax.psum(shards[2].astype(jnp.bfloat16), "ctx").astype(jnp.float32),
-        lax.psum(shards[3].astype(jnp.bfloat16), "ctx").astype(jnp.float32),
-        lax.psum(shards[4].astype(jnp.bfloat16), "ctx").astype(jnp.float32),
-        lax.psum(shards[5].astype(jnp.bfloat16), "ctx").astype(jnp.float32),
-        lax.psum(shards[6].astype(jnp.bfloat16), "ctx").astype(jnp.float32),
-        lax.psum(shards[7].astype(jnp.bfloat16), "ctx").astype(jnp.float32),
-        lax.psum(shards[8].astype(jnp.bfloat16), "ctx").astype(jnp.float32),
-        lax.psum(shards[9].astype(jnp.bfloat16), "ctx").astype(jnp.float32),
-        lax.psum(shards[10].astype(jnp.bfloat16), "ctx").astype(jnp.float32),
-        lax.psum(shards[11].astype(jnp.bfloat16), "ctx").astype(jnp.float32),
-        lax.psum(shards[12].astype(jnp.bfloat16), "ctx").astype(jnp.float32),
-    )
-    return (output[None], token_grad[None]) + tuple(totals)
+    def wide(value):
+        return jnp.transpose(value).reshape(4, -1, rows)
+
+    tall = jnp.transpose(active_low).reshape(4, 4, width // 4, rows)
+    left = jnp.concatenate(
+        [
+            jnp.stack([wide(inputs), wide(attended_low), wide(hidden_low)]),
+            jnp.transpose(tall, (1, 0, 2, 3)),
+        ]
+    )
+    right = jnp.stack(
+        jnp.split(grad_proj, 3, axis=1)
+        + [grad_branch]
+        + jnp.split(grad_upper_low, 4, axis=1)
+        + [grad_mixed]
+    )
+    vectors = [
+        query_bias_grad, value_bias_grad, out_bias_grad, gain_one_grad, shift_one_grad,
+        back_bias_grad, gain_two_grad, shift_two_grad,
+    ]
+    small = jnp.concatenate(
+        [jnp.stack([v.reshape(4, -1) for v in vectors], axis=1), in_bias_grad.reshape(4, 4, -1)],
+        axis=1,
+    )
+    small = jnp.pad(small, ((0, 0), (0, 4), (0, 64)))
+    sums, small_sum = sum_all(left, right, small, 4)
+    panels = jnp.transpose(sums, (0, 2, 3, 1, 4)).reshape(PARTS, width // 4, width)
+    panels = panels.astype(jnp.float32)
+    lines = [small_sum[i, : width // 4] for i in range(8)]
+    return (
+        output[None],
+        token_grad[None],
+        jnp.concatenate([panels[9], panels[10], panels[11]], axis=1),
+        lines[0],
+        lines[1],
+        panels[8],
+        lines[2],
+        lines[3],
+        lines[4],
+        jnp.concatenate([panels[4], panels[5], panels[6], panels[7]], axis=1),
+        small_sum[8:12, : width // 4].reshape(-1),
+        panels[:4].reshape(-1, width),
+        lines[5],
+        lines[6],
+        lines[7],
+    )
 
 
 def solution(mesh):

time: 571 us -> 446 us (0.78)
  waiting for transfers between devices: 299 us -> 23 us
  Pallas kernels: 116 us -> 248 us
  local copies, waits for them, and re-layouts: 24.3 us -> 65.3 us
  blocking collectives: 52.2 us -> 18.4 us
  other arithmetic: 17.2 us -> 39.5 us
  matrix products: 41.9 us -> 29.3 us
    pallas_call x0 -> x1, Pallas kernels: none -> 133 us  [sum_all(): pl.pallas_call(sum_kernel, out_shape=(jax.ShapeDtypeStruct((PARTS, 2, 4,...]
    reduce_scatter x3 -> x0, waiting for transfers between devices: 128 us -> none  [the longest x1 50.6 us: on_device_spread(): lax.psum_scatter(grads[9].astype(jnp.bfloat16), 'fsdp', scatter_dimension...]
    psum x1 -> x0, waiting for transfers between devices: 107 us -> none  [on_device_spread(): lax.psum(shards[0].astype(jnp.bfloat16), 'ctx').astype(jnp.float32)]
    unnamed x10 -> x4, waiting for transfers between devices: 39.1 us -> 2.58 us
    psum x1 -> x0, blocking collectives: 23 us -> none  [on_device_spread(): lax.psum(shards[1].astype(jnp.bfloat16), 'ctx').astype(jnp.float32)]
    dot_general x4 -> x0, matrix products: 10.6 us -> none  [the longest x1 4.42 us: on_device_spread(): jnp.einsum('td,tf->df', hidden_low, grad_upper_low, preferred_element_typ...]
    another operation x0 -> x11, local copies, waits for them, and re-layouts: none -> 10.5 us  [the longest x8 7.38 us: on_device_spread(): jnp.stack([v.reshape(4, -1) for v in vectors], axis=1)]
    unnamed x2 -> x1, blocking collectives: 23.4 us -> 13.2 us
  transfers between devices with their start and end apart: 9 -> 4, of which waited for: 7 -> 2; matrix products, arithmetic and copies ran while one was open for 9% -> 7% of each run, Pallas kernels for 10% -> 13%
where the time goes in v2:
time: 446 us; the launch traced here: 440 us
  Pallas kernels  248 us (56%)
  local copies, waits for them, and re-layouts  65.3 us (15%)
  other arithmetic  39.5 us (9%)
  matrix products  29.3 us (7%)
  waiting for transfers between devices  23 us (5%)
  blocking collectives  18.4 us (4%)
  between operations  16.5 us (4%)
    pallas_call x1, Pallas kernels, sum_all(): pl.pallas_call(sum_kernel, out_shape=(jax.ShapeDtypeStruct((PARTS, 2, 4,...  133 us
    pallas_call x4, Pallas kernels, exchange(): pl.pallas_call(functools.partial(exchange_kernel, n), out_shape=jax.Shape...  96.8 us
    unnamed x142, local copies, waits for them, and re-layouts  21.8 us
    all_gather x1, waiting for transfers between devices, on_device_spread(): lax.all_gather(w_back, 'fsdp', axis=0, tiled=True)  15 us
    unnamed x1, blocking collectives  13.2 us
    dot_general x1, matrix products, on_device_spread(): jnp.dot(hidden_low, in_all, preferred_element_type=jnp.float32)  11.4 us
    pallas_call x1, Pallas kernels, attend_back(): pl.pallas_call(functools.partial(attend_back_kernel, chunks), out_shape=j...  11.1 us
  transfers between devices with their start and end apart: 4, of which 2 were waited for; matrix products, arithmetic and copies ran while one was open for 7% of the time, Pallas kernels for 13%

profile of v2, /device:TPU:0, one launch (start us, length us, event | category | flops | bytes accessed | tf_op | source)
XLA Modules:
  0.0 440.0 jit_solution(15287025498232605157)
XLA Ops:
  13.3 13.2 %all-reduce.9 = (bf16[768]{0:T(1024)(128)(2,1)S(1)}, bf16[768]{0:T(1024)(128)(2,1)S(1)}, bf16[768]{0:T(1024)(128)(2,1)S(1)}, bf16[768]{0:T(1024)(128)(2,1)S(1)},...) all-reduce(bf16[768]{0:T(1024)(128)(2,1)S(1)} %dynamic-update-slice, ...), channel_id=1, replica_groups=mesh['ctx'=8,'fsdp'=4] {'fsdp'}, use_global_device_ids=true, to_apply=%add.2 | all-reduce | flops 6144 | bytes 24576
  28.9 5.2 %all-gather = bf16[4,1,768]{2,1,0:T(2,128)(2,1)S(1)} all-gather(bf16[1,1,768]{2,1,0:T(2,128)(2,1)S(1)} %reshape.388), channel_id=1, replica_groups=mesh['ctx'=8,'fsdp'=4] {'fsdp'}, dimensions={0}, use_global_device_ids=true | all-gather | bytes 7680 | tf_op jit(solution)/shard_map/all_gather | solution.py:937
  38.0 5.3 %all-gather.6.cloned.1.call-done = bf16[768,2304]{1,0:T(8,128)(2,1)} async-done(((bf16[192,2304]{1,0:T(8,128)(2,1)}), bf16[768,2304]{1,0:T(8,128)(2,1)}) %all-gather.6.cloned.1.call-update) | async-done | bytes 3538960 | tf_op jit(solution)/shard_map/all_gather | solution.py:929
  43.4 3.1 fusion.51
  48.6 30.1 %exchange.4 = bf16[8,256,384]{2,1,0:T(8,128)(2,1)S(1)} custom-call(bf16[8,256,384]{2,1,0:T(8,128)(2,1)S(1)} %pad_maximum_fusion.3.in_ref), custom_call_target="tpu_custom_call" | custom-call | tf_op jit(solution)/shard_map/exchange/pallas_call | solution.py:466
  78.7 7.3 %attend.1 = (bf16[16,128,128]{2,1,0:T(8,128)(2,1)S(1)}, bf16[16,128,384]{2,1,0:T(8,128)(2,1)S(1)}, f32[8,128,256]{2,1,0:T(8,128)S(1)}, f32[8,1,384]{2,1,0:T(1,128)S(1)}) custom-call(s32[16]{0:T(128)S(1)} %copy-done, s32[1]{0:T(128)} %copy.217.len_ref, s32[1]{0:T(128)} %bitcast.2.spot_ref, bf16[16,128,384]{2,1,0:T(8,128)(2,1)S(1)} %bitcast.241), custom_call_target="tpu_custom_call" | custom-call | tf_op jit(solution)/shard_map/attend/pallas_call | solution.py:650
  86.0 21.3 %exchange.5 = bf16[8,256,128]{2,1,0:T(8,128)(2,1)S(1)} custom-call(bf16[8,256,128]{2,1,0:T(8,128)(2,1)S(1)} %bitcast.245), custom_call_target="tpu_custom_call" | custom-call | tf_op jit(solution)/shard_map/exchange/pallas_call | solution.py:466
  110.7 2.1 fusion.73
  113.9 11.4 %fusion = (f32[256,3072]{1,0:T(8,128)}, f32[256,3072]{1,0:T(8,128)}) fusion(f32[3072]{0:T(1024)S(1)} %bitcast.298, bf16[768,3072]{1,0:T(8,128)(2,1)} %all-gather.10.cloned.1.call-done, f32[256,768]{1,0:T(8,128)} %copy-done.2, f32[768]{0:T(1024)S(1)} %copy-done.30, f32[768]{0:T(1024)S(1)} %copy-done.29, f32[256]{0:T(256)S(1)} %add_rsqrt_fusion.1, ...), kind=kOutput, calls=%fused_computation.4 | convolution fusion | flops 1258487808 | bytes 11816960 | tf_op jit(solution)/shard_map/dot_general | solution.py:981
  125.4 15.0 %all-gather.12.cloned.1.call-done = bf16[3072,768]{1,0:T(8,128)(2,1)} async-done(((bf16[768,768]{1,0:T(8,128)(2,1)}), bf16[3072,768]{1,0:T(8,128)(2,1)}) %all-gather.12.cloned.1.call-update) | async-done | bytes 4718608 | tf_op jit(solution)/shard_map/all_gather | solution.py:938
  140.5 6.0 %fusion.74 = (f32[256]{0:T(256)S(1)}, f32[256,768]{1,0:T(8,128)S(1)}) fusion(f32[768]{0:T(1024)S(1)} %copy-done.33, bf16[3072,768]{1,0:T(8,128)(2,1)} %all-gather.12.cloned.1.call-done, f32[256,3072]{1,0:T(8,128)} %get-tuple-element.84, f32[256,3072]{1,0:T(8,128)} %get-tuple-element.85, f32[768]{0:T(1024)S(1)} %copy-done.30, f32[768]{0:T(1024)S(1)} %copy-done.29, ...), kind=kOutput, calls=%fused_computation.166 | convolution fusion | flops 1211694848 | bytes 12595200 | tf_op jit(solution)/shard_map/dot_general | solution.py:988
  147.8 1.9 convert_reduce_fusion.1
  149.7 2.7 convert_reduce_fusion
  152.5 1.4 convolution_add_fusion.3
  154.2 1.8 multiply_reduce_fusion
  159.3 1.3 copy.167
  160.6 13.3 %exchange.6 = bf16[8,256,128]{2,1,0:T(8,128)(2,1)S(1)} custom-call(bf16[8,256,128]{2,1,0:T(8,128)(2,1)S(1)} %bitcast.244), custom_call_target="tpu_custom_call" | custom-call | tf_op jit(solution)/shard_map/exchange/pallas_call | solution.py:466
  173.9 11.1 %attend_back.1 = bf16[16,128,384]{2,1,0:T(8,128)(2,1)S(1)} custom-call(s32[16]{0:T(128)S(1)} %copy-done, s32[1]{0:T(128)} %copy.217.len_ref, s32[1]{0:T(128)} %bitcast.2.spot_ref, bf16[16,128,384]{2,1,0:T(8,128)(2,1)S(1)} %get-tuple-element.22.keep_ref, bf16[16,128,128]{2,1,0:T(8,128)(2,1)S(1)} %bitcast.243, f32[8,128,256]{2,1,0:T(8,128)S(1)} %get-tuple-element.23.mix_ref, ...), custom_call_target="tpu_custom_call" | custom-call | tf_op jit(solution)/shard_map/attend_back/pallas_call | solution.py:668
  185.0 32.1 %exchange.7 = bf16[8,256,384]{2,1,0:T(8,128)(2,1)S(1)} custom-call(bf16[8,256,384]{2,1,0:T(8,128)(2,1)S(1)} %bitcast.242), custom_call_target="tpu_custom_call" | custom-call | tf_op jit(solution)/shard_map/exchange/pallas_call | solution.py:466
  217.1 1.3 fusion.71
  218.4 2.2 copy.168
  220.6 1.7 slice_bitcast_fusion.9
  222.3 1.6 fusion.54
  223.9 2.0 copy.170
  226.0 1.7 slice_bitcast_fusion.5
  227.7 1.6 fusion.56
  229.3 2.0 copy.169
  231.4 1.8 slice_bitcast_fusion.7
  233.1 1.6 fusion.55
  234.8 7.5 %fusion.3 = bf16[3072,256]{0,1:T(8,128)(2,1)} fusion(f32[256,3072]{1,0:T(8,128)S(1)} %copy-done.5), kind=kLoop, calls=%fused_computation.7 | loop fusion | flops 51118080 | bytes 4718592 | tf_op jit(solution)/shard_map/convert_element_type | solution.py:985
  243.2 1.9 convert_reduce_fusion.3
  248.6 1.3 stack_reshape.53
  249.9 1.4 stack_reshape.54
  251.3 1.3 stack_reshape.55
  254.6 2.0 copy.177
  256.6 1.8 constant_dynamic-update-slice_fusion.1
  258.3 1.8 constant_dynamic-update-slice_fusion
  264.8 1.9 copy.172
  266.8 1.8 copy.173
  271.2 2.8 pad_maximum_fusion.left_ref
  274.0 132.7 %sum_all.1 = (bf16[12,2,4,48,384]{4,3,2,1,0:T(8,128)(2,1)}, f32[16,256]{1,0:T(8,128)}) custom-call(bf16[7,4,192,256]{3,2,1,0:T(8,128)(2,1)} %pad_maximum_fusion.left_ref, bf16[9,256,768]{2,1,0:T(8,128)(2,1)} %bitcast_dynamic-update-slice_fusion.right_ref, f32[4,16,256]{2,1,0:T(8,128)} %pad.4.small_ref), custom_call_target="tpu_custom_call" | custom-call | tf_op jit(solution)/shard_map/sum_all/pallas_call | solution.py:868
  406.7 2.8 convert_bitcast_fusion
  409.9 2.5 copy-done.1
  419.8 1.8 copy.188
  421.6 1.6 copy.198
  425.2 2.7 pad_maximum_fusion.2
  427.9 1.7 pad_maximum_fusion.1
  430.9 2.0 fusion.26
  (235 shorter events, 46.7 us)
Async XLA Ops:
  7.2 2.9 copy-start.49
  7.2 4.2 copy-start.41
  7.2 4.4 %copy-start.42 = (bf16[192]{0:T(256)(128)(2,1)S(1)}, bf16[192]{0:T(256)(128)(2,1)}, u32[]{:S(2)}) copy-start(bf16[192]{0:T(256)(128)(2,1)} %param.23) | copy-start | bytes 1156
  7.2 4.6 %copy-start.43 = (bf16[192]{0:T(256)(128)(2,1)S(1)}, bf16[192]{0:T(256)(128)(2,1)}, u32[]{:S(2)}) copy-start(bf16[192]{0:T(256)(128)(2,1)} %param.25) | copy-start | bytes 1156
  7.2 4.9 %copy-start.44 = (bf16[192]{0:T(256)(128)(2,1)S(1)}, bf16[192]{0:T(256)(128)(2,1)}, u32[]{:S(2)}) copy-start(bf16[192]{0:T(256)(128)(2,1)} %param.26) | copy-start | bytes 1156
  7.2 5.1 %copy-start.45 = (bf16[192]{0:T(256)(128)(2,1)S(1)}, bf16[192]{0:T(256)(128)(2,1)}, u32[]{:S(2)}) copy-start(bf16[192]{0:T(256)(128)(2,1)} %param.27) | copy-start | bytes 1156
  7.2 5.3 %copy-start.46 = (bf16[192]{0:T(256)(128)(2,1)S(1)}, bf16[192]{0:T(256)(128)(2,1)}, u32[]{:S(2)}) copy-start(bf16[192]{0:T(256)(128)(2,1)} %param.31) | copy-start | bytes 1156
  7.3 5.5 %copy-start.47 = (bf16[192]{0:T(256)(128)(2,1)S(1)}, bf16[192]{0:T(256)(128)(2,1)}, u32[]{:S(2)}) copy-start(bf16[192]{0:T(256)(128)(2,1)} %param.32) | copy-start | bytes 1156
  7.3 5.8 %copy-start.48 = (bf16[192]{0:T(256)(128)(2,1)S(1)}, bf16[192]{0:T(256)(128)(2,1)}, u32[]{:S(2)}) copy-start(bf16[192]{0:T(256)(128)(2,1)} %param.33) | copy-start | bytes 1156
  7.3 21.6 %copy-start.40 = (bf16[768]{0:T(1024)(128)(2,1)S(1)}, bf16[768]{0:T(1024)(128)(2,1)}, u32[]{:S(2)}) copy-start(bf16[768]{0:T(1024)(128)(2,1)} %param.29) | copy-start | bytes 4612
  7.3 29.2 %copy-start.9 = (bf16[1,256,768]{2,1,0:T(8,128)(2,1)S(1)}, bf16[1,256,768]{2,1,0:T(8,128)(2,1)}, u32[]{:S(2)}) copy-start(bf16[1,256,768]{2,1,0:T(8,128)(2,1)} %param.17) | copy-start | bytes 1179652
  7.3 30.1 %copy-start = (s32[16]{0:T(128)S(1)}, s32[16]{0:T(128)}, u32[]{:S(2)}) copy-start(s32[16]{0:T(128)} %pair_ref.3) | copy-start | bytes 196
  7.3 36.0 %all-gather.6.cloned.1.call-start = ((), (), s32[]{:S(2)}) async-start(), calls=%async_computation | async-start | bytes 4423680 | tf_op jit(solution)/shard_map/all_gather | solution.py:929
  8.0 102.6 %all-gather.8.cloned.1.call-start = ((), (), s32[]{:S(2)}) async-start(), calls=%async_computation.1 | async-start | bytes 1474560 | tf_op jit(solution)/shard_map/all_gather | solution.py:932
  8.8 105.1 %all-gather.10.cloned.1.call-start = ((), (), s32[]{:S(2)}) async-start(), calls=%async_computation.2 | async-start | bytes 5898240 | tf_op jit(solution)/shard_map/all_gather | solution.py:936
  9.5 130.9 %all-gather.12.cloned.1.call-start = ((), (), s32[]{:S(2)}) async-start(), calls=%async_computation.3 | async-start | bytes 5898240 | tf_op jit(solution)/shard_map/all_gather | solution.py:938
  108.4 5.5 %copy-start.29 = (f32[768]{0:T(1024)S(1)}, f32[768]{0:T(1024)}, u32[]{:S(2)}) copy-start(f32[768]{0:T(1024)} %convert_element_type.242) | copy-start | bytes 9220
  108.4 5.5 %copy-start.30 = (f32[768]{0:T(1024)S(1)}, f32[768]{0:T(1024)}, u32[]{:S(2)}) copy-start(f32[768]{0:T(1024)} %convert_element_type.243) | copy-start | bytes 9220
  108.4 5.5 %copy-start.37 = (f32[4,1,768]{2,1,0:T(1,128)S(1)}, f32[4,1,768]{2,1,0:T(1,128)}, u32[]{:S(2)}) copy-start(f32[4,1,768]{2,1,0:T(1,128)} %convert_element_type.278) | copy-start | bytes 36868
  110.6 14.7 %copy-start.11 = (bf16[256,4,3,64]{0,3,2,1:T(8,128)(2,1)}, bf16[256,4,3,64]{0,3,2,1:T(8,128)(2,1)S(1)}, u32[]{:S(2)}) copy-start(bf16[256,4,3,64]{0,3,2,1:T(8,128)(2,1)S(1)} %copy.165) | copy-start | bytes 1179652
  113.9 26.5 %copy-start.33 = (f32[768]{0:T(1024)S(1)}, f32[768]{0:T(1024)}, u32[]{:S(2)}) copy-start(f32[768]{0:T(1024)} %convert_element_type.247) | copy-start | bytes 9220
  140.4 9.2 %slice-start.1 = ((s8[4718592]{0:T(1024)(128)(4,1)}), s8[4194304]{0:T(1024)(128)(4,1)S(1)}, s32[]{:S(2)}) async-start(s8[4718592]{0:T(1024)(128)(4,1)} %bitcast.249), calls=%async_computation.5 | async-start | bytes 8388608
  140.4 6.3 %copy-start.18 = (bf16[1,256,768]{2,1,0:T(8,128)(2,1)S(1)}, bf16[1,256,768]{2,1,0:T(8,128)(2,1)}, u32[]{:S(2)}) copy-start(bf16[1,256,768]{2,1,0:T(8,128)(2,1)} %param.18) | copy-start | bytes 1179652
  140.4 6.3 %copy-start.31 = (f32[768]{0:T(1024)S(1)}, f32[768]{0:T(1024)}, u32[]{:S(2)}) copy-start(f32[768]{0:T(1024)} %convert_element_type.248) | copy-start | bytes 9220
  140.4 6.4 %copy-start.39 = (pred[256]{0:T(512)(128)(4,1)S(1)}, pred[256]{0:T(512)(128)(4,1)}, u32[]{:S(2)}) copy-start(pred[256]{0:T(512)(128)(4,1)} %fusion.59) | copy-start | bytes 772
  140.4 7.3 %copy-start.32 = (f32[768]{0:T(1024)S(1)}, f32[768]{0:T(1024)}, u32[]{:S(2)}) copy-start(f32[768]{0:T(1024)} %convert_element_type.249) | copy-start | bytes 9220
  140.4 9.2 %slice-start.2 = ((s8[4718592]{0:T(1024)(128)(4,1)}), s8[524288]{0:T(1024)(128)(4,1)S(1)}, s32[]{:S(2)}) async-start(s8[4718592]{0:T(1024)(128)(4,1)} %bitcast.249), calls=%async_computation.6 | async-start | bytes 1048576
  140.5 9.2 %copy-start.15 = (f32[256,3072]{1,0:T(8,128)S(1)}, f32[256,3072]{1,0:T(8,128)}, u32[]{:S(2)}) copy-start(f32[256,3072]{1,0:T(8,128)} %get-tuple-element.84) | copy-start | bytes 9437188
  146.5 3.2 copy-start.4
  147.8 4.7 %slice-start.3 = ((s8[4718592]{0:T(1024)(128)(4,1)}), s8[4194304]{0:T(1024)(128)(4,1)S(1)}, s32[]{:S(2)}) async-start(s8[4718592]{0:T(1024)(128)(4,1)} %bitcast.307), calls=%async_computation.7 | async-start | bytes 8388608
  154.2 3.6 copy-start.8
  218.4 16.4 %copy-start.5 = (f32[256,3072]{1,0:T(8,128)S(1)}, f32[256,3072]{1,0:T(8,128)}, u32[]{:S(2)}) copy-start(f32[256,3072]{1,0:T(8,128)} %get-tuple-element.85) | copy-start | bytes 9437188
  231.4 10.9 %copy-start.23 = (bf16[4,256,1,64]{1,3,2,0:T(8,128)(2,1)S(1)}, bf16[4,256,1,64]{1,3,2,0:T(8,128)(2,1)}, u32[]{:S(2)}) copy-start(bf16[4,256,1,64]{1,3,2,0:T(8,128)(2,1)} %fusion.54) | copy-start | bytes 393220
  231.4 10.9 %copy-start.25 = (bf16[4,256,1,64]{1,3,2,0:T(8,128)(2,1)S(1)}, bf16[4,256,1,64]{1,3,2,0:T(8,128)(2,1)}, u32[]{:S(2)}) copy-start(bf16[4,256,1,64]{1,3,2,0:T(8,128)(2,1)} %get-tuple-element.66) | copy-start | bytes 393220
  231.4 10.9 %copy-start.26 = (bf16[4,256,1,64]{1,3,2,0:T(8,128)(2,1)S(1)}, bf16[4,256,1,64]{1,3,2,0:T(8,128)(2,1)}, u32[]{:S(2)}) copy-start(bf16[4,256,1,64]{1,3,2,0:T(8,128)(2,1)} %get-tuple-element.67) | copy-start | bytes 393220
  234.8 11.0 %copy-start.36 = (f32[768]{0:T(1024)S(1)}, f32[768]{0:T(1024)}, u32[]{:S(2)}) copy-start(f32[768]{0:T(1024)} %get-tuple-element.45) | copy-start | bytes 9220
  234.8 11.7 %copy-start.35 = (f32[768]{0:T(1024)S(1)}, f32[768]{0:T(1024)}, u32[]{:S(2)}) copy-start(f32[768]{0:T(1024)} %get-tuple-element.27) | copy-start | bytes 9220
  234.8 12.4 %copy-start.34 = (f32[768]{0:T(1024)S(1)}, f32[768]{0:T(1024)}, u32[]{:S(2)}) copy-start(f32[768]{0:T(1024)} %get-tuple-element.32) | copy-start | bytes 9220
  242.3 11.3 %copy-start.24 = (bf16[4,256,1,64]{1,3,2,0:T(8,128)(2,1)S(1)}, bf16[4,256,1,64]{1,3,2,0:T(8,128)(2,1)}, u32[]{:S(2)}) copy-start(bf16[4,256,1,64]{1,3,2,0:T(8,128)(2,1)} %fusion.55) | copy-start | bytes 393220
  242.3 11.3 %copy-start.27 = (bf16[4,256,1,64]{1,3,2,0:T(8,128)(2,1)S(1)}, bf16[4,256,1,64]{1,3,2,0:T(8,128)(2,1)}, u32[]{:S(2)}) copy-start(bf16[4,256,1,64]{1,3,2,0:T(8,128)(2,1)} %get-tuple-element.68) | copy-start | bytes 393220
  242.3 11.3 %copy-start.28 = (bf16[4,256,1,64]{1,3,2,0:T(8,128)(2,1)S(1)}, bf16[4,256,1,64]{1,3,2,0:T(8,128)(2,1)}, u32[]{:S(2)}) copy-start(bf16[4,256,1,64]{1,3,2,0:T(8,128)(2,1)} %get-tuple-element.69) | copy-start | bytes 393220
  243.2 17.0 %copy-start.7 = (f32[256,768]{1,0:T(8,128)S(1)}, f32[256,768]{1,0:T(8,128)}, u32[]{:S(2)}) copy-start(f32[256,768]{1,0:T(8,128)} %copy-done.6) | copy-start | bytes 2359300
  252.8 8.1 %copy-start.17 = (bf16[256,3072]{1,0:T(8,128)(2,1)S(1)}, bf16[256,3072]{1,0:T(8,128)(2,1)}, u32[]{:S(2)}) copy-start(bf16[256,3072]{1,0:T(8,128)(2,1)} %copy-done.16) | copy-start | bytes 4718596
  254.6 9.5 %copy-start.14 = (f32[256,768]{1,0:T(8,128)S(1)}, f32[256,768]{1,0:T(8,128)}, u32[]{:S(2)}) copy-start(f32[256,768]{1,0:T(8,128)} %copy-done.13) | copy-start | bytes 2359300
  266.8 4.5 %copy-start.12 = (bf16[256,4,3,64]{0,3,2,1:T(8,128)(2,1)S(1)}, bf16[256,4,3,64]{0,3,2,1:T(8,128)(2,1)}, u32[]{:S(2)}) copy-start(bf16[256,4,3,64]{0,3,2,1:T(8,128)(2,1)} %copy-done.11) | copy-start | bytes 1179652
  266.8 4.5 %copy-start.22 = (bf16[768,256]{1,0:T(8,128)(2,1)S(1)}, bf16[768,256]{1,0:T(8,128)(2,1)}, u32[]{:S(2)}) copy-start(bf16[768,256]{1,0:T(8,128)(2,1)} %copy.171) | copy-start | bytes 1179652
  416.3 3.5 slice-start
  427.9 3.0 copy-start.21
  (11 other events, 20.8 us)
Sparse Core Ops, SparseCore 0:
  9.7 33.6 all-gather.5
  44.9 17.4 all-gather.7
  64.0 37.4 all-gather.9
  102.9 37.4 all-gather.11

commit v3 on v2

--- a/solution.py
+++ b/solution.py
@@ -430,9 +430,6 @@
     return (output[None], token_grad[None]) + tuple(totals)
 
 
-MESH = pl.DeviceIdType.MESH
-
-
 def exchange_kernel(n, in_ref, out_ref, sent, landed, own):
     me = lax.axis_index("ctx")
     barrier = pltpu.get_barrier_semaphore()
@@ -491,22 +488,6 @@
 
 def send_blocks(queries, keys, values):
     return jnp.concatenate([split_heads(queries), split_heads(keys), split_heads(values)], axis=2)
-
-
-def join_heads(blocks):
-    rows = blocks.shape[1]
-    pairs = blocks.reshape(HEADS // 3, 2, rows, 2, HEAD_DIM)
-    shared = pairs[:, 0, :, 1].astype(jnp.float32) + pairs[:, 1, :, 1].astype(jnp.float32)
-    trio = jnp.stack([pairs[:, 0, :, 0], pairs[:, 1, :, 0], shared.astype(blocks.dtype)], axis=2)
-    return jnp.transpose(trio, (1, 0, 2, 3)).reshape(rows, HEADS * HEAD_DIM)
-
-
-def join_parts(blocks):
-    parts = jnp.split(blocks, 3, axis=2)
-    return jnp.concatenate([join_heads(part) for part in parts], axis=1)
-
-
-BLK = 128
 
 
 def low_lanes(shape):
@@ -681,6 +662,205 @@
     )(pairing, lengths, spot, keep, grad, mix, lse)
 
 
+MESH = pl.DeviceIdType.MESH
+
+
+def remote(src, dst, sems, at, peer):
+    return pltpu.make_async_remote_copy(
+        src_ref=src, dst_ref=dst, send_sem=sems.at[(0,) + at], recv_sem=sems.at[(1,) + at],
+        device_id=peer, device_id_type=MESH,
+    )
+
+
+def greet(peers):
+    barrier = pltpu.get_barrier_semaphore()
+    for peer in peers:
+        pl.semaphore_signal(barrier, inc=1, device_id=peer, device_id_type=MESH)
+    pl.semaphore_wait(barrier, len(peers))
+
+
+def ring_peers(n):
+    me = lax.axis_index("ctx")
+    return [{"ctx": lax.rem(me + k, n)} for k in range(1, n)]
+
+
+def exchange_copies(n, in_ref, out_ref, sems):
+    me = lax.axis_index("ctx")
+    return [
+        remote(in_ref.at[lax.rem(me + k, n)], out_ref.at[me], sems, (k,), {"ctx": lax.rem(me + k, n)})
+        for k in range(1, n)
+    ]
+
+
+def join_pairs(pairs):
+    pieces = []
+    for group in range(HEADS // 3):
+        first, second = pairs(2 * group), pairs(2 * group + 1)
+        shared = first[:, HEAD_DIM:].astype(jnp.float32) + second[:, HEAD_DIM:].astype(jnp.float32)
+        pieces += [first[:, :HEAD_DIM], second[:, :HEAD_DIM], shared.astype(jnp.bfloat16)]
+    return jnp.concatenate(pieces, axis=1)
+
+
+def pair_of(value, peer):
+    own = 3 * (peer // 2) + peer % 2
+    shared = 3 * (peer // 2) + 2
+    cut = lambda head: value[:, head * HEAD_DIM : (head + 1) * HEAD_DIM]
+    return jnp.concatenate([cut(own), cut(shared)], axis=1)
+
+
+def dot_nn(a, b):
+    return jnp.dot(a, b, preferred_element_type=jnp.float32)
+
+
+def dot_nt(a, b):
+    return lax.dot_general(a, b, (((1,), (1,)), ((), ())), preferred_element_type=jnp.float32)
+
+
+def column_sum(value):
+    return jnp.sum(value, axis=0, keepdims=True)
+
+
+def unit_of(value):
+    mean = jnp.mean(value, axis=-1, keepdims=True)
+    centred = value - mean
+    scale = lax.rsqrt(jnp.mean(centred * centred, axis=-1, keepdims=True) + eps)
+    return centred * scale, scale
+
+
+def unit_back(unit, scale, scaled):
+    return scale * (
+        scaled
+        - jnp.mean(scaled, axis=-1, keepdims=True)
+        - unit * jnp.mean(scaled * unit, axis=-1, keepdims=True)
+    )
+
+
+(ROW_BQ, ROW_BV, ROW_BO, ROW_G1, ROW_S1, ROW_BB, ROW_G2, ROW_S2, ROW_BI) = range(9)
+
+
+def layer_kernel(
+    n, pair_ref, len_ref, mixed_ref, tokens_ref, cot_ref, w_out_ref, w_in_ref, w_back_ref, rows_ref,
+    output_ref, grad_in_ref, left_ref, right_ref, resid_ref, sums_ref,
+    mixed_in, grad_out, active, slope, in_sem, out_sem, own_sem,
+):
+    low, wide = jnp.bfloat16, jnp.float32
+    ctx = lax.axis_index("ctx")
+    sums_ref[...] = jnp.zeros_like(sums_ref)
+    greet(ring_peers(n))
+    copies = exchange_copies(n, mixed_ref, mixed_in, in_sem)
+    for cp in copies:
+        cp.start()
+    own = pltpu.make_async_copy(mixed_ref.at[ctx], mixed_in.at[ctx], own_sem.at[0])
+    own.start()
+    row = lambda i: rows_ref[i : i + 1, :]
+    tokens = tokens_ref[...]
+    left_ref[0] = jnp.transpose(tokens).reshape(4, -1, 2 * BLK)
+    spots = lax.broadcasted_iota(jnp.int32, (2 * BLK, 1), 0)
+    place = jnp.where(
+        spots < BLK,
+        pair_ref[2 * ctx] * BLK + spots,
+        pair_ref[2 * ctx + 1] * BLK + spots - BLK,
+    )
+    valid = place < len_ref[0]
+    own.wait()
+    for cp in copies:
+        cp.wait_recv()
+
+    attended = join_pairs(lambda peer: mixed_in[peer])
+    resid_one = tokens.astype(wide) + dot_nn(attended, w_out_ref[...]) + row(ROW_BO)
+    unit_one, scale_one = unit_of(resid_one)
+    hidden = unit_one * row(ROW_G1) + row(ROW_S1)
+    hidden_low = hidden.astype(low)
+    width = tokens.shape[1]
+    count = w_in_ref.shape[1] // width
+    resid_two = hidden + row(ROW_BB)
+    for t in range(count):
+        cols = slice(t * width, (t + 1) * width)
+        upper = dot_nn(hidden_low, w_in_ref[:, cols]) + row(ROW_BI + t)
+        share = 0.5 * (1.0 + lax.erf(upper * (0.5**0.5)))
+        slope[:, cols] = share + upper * (jnp.exp(-0.5 * upper * upper) * (2 * math.pi) ** -0.5)
+        some = (upper * share).astype(low)
+        active[:, cols] = some
+        resid_two = resid_two + dot_nn(some, w_back_ref[cols, :])
+    unit_two, scale_two = unit_of(resid_two)
+    output_ref[...] = jnp.where(valid, unit_two * row(ROW_G2) + row(ROW_S2), 0.0)
+    grad_y = jnp.where(valid, cot_ref[...].astype(wide), 0.0)
+    sums_ref[ROW_G2 : ROW_G2 + 1, :] = column_sum(grad_y * unit_two)
+    sums_ref[ROW_S2 : ROW_S2 + 1, :] = column_sum(grad_y)
+    grad_resid_two = unit_back(unit_two, scale_two, grad_y * row(ROW_G2))
+    grad_mixed = grad_resid_two.astype(low)
+    right_ref[5] = grad_mixed
+    sums_ref[ROW_BB : ROW_BB + 1, :] = column_sum(grad_mixed.astype(wide))
+    grad_hidden = grad_resid_two
+    for t in range(count):
+        cols = slice(t * width, (t + 1) * width)
+        grad_upper = (dot_nt(grad_mixed, w_back_ref[cols, :]) * slope[:, cols]).astype(low)
+        right_ref[1 + t] = grad_upper
+        sums_ref[ROW_BI + t : ROW_BI + t + 1, :] = column_sum(grad_upper.astype(wide))
+        grad_hidden = grad_hidden + dot_nt(grad_upper, w_in_ref[:, cols])
+    sums_ref[ROW_G1 : ROW_G1 + 1, :] = column_sum(grad_hidden * unit_one)
+    sums_ref[ROW_S1 : ROW_S1 + 1, :] = column_sum(grad_hidden)
+    grad_resid_one = unit_back(unit_one, scale_one, grad_hidden * row(ROW_G1))
+    resid_ref[...] = grad_resid_one
+    grad_branch = grad_resid_one.astype(low)
+    right_ref[0] = grad_branch
+    sums_ref[ROW_BO : ROW_BO + 1, :] = column_sum(grad_branch.astype(wide))
+    grad_attended = dot_nt(grad_branch, w_out_ref[...]).astype(low)
+    for peer in range(n):
+        grad_out[peer] = pair_of(grad_attended, peer)
+    backs = exchange_copies(n, grad_out, grad_in_ref, out_sem)
+    for cp in backs:
+        cp.start()
+    back = pltpu.make_async_copy(grad_out.at[ctx], grad_in_ref.at[ctx], own_sem.at[1])
+    back.start()
+    left_ref[1] = jnp.transpose(attended).reshape(4, -1, 2 * BLK)
+    left_ref[2] = jnp.transpose(hidden_low).reshape(4, -1, 2 * BLK)
+    for f in range(4):
+        turned = jnp.transpose(active[:, f * width : (f + 1) * width])
+        for r in range(4):
+            left_ref[3 + r, f] = turned[r * width // 4 : (r + 1) * width // 4]
+    back.wait()
+    for cp in copies:
+        cp.wait_send()
+    for cp in backs:
+        cp.wait()
+
+
+def layer(pairing, lengths, mixed, tokens, cotangent, w_out, w_in, w_back, rows, name):
+    n = mixed.shape[0]
+    count, width = tokens.shape
+    inner = w_in.shape[1]
+    low, wide = jnp.bfloat16, jnp.float32
+    dma = pltpu.SemaphoreType.DMA
+    shape = jax.ShapeDtypeStruct
+    return pl.pallas_call(
+        functools.partial(layer_kernel, n),
+        out_shape=(
+            shape((count, width), wide),
+            shape(mixed.shape, low),
+            shape((7, 4, width // 4, count), low),
+            shape((6, count, width), low),
+            shape((count, width), wide),
+            shape((16, width), wide),
+        ),
+        in_specs=[smem(), smem()] + [vmem()] * 7,
+        out_specs=(vmem(),) * 6,
+        scratch_shapes=[
+            pltpu.VMEM(mixed.shape, low),
+            pltpu.VMEM(mixed.shape, low),
+            pltpu.VMEM((count, inner), low),
+            pltpu.VMEM((count, inner), wide),
+            dma((2, n)),
+            dma((2, n)),
+            dma((2,)),
+        ],
+        compiler_params=pltpu.CompilerParams(
+            collective_id=name, has_side_effects=True, vmem_limit_bytes=56 << 20
+        ),
+        name="layer",
+    )(pairing, lengths, mixed, tokens, cotangent, w_out, w_in, w_back, rows)
+
+
 PARTS = 12
 
 
@@ -693,11 +873,13 @@
 
 
 def sum_kernel(
-    left_ref, right_ref, small_ref, out_ref, small_out,
-    pair_out, pair_in, x_out, x_in, first_sum, y_out, y_in, half_sum, z_out, z_in,
-    s_pair, s_x_out, s_x, s_y_out, s_y, s_z_out, s_z,
-    pair_sem, x_sem, y_sem, z_sem, spread_sem, last_sem, s_sem,
+    n, left_ref, right_ref, sums_ref, blocks_ref, w_qkv_ref, resid_ref,
+    token_ref, qkv_out, out_out, in_out, back_out, small_out,
+    blocks_in, right_all, total_ref, pair_out, pair_in, x_out, x_in, first_sum, y_out, y_in, half_sum,
+    z_out, z_in, s_pair, s_x_out, s_x, s_y_out, s_y, s_z_out, s_z,
+    block_sem, own_sem, pair_sem, x_sem, y_sem, z_sem, spread_sem, last_sem, s_sem,
 ):
+    low, wide = jnp.bfloat16, jnp.float32
     ctx = lax.axis_index("ctx")
     fsdp = lax.axis_index("fsdp")
     z, y = ctx // 2, lax.rem(ctx, 2)
@@ -706,47 +888,46 @@
     across = {"fsdp": 2 * (1 - x) + core}
     beside = {"ctx": 2 * z + 1 - y}
     along = [{"ctx": 2 * lax.rem(z + k, 4) + y} for k in (1, 2, 3)]
-    barrier = pltpu.get_barrier_semaphore()
-    for peer in [sibling, across, beside] + along:
-        pl.semaphore_signal(barrier, inc=1, device_id=peer, device_id_type=MESH)
-    pl.semaphore_wait(barrier, 6)
-
-    def copy(src, dst, sems, at, peer):
-        return pltpu.make_async_remote_copy(
-            src_ref=src, dst_ref=dst, send_sem=sems.at[(0,) + at], recv_sem=sems.at[(1,) + at],
-            device_id=peer, device_id_type=MESH,
-        )
+    greet(ring_peers(n) + [sibling, across])
+    blocks = exchange_copies(n, blocks_ref, blocks_in, block_sem)
+    for cp in blocks:
+        cp.start()
+    own = pltpu.make_async_copy(blocks_ref.at[ctx], blocks_in.at[ctx], own_sem)
+    own.start()
+    right_all[3:] = right_ref[...]
 
     def pair_copy(c):
-        return copy(pair_out.at[c], pair_in.at[c], pair_sem, (c,), sibling)
+        return remote(pair_out.at[lax.rem(c, 2)], pair_in.at[c], pair_sem, (c,), sibling)
 
     def x_copy(c):
-        return copy(x_out.at[c], x_in.at[c], x_sem, (c,), across)
+        return remote(x_out.at[c], x_in.at[c], x_sem, (c,), across)
 
     def y_copy(c):
-        return copy(y_out.at[c], y_in.at[c], y_sem, (c,), beside)
+        return remote(y_out.at[c], y_in.at[c], y_sem, (c,), beside)
 
     def z_copy(c, k):
-        return copy(
+        return remote(
             z_out.at[c, lax.rem(z + k, 4)], z_in.at[c, k - 1], z_sem, (c, k - 1), along[k - 1]
         )
 
     def spread_copy(c, k):
-        piece = out_ref.at[c, y, z]
-        return copy(piece, piece, spread_sem, (c, k - 1), along[k - 1])
+        piece = total_ref.at[c, y, z]
+        return remote(piece, piece, spread_sem, (c, k - 1), along[k - 1])
 
     def last_copy(c):
-        return copy(out_ref.at[c, y], out_ref.at[c, y], last_sem, (c,), beside)
+        return remote(total_ref.at[c, y], total_ref.at[c, y], last_sem, (c,), beside)
 
     def partial(c, shard):
         left, right = sum_sources(c)
-        return jnp.dot(left_ref[left, shard], right_ref[right], preferred_element_type=jnp.float32)
-
-    low = jnp.bfloat16
+        return jnp.dot(left_ref[left, shard], right_all[right], preferred_element_type=jnp.float32)
 
     def stage_pair(c):
+        @pl.when(c >= 2)
+        def _():
+            pair_copy(c - 2).wait_send()
+
         for side in range(2):
-            pair_out[c, side] = partial(c, 2 * side + 1 - core).astype(low)
+            pair_out[lax.rem(c, 2), side] = partial(c, 2 * side + 1 - core).astype(low)
         pair_copy(c).start()
 
     def stage_x(c):
@@ -778,7 +959,7 @@
         for k in (1, 2, 3):
             z_copy(c, k).wait_recv()
             total = total + z_in[c, k - 1].astype(jnp.float32)
-        out_ref[c, y, z] = total.astype(low)
+        total_ref[c, y, z] = total.astype(low)
         for k in (1, 2, 3):
             spread_copy(c, k).start()
 
@@ -791,30 +972,40 @@
     order = [0, 1, 4, 2, 3, 5]
 
     def small_step(t):
-        def s_copy(src, dst, k, peer):
-            return copy(src, dst, s_sem, (k,), peer)
-
-        send_pair = s_copy(s_pair.at[0], s_pair.at[1], 0, sibling)
-        send_x = s_copy(s_x_out, s_x, 1, across)
-        send_y = s_copy(s_y_out, s_y, 2, beside)
-        send_z = [s_copy(s_z_out, s_z.at[k], 3 + k, along[k]) for k in range(3)]
+        send_pair = remote(s_pair.at[0], s_pair.at[1], s_sem, (0,), sibling)
+        send_x = remote(s_x_out, s_x, s_sem, (1,), across)
+        send_y = remote(s_y_out, s_y, s_sem, (2,), beside)
+        send_z = [remote(s_z_out, s_z.at[k], s_sem, (3 + k,), along[k]) for k in range(3)]
 
         @pl.when(t == 0)
         def _():
-            for side in range(2):
-                s_pair[0, side] = small_ref[2 * side + 1 - core]
+            own.wait()
+            for cp in blocks:
+                cp.wait_recv()
+            for part in range(3):
+                right_all[part] = join_pairs(
+                    lambda peer: blocks_in[peer, :, part * 2 * HEAD_DIM : (part + 1) * 2 * HEAD_DIM]
+                )
+            s_pair[0] = sums_ref[...]
+            s_pair[0, ROW_BQ : ROW_BQ + 1] = column_sum(right_all[0].astype(wide))
+            s_pair[0, ROW_BV : ROW_BV + 1] = column_sum(right_all[2].astype(wide))
             send_pair.start()
 
         @pl.when(t == 1)
         def _():
             send_pair.wait()
-            s_x_out[...] = small_ref[2 * (1 - x) + core] + s_pair[1, 1 - x]
+            s_x_out[...] = s_pair[0] + s_pair[1]
             send_x.start()
+            width = resid_ref.shape[1]
+            token_ref[...] = resid_ref[...] + sum(
+                dot_nt(right_all[part], w_qkv_ref[:, part * width : (part + 1) * width])
+                for part in range(3)
+            )
 
         @pl.when(t == 2)
         def _():
             send_x.wait()
-            s_y_out[...] = small_ref[2 * x + core] + s_pair[1, x] + s_x[...]
+            s_y_out[...] = s_x_out[...] + s_x[...]
             send_y.start()
 
         @pl.when(t == 3)
@@ -828,16 +1019,23 @@
         def _():
             for cp in send_z:
                 cp.wait()
-            total = jnp.zeros_like(s_z_out)
-            for place in range(4):
-                k = lax.rem(place - z + 4, 4)
-                behind = 4 - k
-                other = s_z[jnp.where(k == 0, 0, behind - 1)]
+            total = jnp.zeros(s_z_out.shape, wide)
+            for spot in range(4):
+                k = lax.rem(spot - z + 4, 4)
+                other = s_z[jnp.where(k == 0, 0, 3 - k)]
                 total = total + jnp.where(k == 0, s_z_out[...], other)
-            small_out[...] = total
+            quarter = total.shape[1] // 4
+            cuts = [slice(f * quarter, (f + 1) * quarter) for f in range(4)]
+            pick = lambda choices: sum(
+                jnp.where(fsdp == f, choice, 0.0) for f, choice in enumerate(choices)
+            )
+            small_out[:8] = pick([total[:8, cut] for cut in cuts])
+            line = pick([total[ROW_BI + f : ROW_BI + f + 1] for f in range(4)])
+            for j, cut in enumerate(cuts):
+                small_out[8 + j : 9 + j] = line[:, cut]
 
     def slot(t, carry):
-        small_step(t)
+        small_step(t - 9)
         for index in order:
             c = t - index
 
@@ -850,7 +1048,6 @@
     lax.fori_loop(0, PARTS + 5, slot, 0)
 
     def drain(c, carry):
-        pair_copy(c).wait_send()
         x_copy(c).wait_send()
         y_copy(c).wait_send()
         for k in (1, 2, 3):
@@ -860,21 +1057,50 @@
         return carry
 
     lax.fori_loop(0, PARTS, drain, 0)
-
-
-def sum_all(left, right, small, name):
+    for c in (PARTS - 2, PARTS - 1):
+        pair_copy(c).wait_send()
+    for cp in blocks:
+        cp.wait_send()
+
+    def panel(c, target, rows_at, cols_at):
+        for half in range(2):
+            for spot in range(4):
+                target[
+                    rows_at + 48 * spot : rows_at + 48 * spot + 48,
+                    cols_at + 384 * half : cols_at + 384 * half + 384,
+                ] = total_ref[c, half, spot]
+
+    for k in range(4):
+        panel(k, back_out, 192 * k, 0)
+        panel(4 + k, in_out, 0, 768 * k)
+    panel(8, out_out, 0, 0)
+    for k in range(3):
+        panel(9 + k, qkv_out, 0, 768 * k)
+
+
+def sum_all(left, right, sums, blocks, w_qkv, resid, name):
+    n = blocks.shape[0]
     low, wide = jnp.bfloat16, jnp.float32
     dma = pltpu.SemaphoreType.DMA
+    shape = jax.ShapeDtypeStruct
+    small = pltpu.VMEM(sums.shape, wide)
     return pl.pallas_call(
-        sum_kernel,
+        functools.partial(sum_kernel, n),
         out_shape=(
-            jax.ShapeDtypeStruct((PARTS, 2, 4, 48, 384), low),
-            jax.ShapeDtypeStruct(small.shape[1:], wide),
+            shape(resid.shape, wide),
+            shape((192, 2304), low),
+            shape((192, 768), low),
+            shape((192, 3072), low),
+            shape((768, 768), low),
+            shape((16, 192), wide),
         ),
-        in_specs=[vmem(), vmem(), vmem()],
-        out_specs=(vmem(), vmem()),
+        in_specs=[vmem()] * 6,
+        out_specs=(vmem(),) * 6,
         scratch_shapes=[
-            pltpu.VMEM((PARTS, 2, 192, 768), low),
+            pltpu.VMEM(blocks.shape, low),
+            pltpu.VMEM((9,) + right.shape[1:], low),
+            pltpu.VMEM((PARTS, 2, 4, 48, 384), low),
+            pltpu.VMEM((2, 2, 192, 768), low),
             pltpu.VMEM((PARTS, 2, 192, 768), low),
             pltpu.VMEM((PARTS, 192, 768), low),
             pltpu.VMEM((PARTS, 192, 768), low),
@@ -884,13 +1110,11 @@
             pltpu.VMEM((2, 192, 384), wide),
             pltpu.VMEM((PARTS, 4, 48, 384), low),
             pltpu.VMEM((PARTS, 3, 48, 384), low),
-            pltpu.VMEM((2, 2) + small.shape[1:], wide),
-            pltpu.VMEM(small.shape[1:], wide),
-            pltpu.VMEM(small.shape[1:], wide),
-            pltpu.VMEM(small.shape[1:], wide),
-            pltpu.VMEM(small.shape[1:], wide),
-            pltpu.VMEM(small.shape[1:], wide),
-            pltpu.VMEM((3,) + small.shape[1:], wide),
+            pltpu.VMEM((2,) + sums.shape, wide),
+            small, small, small, small, small,
+            pltpu.VMEM((3,) + sums.shape, wide),
+            dma((2, n)),
+            dma,
             dma((2, PARTS)),
             dma((2, PARTS)),
             dma((2, PARTS)),
@@ -900,10 +1124,10 @@
             dma((2, 6)),
         ],
         compiler_params=pltpu.CompilerParams(
-            collective_id=name, has_side_effects=True, vmem_limit_bytes=58 << 20
+            collective_id=name, has_side_effects=True, vmem_limit_bytes=60 << 20
         ),
         name="sum_all",
-    )(left, right, small)
+    )(left, right, sums, blocks, w_qkv, resid)
 
 
 def on_device_spread(
@@ -970,108 +1194,38 @@
     sent = send_blocks(queries, keys, values)
     packed = exchange(sent, 0).reshape(-1, half, 6 * HEAD_DIM)
     mixed_out, keep, mix, lse = attend(pairing, lengths, spot, packed)
-    attended_low = join_heads(exchange(mixed_out.reshape(-1, rows, 2 * HEAD_DIM), 1))
-    resid_one = (
-        inputs.astype(jnp.float32)
-        + jnp.dot(attended_low, out_all, preferred_element_type=jnp.float32)
-        + out_bias.astype(jnp.float32)
-    )
-    hidden = layer_norm(resid_one, gain_one.astype(jnp.float32), shift_one.astype(jnp.float32))
-    hidden_low = hidden.astype(jnp.bfloat16)
-    upper = jnp.dot(hidden_low, in_all, preferred_element_type=jnp.float32) + in_bias.astype(
-        jnp.float32
-    )
-    active, gelu_back = jax.vjp(lambda value: jax.nn.gelu(value, approximate=False), upper)
-    active_low = active.astype(jnp.bfloat16)
-    resid_two = (
-        hidden
-        + jnp.dot(active_low, back_all, preferred_element_type=jnp.float32)
-        + back_bias.astype(jnp.float32)
-    )
-    normed = layer_norm(resid_two, gain_two.astype(jnp.float32), shift_two.astype(jnp.float32))
-    output = jnp.where(valid[:, None], normed, 0.0)
-    qkv_back, out_back, gain_one_back, in_back, back_back, gain_two_back = (
-        qkv_all,
-        out_all,
-        gain_one,
-        in_all,
-        back_all,
-        gain_two,
-    )
-    grad_y = jnp.where(valid[:, None], cotangent[0].astype(jnp.float32), 0.0)
-    grad_resid_two, gain_two_grad, shift_two_grad = norm_back(
-        resid_two, gain_two_back.astype(jnp.float32), grad_y
-    )
-    grad_mixed = grad_resid_two.astype(jnp.bfloat16)
-    back_bias_grad = jnp.sum(grad_mixed.astype(jnp.float32), axis=0)
-    grad_active = jnp.einsum("td,fd->tf", grad_mixed, back_back, preferred_element_type=jnp.float32)
-    (grad_upper,) = gelu_back(grad_active)
-    grad_upper_low = grad_upper.astype(jnp.bfloat16)
-    in_bias_grad = jnp.sum(grad_upper_low.astype(jnp.float32), axis=0)
-    grad_hidden = grad_resid_two + jnp.einsum(
-        "tf,df->td", grad_upper_low, in_back, preferred_element_type=jnp.float32
-    )
-    grad_resid_one, gain_one_grad, shift_one_grad = norm_back(
-        resid_one, gain_one_back.astype(jnp.float32), grad_hidden
-    )
-    grad_branch = grad_resid_one.astype(jnp.bfloat16)
-    out_bias_grad = jnp.sum(grad_branch.astype(jnp.float32), axis=0)
-    grad_attended = jnp.einsum(
-        "td,cd->tc", grad_branch, out_back, preferred_element_type=jnp.float32
-    ).astype(jnp.bfloat16)
-    grad_in = exchange(split_heads(grad_attended), 2).reshape(-1, half, 2 * HEAD_DIM)
-    grad_blocks = attend_back(pairing, lengths, spot, keep, grad_in, mix, lse)
-    grad_proj = join_parts(exchange(grad_blocks.reshape(-1, rows, 6 * HEAD_DIM), 3))
-    query_bias_grad = jnp.sum(grad_proj[:, :width].astype(jnp.float32), axis=0)
-    value_bias_grad = jnp.sum(grad_proj[:, 2 * width :].astype(jnp.float32), axis=0)
-    token_grad = grad_resid_one + jnp.einsum(
-        "tf,df->td", grad_proj, qkv_back, preferred_element_type=jnp.float32
-    )
-    def wide(value):
-        return jnp.transpose(value).reshape(4, -1, rows)
-
-    tall = jnp.transpose(active_low).reshape(4, 4, width // 4, rows)
-    left = jnp.concatenate(
-        [
-            jnp.stack([wide(inputs), wide(attended_low), wide(hidden_low)]),
-            jnp.transpose(tall, (1, 0, 2, 3)),
-        ]
-    )
-    right = jnp.stack(
-        jnp.split(grad_proj, 3, axis=1)
-        + [grad_branch]
-        + jnp.split(grad_upper_low, 4, axis=1)
-        + [grad_mixed]
-    )
     vectors = [
-        query_bias_grad, value_bias_grad, out_bias_grad, gain_one_grad, shift_one_grad,
-        back_bias_grad, gain_two_grad, shift_two_grad,
+        query_bias, value_bias, out_bias, gain_one, shift_one, back_bias, gain_two, shift_two
     ]
-    small = jnp.concatenate(
-        [jnp.stack([v.reshape(4, -1) for v in vectors], axis=1), in_bias_grad.reshape(4, 4, -1)],
-        axis=1,
-    )
-    small = jnp.pad(small, ((0, 0), (0, 4), (0, 64)))
-    sums, small_sum = sum_all(left, right, small, 4)
-    panels = jnp.transpose(sums, (0, 2, 3, 1, 4)).reshape(PARTS, width // 4, width)
-    panels = panels.astype(jnp.float32)
-    lines = [small_sum[i, : width // 4] for i in range(8)]
+    vectors = jnp.concatenate([jnp.stack(vectors), in_bias.reshape(-1, width)]).astype(jnp.float32)
+    vectors = jnp.pad(vectors, ((0, 16 - vectors.shape[0]), (0, 0)))
+    output, grad_in, left, right, resid, sums = layer(
+        pairing, lengths, mixed_out.reshape(-1, rows, 2 * HEAD_DIM), inputs, cotangent[0],
+        out_all, in_all, back_all, vectors, 1,
+    )
+    grad_blocks = attend_back(
+        pairing, lengths, spot, keep, grad_in.reshape(-1, half, 2 * HEAD_DIM), mix, lse
+    )
+    token_grad, qkv_sum, out_sum, in_sum, back_sum, small = sum_all(
+        left, right, sums, grad_blocks.reshape(-1, rows, 6 * HEAD_DIM), qkv_all, resid, 2
+    )
+    wide = lambda value: value.astype(jnp.float32)
     return (
         output[None],
         token_grad[None],
-        jnp.concatenate([panels[9], panels[10], panels[11]], axis=1),
-        lines[0],
-        lines[1],
-        panels[8],
-        lines[2],
-        lines[3],
-        lines[4],
-        jnp.concatenate([panels[4], panels[5], panels[6], panels[7]], axis=1),
-        small_sum[8:12, : width // 4].reshape(-1),
-        panels[:4].reshape(-1, width),
-        lines[5],
-        lines[6],
-        lines[7],
+        wide(qkv_sum),
+        small[ROW_BQ],
+        small[ROW_BV],
+        wide(out_sum),
+        small[ROW_BO],
+        small[ROW_G1],
+        small[ROW_S1],
+        wide(in_sum),
+        small[ROW_BI : ROW_BI + 4].reshape(-1),
+        wide(back_sum),
+        small[ROW_BB],
+        small[ROW_G2],
+        small[ROW_S2],
     )
 
 

time: 446 us -> 366 us (0.82); the launches traced: 440 us -> 365 us
  local copies, waits for them, and re-layouts: 65.3 us -> 11.9 us
  waiting for transfers between devices: 23 us -> 66.2 us
  other arithmetic: 39.5 us -> 8.63 us
  matrix products: 29.3 us -> 3.1 us
  Pallas kernels: 248 us -> 241 us
    pallas_call x4 -> x1, Pallas kernels: 96.8 us -> 30.1 us  [exchange(): pl.pallas_call(functools.partial(exchange_kernel, n), out_shape=jax.Shape...]
    pallas_call x1 -> x2, Pallas kernels: 133 us -> 193 us  [the longest x1 153 us: sum_all(): pl.pallas_call(functools.partial(sum_kernel, n), out_shape=(shape(resid.s...]
    dot_general x7 -> x0, matrix products: 26.2 us -> none  [the longest x1 11.4 us: on_device_spread(): jnp.dot(hidden_low, in_all, preferred_element_type=jnp.float32)]
    all_gather x1, waiting for transfers between devices: 15 us -> 38.9 us  [on_device_spread(): lax.all_gather(w_back, 'fsdp', axis=0, tiled=True)]
    another operation x15 -> x8, local copies, waits for them, and re-layouts: 16.6 us -> 0.04 us  [on_device_spread(): jnp.stack(vectors)]
    all_gather x1, waiting for transfers between devices: 0.02 us -> 14.6 us  [on_device_spread(): lax.all_gather(w_in, 'fsdp', axis=0, tiled=True)]
    unnamed x142 -> x61, local copies, waits for them, and re-layouts: 21.8 us -> 7.25 us
    convert_element_type x13 -> x4, other arithmetic: 20.5 us -> 7.54 us  [on_device_spread(): wide = lambda value: value.astype(jnp.float32)]
  transfers between devices with their start and end apart: 4 -> 4, of which waited for: 2 -> 3; matrix products, arithmetic and copies ran while one was open for 7% -> 2% of each run, Pallas kernels for 13% -> 10%
where the time goes in v3:
time: 366 us; the launch traced here: 365 us
  Pallas kernels  241 us (66%)
  waiting for transfers between devices  66.2 us (18%)
  blocking collectives  18.6 us (5%)
  between operations  15.5 us (4%)
  local copies, waits for them, and re-layouts  11.9 us (3%)
  other arithmetic  8.63 us (2%)
    pallas_call x1, Pallas kernels, sum_all(): pl.pallas_call(functools.partial(sum_kernel, n), out_shape=(shape(resid.s...  153 us
    pallas_call x1, Pallas kernels, layer(): pl.pallas_call(functools.partial(layer_kernel, n), out_shape=(shape((coun...  39.6 us
    all_gather x1, waiting for transfers between devices, on_device_spread(): lax.all_gather(w_back, 'fsdp', axis=0, tiled=True)  38.9 us
    pallas_call x1, Pallas kernels, exchange(): pl.pallas_call(functools.partial(exchange_kernel, n), out_shape=jax.Shape...  30.1 us
    all_gather x1, waiting for transfers between devices, on_device_spread(): lax.all_gather(w_in, 'fsdp', axis=0, tiled=True)  14.6 us
    unnamed x1, blocking collectives  13.2 us
    pallas_call x1, Pallas kernels, attend_back(): pl.pallas_call(functools.partial(attend_back_kernel, chunks), out_shape=j...  11.1 us
    all_gather x1, waiting for transfers between devices, on_device_spread(): lax.all_gather(w_qkv, 'fsdp', axis=0, tiled=True)  10 us
  transfers between devices with their start and end apart: 4, of which 3 were waited for; matrix products, arithmetic and copies ran while one was open for 2% of the time, Pallas kernels for 10%

profile of v3, /device:TPU:0, one launch (start us, length us, event | category | flops | bytes accessed | tf_op | source)
XLA Modules:
  0.0 365.2 jit_solution(13760660526429666350)
XLA Ops:
  7.3 0.7 all-gather.6.cloned.1.call-update
  8.0 0.0 all-gather.8.cloned.1.call-start
  8.1 0.7 all-gather.8.cloned.1.call-update
  8.8 0.7 all-gather.10.cloned.1.call-update
  9.5 0.0 all-gather.12.cloned.1.call-start
  9.6 0.5 all-gather.12.cloned.1.call-update
  10.1 0.6 dynamic-slice
  11.4 0.2 dynamic-update-slice.6
  11.6 0.2 dynamic-update-slice.5
  11.8 0.2 dynamic-update-slice.4
  12.1 0.2 dynamic-update-slice.3
  12.3 0.2 dynamic-update-slice.2
  12.6 0.2 dynamic-update-slice
  12.8 0.2 dynamic-update-slice.1
  13.0 0.2 dynamic-update-slice.7
  13.3 13.2 %all-reduce.9 = (bf16[768]{0:T(1024)(128)(2,1)S(1)}, bf16[768]{0:T(1024)(128)(2,1)S(1)}, bf16[768]{0:T(1024)(128)(2,1)S(1)}, bf16[768]{0:T(1024)(128)(2,1)S(1)},...) all-reduce(bf16[768]{0:T(1024)(128)(2,1)S(1)} %dynamic-update-slice, ...), channel_id=1, replica_groups=mesh['ctx'=8,'fsdp'=4] {'fsdp'}, use_global_device_ids=true, to_apply=%add.2 | all-reduce | flops 6144 | bytes 24576
  27.2 5.4 %all-gather = bf16[4,1,768]{2,1,0:T(2,128)(2,1)S(1)} all-gather(bf16[1,1,768]{2,1,0:T(2,128)(2,1)S(1)} %reshape.108), channel_id=1, replica_groups=mesh['ctx'=8,'fsdp'=4] {'fsdp'}, dimensions={0}, use_global_device_ids=true | all-gather | bytes 7680 | tf_op jit(solution)/shard_map/all_gather | solution.py:1161
  32.6 0.1 concatenate.19
  32.7 0.6 pad_convert_fusion.rows_ref
  33.3 10.0 %all-gather.6.cloned.1.call-done.w_qkv_ref = bf16[768,2304]{1,0:T(8,128)(2,1)} async-done(((bf16[192,2304]{1,0:T(8,128)(2,1)}), bf16[768,2304]{1,0:T(8,128)(2,1)}) %all-gather.6.cloned.1.call-update) | async-done | bytes 3538960 | tf_op jit(solution)/shard_map/all_gather | solution.py:1153
  43.3 3.1 fusion.2
  46.5 0.1 fusion.1
  46.6 0.2 copy.50
  46.8 0.2 copy.52
  47.1 0.3 copy.53
  47.5 0.3 copy.51
  47.8 0.2 copy.54
  48.1 0.3 copy.55
  48.3 0.2 pad_maximum_fusion.in_ref
  48.6 30.1 %exchange.1 = bf16[8,256,384]{2,1,0:T(8,128)(2,1)S(1)} custom-call(bf16[8,256,384]{2,1,0:T(8,128)(2,1)S(1)} %pad_maximum_fusion.in_ref), custom_call_target="tpu_custom_call" | custom-call | tf_op jit(solution)/shard_map/exchange/pallas_call | solution.py:463
  78.7 7.3 %attend.1 = (bf16[16,128,128]{2,1,0:T(8,128)(2,1)S(1)}, bf16[16,128,384]{2,1,0:T(8,128)(2,1)S(1)}, f32[8,128,256]{2,1,0:T(8,128)S(1)}, f32[8,1,384]{2,1,0:T(1,128)S(1)}) custom-call(s32[16]{0:T(128)S(1)} %copy-done.3, s32[1]{0:T(128)S(6)} %copy.69.len_ref, s32[1]{0:T(128)} %bitcast.spot_ref, bf16[16,128,384]{2,1,0:T(8,128)(2,1)S(1)} %bitcast.42), custom_call_target="tpu_custom_call" | custom-call | tf_op jit(solution)/shard_map/attend/pallas_call | solution.py:631
  86.1 0.8 copy-done.1
  86.9 14.6 %all-gather.10.cloned.1.call-done.w_in_ref = bf16[768,3072]{1,0:T(8,128)(2,1)} async-done(((bf16[192,3072]{1,0:T(8,128)(2,1)}), bf16[768,3072]{1,0:T(8,128)(2,1)}) %all-gather.10.cloned.1.call-update) | async-done | bytes 4718608 | tf_op jit(solution)/shard_map/all_gather | solution.py:1160
  101.5 38.9 %all-gather.12.cloned.1.call-done.w_back_ref = bf16[3072,768]{1,0:T(8,128)(2,1)} async-done(((bf16[768,768]{1,0:T(8,128)(2,1)}), bf16[3072,768]{1,0:T(8,128)(2,1)}) %all-gather.12.cloned.1.call-update) | async-done | bytes 4718608 | tf_op jit(solution)/shard_map/all_gather | solution.py:1162
  140.4 39.6 %layer.1 = (f32[256,768]{1,0:T(8,128)}, bf16[8,256,128]{2,1,0:T(8,128)(2,1)}, bf16[7,4,192,256]{3,2,1,0:T(8,128)(2,1)}, bf16[6,256,768]{2,1,0:T(8,128)(2,1)}, f32[256,768]{1,0:T(8,128)}, /*index=5*/f32[16,768]{1,0:T(8,128)}) custom-call(s32[16]{0:T(128)} %pair_ref.5, s32[1]{0:T(128)S(6)} %copy.69.len_ref, bf16[8,256,128]{2,1,0:T(8,128)(2,1)} %bitcast.44, ...), custom_call_target="tpu_custom_call" | custom-call | tf_op jit(solution)/shard_map/layer/pallas_call | solution.py:836
  180.1 1.0 copy-done.2
  181.1 11.1 %attend_back.1 = bf16[16,128,384]{2,1,0:T(8,128)(2,1)S(1)} custom-call(s32[16]{0:T(128)S(1)} %copy-done.4, s32[1]{0:T(128)S(6)} %copy.69.len_ref, s32[1]{0:T(128)} %bitcast.spot_ref, bf16[16,128,384]{2,1,0:T(8,128)(2,1)S(1)} %get-tuple-element.36.keep_ref, bf16[16,128,128]{2,1,0:T(8,128)(2,1)S(1)} %bitcast.45, f32[8,128,256]{2,1,0:T(8,128)S(1)} %get-tuple-element.38.mix_ref, ...), custom_call_target="tpu_custom_call" | custom-call | tf_op jit(solution)/shard_map/attend_back/pallas_call | solution.py:649
  192.2 1.1 copy-done
  193.3 152.9 %sum_all.1 = (f32[256,768]{1,0:T(8,128)}, bf16[192,2304]{1,0:T(8,128)(2,1)}, bf16[192,768]{1,0:T(8,128)(2,1)}, bf16[192,3072]{1,0:T(8,128)(2,1)}, bf16[768,768]{1,0:T(8,128)(2,1)}, /*index=5*/f32[16,192]{1,0:T(8,128)}) custom-call(bf16[7,4,192,256]{3,2,1,0:T(8,128)(2,1)} %get-tuple-element.33.left_ref, bf16[6,256,768]{2,1,0:T(8,128)(2,1)} %get-tuple-element.34.right_ref, ...), custom_call_target="tpu_custom_call" | custom-call | tf_op jit(solution)/shard_map/sum_all/pallas_call | solution.py:1087
  346.2 0.8 slice.69
  347.0 1.6 fusion.4
  348.6 0.7 reshape.83
  349.3 1.8 convert_element_type.33
  351.1 2.5 convert_element_type.32
  353.6 1.7 convert_element_type.34
  355.3 1.6 convert_element_type.35
  356.9 0.9 copy.70
  357.7 0.9 copy.71
  (73 shorter events, 0.5 us)
Async XLA Ops:
  7.2 2.9 copy-start.19
  7.2 4.2 %copy-start.11 = (bf16[192]{0:T(256)(128)(2,1)S(1)}, bf16[192]{0:T(256)(128)(2,1)}, u32[]{:S(2)}) copy-start(bf16[192]{0:T(256)(128)(2,1)} %param.32) | copy-start | bytes 1156
  7.2 4.4 %copy-start.12 = (bf16[192]{0:T(256)(128)(2,1)S(1)}, bf16[192]{0:T(256)(128)(2,1)}, u32[]{:S(2)}) copy-start(bf16[192]{0:T(256)(128)(2,1)} %param.31) | copy-start | bytes 1156
  7.2 4.6 %copy-start.13 = (bf16[192]{0:T(256)(128)(2,1)S(1)}, bf16[192]{0:T(256)(128)(2,1)}, u32[]{:S(2)}) copy-start(bf16[192]{0:T(256)(128)(2,1)} %param.27) | copy-start | bytes 1156
  7.2 4.9 %copy-start.14 = (bf16[192]{0:T(256)(128)(2,1)S(1)}, bf16[192]{0:T(256)(128)(2,1)}, u32[]{:S(2)}) copy-start(bf16[192]{0:T(256)(128)(2,1)} %param.26) | copy-start | bytes 1156
  7.2 5.1 %copy-start.15 = (bf16[192]{0:T(256)(128)(2,1)S(1)}, bf16[192]{0:T(256)(128)(2,1)}, u32[]{:S(2)}) copy-start(bf16[192]{0:T(256)(128)(2,1)} %param.25) | copy-start | bytes 1156
  7.2 5.3 %copy-start.16 = (bf16[192]{0:T(256)(128)(2,1)S(1)}, bf16[192]{0:T(256)(128)(2,1)}, u32[]{:S(2)}) copy-start(bf16[192]{0:T(256)(128)(2,1)} %param.22) | copy-start | bytes 1156
  7.3 5.5 %copy-start.17 = (bf16[192]{0:T(256)(128)(2,1)S(1)}, bf16[192]{0:T(256)(128)(2,1)}, u32[]{:S(2)}) copy-start(bf16[192]{0:T(256)(128)(2,1)} %param.23) | copy-start | bytes 1156
  7.3 5.8 %copy-start.18 = (bf16[192]{0:T(256)(128)(2,1)S(1)}, bf16[192]{0:T(256)(128)(2,1)}, u32[]{:S(2)}) copy-start(bf16[192]{0:T(256)(128)(2,1)} %param.33) | copy-start | bytes 1156
  7.3 19.9 %copy-start.10 = (bf16[768]{0:T(1024)(128)(2,1)S(1)}, bf16[768]{0:T(1024)(128)(2,1)}, u32[]{:S(2)}) copy-start(bf16[768]{0:T(1024)(128)(2,1)} %param.29) | copy-start | bytes 4612
  7.3 36.1 %copy-start.5 = (bf16[1,256,768]{2,1,0:T(8,128)(2,1)S(1)}, bf16[1,256,768]{2,1,0:T(8,128)(2,1)}, u32[]{:S(2)}) copy-start(bf16[1,256,768]{2,1,0:T(8,128)(2,1)} %param.17) | copy-start | bytes 1179652
  7.3 36.0 %all-gather.6.cloned.1.call-start = ((), (), s32[]{:S(2)}) async-start(), calls=%async_computation | async-start | bytes 4423680 | tf_op jit(solution)/shard_map/all_gather | solution.py:1153
  8.0 78.8 %all-gather.8.cloned.1.call-start = ((), (), s32[]{:S(2)}) async-start(), calls=%async_computation.1 | async-start | bytes 1474560 | tf_op jit(solution)/shard_map/all_gather | solution.py:1156
  8.8 92.7 %all-gather.10.cloned.1.call-start = ((), (), s32[]{:S(2)}) async-start(), calls=%async_computation.2 | async-start | bytes 5898240 | tf_op jit(solution)/shard_map/all_gather | solution.py:1160
  9.5 130.9 %all-gather.12.cloned.1.call-start = ((), (), s32[]{:S(2)}) async-start(), calls=%async_computation.3 | async-start | bytes 5898240 | tf_op jit(solution)/shard_map/all_gather | solution.py:1162
  48.6 30.2 %copy-start.3 = (s32[16]{0:T(128)S(1)}, s32[16]{0:T(128)}, u32[]{:S(2)}) copy-start(s32[16]{0:T(128)} %pair_ref.5) | copy-start | bytes 196
  86.1 0.8 copy-start.1
  140.4 39.6 %copy-start.4 = (s32[16]{0:T(128)S(1)}, s32[16]{0:T(128)}, u32[]{:S(2)}) copy-start(s32[16]{0:T(128)} %pair_ref.5) | copy-start | bytes 196
  180.1 1.0 copy-start.2
  192.2 1.1 copy-start
  346.2 7.4 %copy-start.7 = (bf16[192,3072]{1,0:T(8,128)(2,1)S(1)}, bf16[192,3072]{1,0:T(8,128)(2,1)}, u32[]{:S(2)}) copy-start(bf16[192,3072]{1,0:T(8,128)(2,1)} %get-tuple-element.45) | copy-start | bytes 3538948
  353.6 1.7 copy-start.6
  355.3 1.6 copy-start.8
  355.3 2.5 copy-start.9
Sparse Core Ops, SparseCore 0:
  9.7 33.6 all-gather.5
  44.9 17.4 all-gather.7
  64.0 37.4 all-gather.9
  102.9 37.4 all-gather.11

commit v4 on v3

--- a/solution.py
+++ b/solution.py
@@ -428,66 +428,6 @@
         lax.psum(shards[12].astype(jnp.bfloat16), "ctx").astype(jnp.float32),
     )
     return (output[None], token_grad[None]) + tuple(totals)
-
-
-def exchange_kernel(n, in_ref, out_ref, sent, landed, own):
-    me = lax.axis_index("ctx")
-    barrier = pltpu.get_barrier_semaphore()
-    for k in range(1, n):
-        pl.semaphore_signal(
-            barrier, inc=1, device_id={"ctx": lax.rem(me + k, n)}, device_id_type=MESH
-        )
-    pl.semaphore_wait(barrier, n - 1)
-    copies = []
-    for k in range(1, n):
-        peer = lax.rem(me + k, n)
-        copy = pltpu.make_async_remote_copy(
-            src_ref=in_ref.at[peer],
-            dst_ref=out_ref.at[me],
-            send_sem=sent.at[k],
-            recv_sem=landed.at[k],
-            device_id={"ctx": peer},
-            device_id_type=MESH,
-        )
-        copy.start()
-        copies.append(copy)
-    local = pltpu.make_async_copy(in_ref.at[me], out_ref.at[me], own)
-    local.start()
-    local.wait()
-    for copy in copies:
-        copy.wait()
-
-
-def exchange(blocks, name):
-    n = blocks.shape[0]
-    return pl.pallas_call(
-        functools.partial(exchange_kernel, n),
-        out_shape=jax.ShapeDtypeStruct(blocks.shape, blocks.dtype),
-        in_specs=[vmem()],
-        out_specs=vmem(),
-        scratch_shapes=[
-            pltpu.SemaphoreType.DMA((n,)),
-            pltpu.SemaphoreType.DMA((n,)),
-            pltpu.SemaphoreType.DMA,
-        ],
-        compiler_params=pltpu.CompilerParams(
-            collective_id=name, has_side_effects=True, vmem_limit_bytes=16 << 20
-        ),
-        name="exchange",
-    )(blocks)
-
-
-def split_heads(value):
-    rows = value.shape[0]
-    trio = value.reshape(rows, HEADS // 3, 3, HEAD_DIM)
-    own = trio[:, :, :2]
-    shared = jnp.broadcast_to(trio[:, :, 2:], own.shape)
-    both = jnp.concatenate([own, shared], axis=-1)
-    return jnp.transpose(both.reshape(rows, -1, 2 * HEAD_DIM), (1, 0, 2))
-
-
-def send_blocks(queries, keys, values):
-    return jnp.concatenate([split_heads(queries), split_heads(keys), split_heads(values)], axis=2)
 
 
 def low_lanes(shape):
@@ -739,16 +679,34 @@
 
 
 def layer_kernel(
-    n, pair_ref, len_ref, mixed_ref, tokens_ref, cot_ref, w_out_ref, w_in_ref, w_back_ref, rows_ref,
+    n, pair_ref, len_ref, mixed_ref, tokens_ref, cot_ref, rows_ref, out_full, in_full, back_ref,
     output_ref, grad_in_ref, left_ref, right_ref, resid_ref, sums_ref,
-    mixed_in, grad_out, active, slope, in_sem, out_sem, own_sem,
+    mixed_in, grad_out, active, slope, w_out, w_in, w_back, in_sem, out_sem, back_sem, own_sem,
 ):
     low, wide = jnp.bfloat16, jnp.float32
     ctx = lax.axis_index("ctx")
     sums_ref[...] = jnp.zeros_like(sums_ref)
-    greet(ring_peers(n))
+    fsdp = lax.axis_index("fsdp")
+    x, core = fsdp // 2, lax.rem(fsdp, 2)
+    greet(ring_peers(n) + chip_peers())
     copies = exchange_copies(n, mixed_ref, mixed_in, in_sem)
     for cp in copies:
+        cp.start()
+    back_shards = gather_copies(back_ref, w_back, back_sem, 0)
+    for step in (0, 1):
+        back_shards[step].start()
+    width = tokens_ref.shape[1]
+    count = w_in.shape[0]
+    loads = [
+        pltpu.make_async_copy(out_full, w_out, own_sem.at[2]),
+        pltpu.make_async_copy(back_ref, w_back.at[fsdp], own_sem.at[3]),
+    ] + [
+        pltpu.make_async_copy(
+            in_full.at[:, :, t * width : (t + 1) * width], w_in.at[t], own_sem.at[4 + t]
+        )
+        for t in range(count)
+    ]
+    for cp in loads:
         cp.start()
     own = pltpu.make_async_copy(mixed_ref.at[ctx], mixed_in.at[ctx], own_sem.at[0])
     own.start()
@@ -767,21 +725,36 @@
         cp.wait_recv()
 
     attended = join_pairs(lambda peer: mixed_in[peer])
-    resid_one = tokens.astype(wide) + dot_nn(attended, w_out_ref[...]) + row(ROW_BO)
+    loads[0].wait()
+    resid_one = (
+        tokens.astype(wide)
+        + dot_nn(attended, w_out[...].reshape(width, width))
+        + row(ROW_BO)
+    )
     unit_one, scale_one = unit_of(resid_one)
     hidden = unit_one * row(ROW_G1) + row(ROW_S1)
     hidden_low = hidden.astype(low)
-    width = tokens.shape[1]
-    count = w_in_ref.shape[1] // width
     resid_two = hidden + row(ROW_BB)
-    for t in range(count):
-        cols = slice(t * width, (t + 1) * width)
-        upper = dot_nn(hidden_low, w_in_ref[:, cols]) + row(ROW_BI + t)
+    for cp in loads[2:]:
+        cp.wait()
+    order = [fsdp, 2 * x + 1 - core, 2 * (1 - x) + core, 2 * (1 - x) + 1 - core]
+    for step, t in enumerate(order):
+        bias = rows_ref[pl.ds(ROW_BI + t, 1), :]
+        upper = dot_nn(hidden_low, w_in[t].reshape(width, width)) + bias
         share = 0.5 * (1.0 + lax.erf(upper * (0.5**0.5)))
-        slope[:, cols] = share + upper * (jnp.exp(-0.5 * upper * upper) * (2 * math.pi) ** -0.5)
+        slope[t] = share + upper * (jnp.exp(-0.5 * upper * upper) * (2 * math.pi) ** -0.5)
         some = (upper * share).astype(low)
-        active[:, cols] = some
-        resid_two = resid_two + dot_nn(some, w_back_ref[cols, :])
+        active[t] = some
+        if step == 0:
+            loads[1].wait()
+        elif step == 1:
+            back_shards[1].wait_recv()
+        elif step == 2:
+            back_shards[0].wait_recv()
+            back_shards[2].start()
+        else:
+            back_shards[2].wait_recv()
+        resid_two = resid_two + dot_nn(some, w_back[t])
     unit_two, scale_two = unit_of(resid_two)
     output_ref[...] = jnp.where(valid, unit_two * row(ROW_G2) + row(ROW_S2), 0.0)
     grad_y = jnp.where(valid, cot_ref[...].astype(wide), 0.0)
@@ -793,11 +766,10 @@
     sums_ref[ROW_BB : ROW_BB + 1, :] = column_sum(grad_mixed.astype(wide))
     grad_hidden = grad_resid_two
     for t in range(count):
-        cols = slice(t * width, (t + 1) * width)
-        grad_upper = (dot_nt(grad_mixed, w_back_ref[cols, :]) * slope[:, cols]).astype(low)
+        grad_upper = (dot_nt(grad_mixed, w_back[t]) * slope[t]).astype(low)
         right_ref[1 + t] = grad_upper
         sums_ref[ROW_BI + t : ROW_BI + t + 1, :] = column_sum(grad_upper.astype(wide))
-        grad_hidden = grad_hidden + dot_nt(grad_upper, w_in_ref[:, cols])
+        grad_hidden = grad_hidden + dot_nt(grad_upper, w_in[t].reshape(width, width))
     sums_ref[ROW_G1 : ROW_G1 + 1, :] = column_sum(grad_hidden * unit_one)
     sums_ref[ROW_S1 : ROW_S1 + 1, :] = column_sum(grad_hidden)
     grad_resid_one = unit_back(unit_one, scale_one, grad_hidden * row(ROW_G1))
@@ -805,7 +777,7 @@
     grad_branch = grad_resid_one.astype(low)
     right_ref[0] = grad_branch
     sums_ref[ROW_BO : ROW_BO + 1, :] = column_sum(grad_branch.astype(wide))
-    grad_attended = dot_nt(grad_branch, w_out_ref[...]).astype(low)
+    grad_attended = dot_nt(grad_branch, w_out[...].reshape(width, width)).astype(low)
     for peer in range(n):
         grad_out[peer] = pair_of(grad_attended, peer)
     backs = exchange_copies(n, grad_out, grad_in_ref, out_sem)
@@ -816,7 +788,7 @@
     left_ref[1] = jnp.transpose(attended).reshape(4, -1, 2 * BLK)
     left_ref[2] = jnp.transpose(hidden_low).reshape(4, -1, 2 * BLK)
     for f in range(4):
-        turned = jnp.transpose(active[:, f * width : (f + 1) * width])
+        turned = jnp.transpose(active[f])
         for r in range(4):
             left_ref[3 + r, f] = turned[r * width // 4 : (r + 1) * width // 4]
     back.wait()
@@ -824,15 +796,17 @@
         cp.wait_send()
     for cp in backs:
         cp.wait()
-
-
-def layer(pairing, lengths, mixed, tokens, cotangent, w_out, w_in, w_back, rows, name):
+    for cp in back_shards:
+        cp.wait_send()
+
+
+def layer(pairing, lengths, mixed, tokens, cotangent, rows, out_full, in_full, w_back, name):
     n = mixed.shape[0]
     count, width = tokens.shape
-    inner = w_in.shape[1]
     low, wide = jnp.bfloat16, jnp.float32
     dma = pltpu.SemaphoreType.DMA
     shape = jax.ShapeDtypeStruct
+    anywhere = pl.BlockSpec(memory_space=pl.ANY)
     return pl.pallas_call(
         functools.partial(layer_kernel, n),
         out_shape=(
@@ -843,22 +817,165 @@
             shape((count, width), wide),
             shape((16, width), wide),
         ),
-        in_specs=[smem(), smem()] + [vmem()] * 7,
+        in_specs=[smem(), smem()] + [vmem()] * 4 + [anywhere] * 3,
         out_specs=(vmem(),) * 6,
         scratch_shapes=[
             pltpu.VMEM(mixed.shape, low),
             pltpu.VMEM(mixed.shape, low),
-            pltpu.VMEM((count, inner), low),
-            pltpu.VMEM((count, inner), wide),
+            pltpu.VMEM((4, count, width), low),
+            pltpu.VMEM((4, count, width), wide),
+            pltpu.VMEM(out_full.shape, low),
+            pltpu.VMEM((4, 4, width // 4, width), low),
+            pltpu.VMEM((4,) + w_back.shape, low),
             dma((2, n)),
             dma((2, n)),
-            dma((2,)),
+            dma((2, 1, 3)),
+            dma((8,)),
         ],
         compiler_params=pltpu.CompilerParams(
             collective_id=name, has_side_effects=True, vmem_limit_bytes=56 << 20
         ),
         name="layer",
-    )(pairing, lengths, mixed, tokens, cotangent, w_out, w_in, w_back, rows)
+    )(pairing, lengths, mixed, tokens, cotangent, rows, out_full, in_full, w_back)
+
+
+def gather_copies(src, full, sems, index):
+    fsdp = lax.axis_index("fsdp")
+    x, core = fsdp // 2, lax.rem(fsdp, 2)
+    sibling, across = {"fsdp": 2 * x + 1 - core}, {"fsdp": 2 * (1 - x) + core}
+    other = 2 * (1 - x) + core
+    return (
+        remote(src, full.at[fsdp], sems, (index, 0), across),
+        remote(src, full.at[fsdp], sems, (index, 1), sibling),
+        remote(full.at[other], full.at[other], sems, (index, 2), sibling),
+    )
+
+
+def chip_peers():
+    fsdp = lax.axis_index("fsdp")
+    x, core = fsdp // 2, lax.rem(fsdp, 2)
+    return [{"fsdp": 2 * x + 1 - core}, {"fsdp": 2 * (1 - x) + core}]
+
+
+def project_kernel(
+    n, tokens_ref, small_ref, qkv_ref, out_ref, in_ref,
+    packed_ref, rows_ref, qkv_full, out_full, in_full,
+    qkv_here, small_here, send, sems, own_sem, block_sem,
+):
+    low, wide = jnp.bfloat16, jnp.float32
+    ctx = lax.axis_index("ctx")
+    fsdp = lax.axis_index("fsdp")
+    greet(ring_peers(n) + chip_peers())
+    qkv = gather_copies(qkv_ref, qkv_here, sems, 0)
+    small = gather_copies(small_ref, small_here, sems, 1)
+    for step in (0, 1):
+        small[step].start()
+        qkv[step].start()
+    locals_ = [
+        pltpu.make_async_copy(src, dst, own_sem.at[i])
+        for i, (src, dst) in enumerate(
+            [
+                (qkv_ref, qkv_here.at[fsdp]),
+                (small_ref, small_here.at[fsdp]),
+                (out_ref, out_full.at[fsdp]),
+                (in_ref, in_full.at[fsdp]),
+            ]
+        )
+    ]
+    for cp in locals_:
+        cp.start()
+    small[0].wait_recv()
+    small[2].start()
+    qkv[0].wait_recv()
+    qkv[2].start()
+    later = [gather_copies(out_ref, out_full, sems, 2), gather_copies(in_ref, in_full, sems, 3)]
+    for step in (0, 1):
+        for cps in later:
+            cps[step].start()
+    for cps in (small, qkv):
+        cps[1].wait_recv()
+        cps[2].wait_recv()
+    locals_[0].wait()
+    locals_[1].wait()
+    keep = pltpu.make_async_copy(qkv_here, qkv_full, own_sem.at[4])
+    keep.start()
+    for f in range(4):
+        width = small_here.shape[2]
+        cols = slice(f * width, (f + 1) * width)
+        rows_ref[:8, cols] = small_here[f, :8]
+        for j in range(4):
+            rows_ref[ROW_BI + f : ROW_BI + f + 1, j * width : (j + 1) * width] = small_here[
+                f, 8 + j : 9 + j
+            ]
+    rows_ref[12:] = jnp.zeros_like(rows_ref[12:])
+    tokens = tokens_ref[...]
+    width = tokens.shape[1]
+    half = width // 2
+    for g in range(2):
+        parts = []
+        for part, bias in ((0, ROW_BQ), (1, None), (2, ROW_BV)):
+            at = part * width + g * half
+            value = dot_nn(tokens, qkv_here[:, :, at : at + half].reshape(width, half))
+            if bias is not None:
+                value = value + rows_ref[bias : bias + 1, g * half : (g + 1) * half]
+            parts.append(value.astype(low))
+        for spot in range(n // 2):
+            send[g * n // 2 + spot] = jnp.concatenate(
+                [pair_of(value, spot) for value in parts], axis=1
+            )
+    blocks = exchange_copies(n, send, packed_ref, block_sem)
+    for cp in blocks:
+        cp.start()
+    own = pltpu.make_async_copy(send.at[ctx], packed_ref.at[ctx], own_sem.at[5])
+    own.start()
+    for cps in later:
+        cps[0].wait_recv()
+        cps[2].start()
+    own.wait()
+    keep.wait()
+    locals_[2].wait()
+    locals_[3].wait()
+    for cp in blocks:
+        cp.wait()
+    for cps in later:
+        cps[0].wait_send()
+        cps[1].wait()
+        cps[2].wait()
+    for cps in (small, qkv):
+        for cp in cps:
+            cp.wait_send()
+
+
+def project(tokens, small, w_qkv, w_out, w_in, n, name):
+    low, wide = jnp.bfloat16, jnp.float32
+    dma = pltpu.SemaphoreType.DMA
+    shape = jax.ShapeDtypeStruct
+    count, width = tokens.shape
+    anywhere = pl.BlockSpec(memory_space=pl.ANY)
+    return pl.pallas_call(
+        functools.partial(project_kernel, n),
+        out_shape=(
+            shape((n, count, 6 * HEAD_DIM), low),
+            shape((16, width), wide),
+            shape((4,) + w_qkv.shape, low),
+            shape((4,) + w_out.shape, low),
+            shape((4,) + w_in.shape, low),
+        ),
+        in_specs=[vmem(), vmem()] + [anywhere] * 3,
+        out_specs=(vmem(), vmem()) + (anywhere,) * 3,
+        scratch_shapes=[
+            pltpu.VMEM((4,) + w_qkv.shape, low),
+            pltpu.VMEM((4,) + small.shape, wide),
+            pltpu.VMEM((n, count, 6 * HEAD_DIM), low),
+            dma((2, 4, 3)),
+            dma((6,)),
+            dma((2, n)),
+        ],
+        compiler_params=pltpu.CompilerParams(
+            collective_id=name, has_side_effects=True, vmem_limit_bytes=40 << 20
+        ),
+        name="project",
+    )(tokens, small, w_qkv, w_out, w_in)
 
 
 PARTS = 12
@@ -1149,65 +1266,31 @@
     ln2_gain,
     ln2_bias,
 ):
-    gathered = (
-        lax.all_gather(w_qkv, "fsdp", axis=0, tiled=True),
-        lax.all_gather(bias_q, "fsdp", axis=0, tiled=True),
-        lax.all_gather(bias_v, "fsdp", axis=0, tiled=True),
-        lax.all_gather(w_out, "fsdp", axis=0, tiled=True),
-        lax.all_gather(bias_out, "fsdp", axis=0, tiled=True),
-        lax.all_gather(ln1_gain, "fsdp", axis=0, tiled=True),
-        lax.all_gather(ln1_bias, "fsdp", axis=0, tiled=True),
-        lax.all_gather(w_in, "fsdp", axis=0, tiled=True),
-        lax.all_gather(bias_in, "fsdp", axis=0, tiled=True),
-        lax.all_gather(w_back, "fsdp", axis=0, tiled=True),
-        lax.all_gather(bias_back, "fsdp", axis=0, tiled=True),
-        lax.all_gather(ln2_gain, "fsdp", axis=0, tiled=True),
-        lax.all_gather(ln2_bias, "fsdp", axis=0, tiled=True),
-    )
-    (
-        qkv_all,
-        query_bias,
-        value_bias,
-        out_all,
-        out_bias,
-        gain_one,
-        shift_one,
-        in_all,
-        in_bias,
-        back_all,
-        back_bias,
-        gain_two,
-        shift_two,
-    ) = gathered
     rows = tokens.shape[1]
     half = rows // 2
     width = tokens.shape[2]
-    length = lengths[0]
-    query_place = places(pairing, lax.axis_index("ctx") * rows, rows, half)
-    valid = query_place < length
+    n = pairing.shape[0] // 2
     inputs = tokens[0]
-    proj = jnp.dot(inputs, qkv_all, preferred_element_type=jnp.float32)
-    queries = (proj[:, :width] + query_bias.astype(jnp.float32)).astype(jnp.bfloat16)
-    keys = proj[:, width : 2 * width].astype(jnp.bfloat16)
-    values = (proj[:, 2 * width :] + value_bias.astype(jnp.float32)).astype(jnp.bfloat16)
+    vectors = [bias_q, bias_v, bias_out, ln1_gain, ln1_bias, bias_back, ln2_gain, ln2_bias]
+    small = jnp.concatenate([jnp.stack(vectors), bias_in.reshape(4, -1)]).astype(jnp.float32)
+    small = jnp.pad(small, ((0, 16 - small.shape[0]), (0, 0)))
+    packed, lines, qkv_full, out_full, in_full = project(
+        inputs, small, w_qkv, w_out, w_in, n, 0
+    )
     spot = lax.rem(lax.axis_index("ctx"), 2).astype(jnp.int32).reshape(1)
-    sent = send_blocks(queries, keys, values)
-    packed = exchange(sent, 0).reshape(-1, half, 6 * HEAD_DIM)
-    mixed_out, keep, mix, lse = attend(pairing, lengths, spot, packed)
-    vectors = [
-        query_bias, value_bias, out_bias, gain_one, shift_one, back_bias, gain_two, shift_two
-    ]
-    vectors = jnp.concatenate([jnp.stack(vectors), in_bias.reshape(-1, width)]).astype(jnp.float32)
-    vectors = jnp.pad(vectors, ((0, 16 - vectors.shape[0]), (0, 0)))
+    mixed_out, keep, mix, lse = attend(
+        pairing, lengths, spot, packed.reshape(-1, half, 6 * HEAD_DIM)
+    )
     output, grad_in, left, right, resid, sums = layer(
         pairing, lengths, mixed_out.reshape(-1, rows, 2 * HEAD_DIM), inputs, cotangent[0],
-        out_all, in_all, back_all, vectors, 1,
+        lines, out_full, in_full, w_back, 1,
     )
     grad_blocks = attend_back(
         pairing, lengths, spot, keep, grad_in.reshape(-1, half, 2 * HEAD_DIM), mix, lse
     )
     token_grad, qkv_sum, out_sum, in_sum, back_sum, small = sum_all(
-        left, right, sums, grad_blocks.reshape(-1, rows, 6 * HEAD_DIM), qkv_all, resid, 2
+        left, right, sums, grad_blocks.reshape(-1, rows, 6 * HEAD_DIM), qkv_full.reshape(width, -1),
+        resid, 2
     )
     wide = lambda value: value.astype(jnp.float32)
     return (

time: 366 us -> 316 us (0.86)
  waiting for transfers between devices: 66.2 us -> 0 us
  Pallas kernels: 241 us -> 283 us
  blocking collectives: 18.6 us -> 0 us
  between operations: 15.5 us -> 1.43 us
  local copies, waits for them, and re-layouts: 11.9 us -> 24.3 us
    all_gather x4 -> x0, waiting for transfers between devices: 63.6 us -> none  [the longest x1 38.9 us: on_device_spread(): lax.all_gather(w_back, 'fsdp', axis=0, tiled=True)]
    pallas_call x1, Pallas kernels: 30.1 us -> 62 us  [project(): pl.pallas_call(functools.partial(project_kernel, n), out_shape=(shape((n,...]
    pallas_call x1, Pallas kernels: 39.6 us -> 54.8 us  [layer(): pl.pallas_call(functools.partial(layer_kernel, n), out_shape=(shape((coun...]
    unnamed x1 -> x0, blocking collectives: 13.2 us -> none
    unnamed x61 -> x38, local copies, waits for them, and re-layouts: 7.25 us -> 15.2 us
    all_gather x1 -> x0, blocking collectives: 5.38 us -> none  [on_device_spread(): lax.all_gather(bias_in, 'fsdp', axis=0, tiled=True)]
    another operation x8, local copies, waits for them, and re-layouts: 0.04 us -> 5.26 us  [on_device_spread(): jnp.stack(vectors)]
    pallas_call x1, Pallas kernels: 153 us -> 148 us  [sum_all(): pl.pallas_call(functools.partial(sum_kernel, n), out_shape=(shape(resid.s...]
  transfers between devices with their start and end apart: 4 -> 0, of which waited for: 3 -> 0; matrix products, arithmetic and copies ran while one was open for 2% -> 0% of each run, Pallas kernels for 10% -> 0%
where the time goes in v4:
time: 316 us; the launch traced here: 315 us
  Pallas kernels  283 us (90%)
  local copies, waits for them, and re-layouts  24.3 us (8%)
  other arithmetic  6.48 us (2%)
    pallas_call x1, Pallas kernels, sum_all(): pl.pallas_call(functools.partial(sum_kernel, n), out_shape=(shape(resid.s...  148 us
    pallas_call x1, Pallas kernels, project(): pl.pallas_call(functools.partial(project_kernel, n), out_shape=(shape((n,...  62 us
    pallas_call x1, Pallas kernels, layer(): pl.pallas_call(functools.partial(layer_kernel, n), out_shape=(shape((coun...  54.8 us
    unnamed x38, local copies, waits for them, and re-layouts  15.2 us
    pallas_call x1, Pallas kernels, attend_back(): pl.pallas_call(functools.partial(attend_back_kernel, chunks), out_shape=j...  11.1 us
    pallas_call x1, Pallas kernels, attend(): pl.pallas_call(functools.partial(attend_kernel, chunks), out_shape=(jax.S...  7.33 us
    convert_element_type x4, other arithmetic, on_device_spread(): wide = lambda value: value.astype(jnp.float32)  6.47 us

profile of v4, /device:TPU:0, one launch (start us, length us, event | category | flops | bytes accessed | tf_op | source)
XLA Modules:
  0.0 315.2 jit_solution(136246232889228381)
XLA Ops:
  0.6 0.0 copy-start.11
  1.3 0.7 stack.24
  2.0 0.7 stack.25
  2.6 0.7 stack.26
  3.3 0.7 stack.27
  4.0 0.7 stack.28
  4.6 0.7 stack.29
  5.3 0.7 stack.30
  5.9 0.7 stack.31
  6.6 0.8 reshape.55
  7.4 0.0 copy-start.3
  7.4 1.0 copy-done.3
  8.4 1.3 copy-done.5
  9.7 1.2 copy-done.6
  10.8 1.0 copy-done.9
  11.8 62.0 %project.1 = (bf16[8,256,384]{2,1,0:T(8,128)(2,1)S(1)}, f32[16,768]{1,0:T(8,128)S(1)}, bf16[4,192,2304]{2,1,0:T(8,128)(2,1)S(1)}, bf16[4,192,768]{2,1,0:T(8,128)(2,1)S(1)}, bf16[4,192,3072]{2,1,0:T(8,128)(2,1)S(1)}) custom-call(bf16[256,768]{1,0:T(8,128)(2,1)S(1)} %bitcast.21, f32[16,192]{1,0:T(8,128)S(1)} %pad_convert_fusion.small_ref, ...), custom_call_target="tpu_custom_call" | custom-call | tf_op jit(solution)/shard_map/project/pallas_call | solution.py:955
  73.9 0.0 copy-start.1
  73.9 2.1 copy-done.1
  76.0 1.8 copy-done.2
  77.8 1.0 copy-done.4
  78.8 0.6 copy-done.10
  79.4 0.0 copy-done.11
  79.4 7.3 %attend.1 = (bf16[16,128,128]{2,1,0:T(8,128)(2,1)S(1)}, bf16[16,128,384]{2,1,0:T(8,128)(2,1)S(1)}, f32[8,128,256]{2,1,0:T(8,128)S(1)}, f32[8,1,384]{2,1,0:T(1,128)S(1)}) custom-call(s32[16]{0:T(128)S(1)} %copy-done.11, s32[1]{0:T(128)S(6)} %copy.34.len_ref, s32[1]{0:T(128)} %bitcast.spot_ref, bf16[16,128,384]{2,1,0:T(8,128)(2,1)S(1)} %bitcast.22), custom_call_target="tpu_custom_call" | custom-call | tf_op jit(solution)/shard_map/attend/pallas_call | solution.py:571
  86.8 0.0 copy-start.8
  86.8 0.8 copy-done.8
  87.6 54.8 %layer.1 = (f32[256,768]{1,0:T(8,128)}, bf16[8,256,128]{2,1,0:T(8,128)(2,1)}, bf16[7,4,192,256]{3,2,1,0:T(8,128)(2,1)}, bf16[6,256,768]{2,1,0:T(8,128)(2,1)}, f32[256,768]{1,0:T(8,128)}, /*index=5*/f32[16,768]{1,0:T(8,128)}) custom-call(s32[16]{0:T(128)} %pair_ref.5, s32[1]{0:T(128)S(6)} %copy.34.len_ref, bf16[8,256,128]{2,1,0:T(8,128)(2,1)} %bitcast.24, ...), custom_call_target="tpu_custom_call" | custom-call | tf_op jit(solution)/shard_map/layer/pallas_call | solution.py:810
  142.4 0.0 copy-done.12
  142.4 0.0 copy-start.7
  142.4 1.0 copy-done.7
  143.4 11.1 %attend_back.1 = bf16[16,128,384]{2,1,0:T(8,128)(2,1)S(1)} custom-call(s32[16]{0:T(128)S(1)} %copy-done.12, s32[1]{0:T(128)S(6)} %copy.34.len_ref, s32[1]{0:T(128)} %bitcast.spot_ref, bf16[16,128,384]{2,1,0:T(8,128)(2,1)S(1)} %get-tuple-element.45.keep_ref, bf16[16,128,128]{2,1,0:T(8,128)(2,1)S(1)} %bitcast.23, ...), custom_call_target="tpu_custom_call" | custom-call | tf_op jit(solution)/shard_map/attend_back/pallas_call | solution.py:589
  154.5 0.0 copy-start
  154.5 1.1 copy-done
  155.7 147.7 %sum_all.1 = (f32[256,768]{1,0:T(8,128)}, bf16[192,2304]{1,0:T(8,128)(2,1)}, bf16[192,768]{1,0:T(8,128)(2,1)}, bf16[192,3072]{1,0:T(8,128)(2,1)}, bf16[768,768]{1,0:T(8,128)(2,1)}, /*index=5*/f32[16,192]{1,0:T(8,128)}) custom-call(bf16[7,4,192,256]{3,2,1,0:T(8,128)(2,1)} %get-tuple-element.42.left_ref, bf16[6,256,768]{2,1,0:T(8,128)(2,1)} %get-tuple-element.43.right_ref, ...), custom_call_target="tpu_custom_call" | custom-call | tf_op jit(solution)/shard_map/sum_all/pallas_call | solution.py:1204
  303.4 0.0 copy-start.15
  303.4 0.8 slice.32
  304.2 1.6 fusion
  305.7 0.7 reshape.61
  306.4 1.9 convert_element_type.16
  308.3 0.0 copy-done.15
  308.3 1.3 convert_element_type.15
  309.6 0.0 copy-done.14
  309.6 1.7 convert_element_type.17
  311.3 0.0 copy-done.13
  311.3 1.6 convert_element_type.18
  312.9 0.0 copy-done.16
  312.9 0.9 copy.35
  313.8 0.5 copy-done.17
  314.3 0.9 copy.36
  (13 shorter events, 0.1 us)
Async XLA Ops:
  0.6 78.8 %copy-start.11 = (s32[16]{0:T(128)S(1)}, s32[16]{0:T(128)}, u32[]{:S(2)}) copy-start(s32[16]{0:T(128)} %pair_ref.5) | copy-start | bytes 196
  7.4 1.0 copy-start.3
  8.4 1.3 copy-start.5
  9.7 1.2 copy-start.6
  10.8 1.0 copy-start.9
  73.9 2.1 copy-start.1
  76.0 1.8 copy-start.2
  77.8 1.0 copy-start.4
  78.8 0.6 copy-start.10
  86.8 0.8 copy-start.8
  87.6 54.8 %copy-start.12 = (s32[16]{0:T(128)S(1)}, s32[16]{0:T(128)}, u32[]{:S(2)}) copy-start(s32[16]{0:T(128)} %pair_ref.5) | copy-start | bytes 196
  142.4 1.0 copy-start.7
  154.5 1.1 copy-start
  303.4 5.0 %copy-start.15 = (bf16[192,2304]{1,0:T(8,128)(2,1)S(1)}, bf16[192,2304]{1,0:T(8,128)(2,1)}, u32[]{:S(2)}) copy-start(bf16[192,2304]{1,0:T(8,128)(2,1)} %get-tuple-element.52) | copy-start | bytes 2654212
  306.4 3.2 %copy-start.14 = (bf16[192,3072]{1,0:T(8,128)(2,1)S(1)}, bf16[192,3072]{1,0:T(8,128)(2,1)}, u32[]{:S(2)}) copy-start(bf16[192,3072]{1,0:T(8,128)(2,1)} %get-tuple-element.55) | copy-start | bytes 3538948
  309.6 1.7 copy-start.13
  311.3 1.6 copy-start.16
  312.9 1.4 copy-start.17

commit v5 on v4

--- a/solution.py
+++ b/solution.py
@@ -434,12 +434,15 @@
     return lax.broadcasted_iota(jnp.int32, shape, 1) < 64
 
 
-def attend_kernel(chunks, pair_ref, len_ref, spot_ref, in_ref, out_ref, keep_ref, mix_ref, lse_ref):
+def attend_kernel(
+    chunks, pair_ref, len_ref, spot_ref, in_ref, out_ref, keep_ref, mix_ref, lse_ref, back_ref
+):
     length = len_ref[0]
     spot = spot_ref[0]
     blocks = 2 * chunks
     for s in range(blocks):
         keep_ref[pair_ref[s]] = in_ref[s]
+        back_ref[pair_ref[s]] = s
     left = low_lanes((256, BLK))
     left_half = left[:BLK]
     for c in range(chunks):
@@ -454,7 +457,7 @@
         value = keep_ref[: 2 * c + 2, :, 2 * BLK :].reshape(keys, BLK)
         scores = mask_scores(
             lax.dot_general(key, query, (((1,), (1,)), ((), ())), preferred_element_type=jnp.float32),
-            c, spot, length,
+            c, spot, length, 0, True,
         )
         top = jnp.max(scores, axis=0, keepdims=True)
         probs = jnp.exp(scores - top)
@@ -479,82 +482,77 @@
         out_ref[s] = jnp.transpose(piece).astype(jnp.bfloat16)
 
 
-def mask_scores(scores, c, spot, length):
+def mask_scores(scores, c, spot, length, start, edged):
     keys, width = scores.shape
+    row = start + lax.broadcasted_iota(jnp.int32, (keys, width), 0)
+    scores = jnp.where(row < length, scores, neg_big)
+    if not edged:
+        return scores
     edge = 256 * c
-    row = lax.broadcasted_iota(jnp.int32, (keys, width), 0)
-    scores = jnp.where(row < length, scores, neg_big)
     lane = lax.broadcasted_iota(jnp.int32, (256, width), 1)
     query_place = edge + jnp.where(lane < 256, lane, lane - 256 + spot * BLK)
     key_place = edge + lax.broadcasted_iota(jnp.int32, (256, width), 0)
     seen = key_place <= query_place
     if c == 0:
         seen = seen | (key_place < NMEM)
-    tail = jnp.where(seen, scores[edge:], neg_big)
-    if c == 0:
+    tail = jnp.where(seen, scores[keys - 256 :], neg_big)
+    if keys == 256:
         return tail
-    return jnp.concatenate([scores[:edge], tail], axis=0)
-
-
-def attend_back_kernel(
-    chunks, pair_ref, len_ref, spot_ref, keep_ref, grad_ref, mix_ref, lse_ref, out_ref, g_ref,
-    q_sum, k_sum, v_sum
+    return jnp.concatenate([scores[: keys - 256], tail], axis=0)
+
+
+def attend_back(
+    c, length, spot, keep_ref, g_ref, mix_ref, lse_ref, q_sum, k_sum, v_sum
 ):
-    length = len_ref[0]
-    spot = spot_ref[0]
-    blocks = 2 * chunks
-    for s in range(blocks):
-        g_ref[pair_ref[s]] = grad_ref[s]
-    k_sum[...] = jnp.zeros_like(k_sum)
-    v_sum[...] = jnp.zeros_like(v_sum)
+    zero = jnp.zeros((), jnp.bfloat16)
     left = low_lanes((256, BLK))
     left_half = left[:BLK]
-    zero = jnp.zeros((), jnp.bfloat16)
-    for c in range(chunks):
-        keys = 256 * (c + 1)
-        own = keep_ref[2 * c : 2 * c + 2, :, :BLK].reshape(256, BLK)
-        shared = keep_ref[2 * c + spot, :, :BLK]
-        query = jnp.concatenate(
-            [jnp.where(left, own, zero), jnp.where(left_half, zero, shared)], axis=0
-        ) * jnp.bfloat16(0.125)
-        g_own = g_ref[2 * c : 2 * c + 2].reshape(256, BLK)
-        g_shared = g_ref[2 * c + spot]
-        grad = jnp.concatenate(
-            [jnp.where(left, g_own, zero), jnp.where(left_half, zero, g_shared)], axis=0
+    own = keep_ref[2 * c : 2 * c + 2, :, :BLK].reshape(256, BLK)
+    shared = keep_ref[2 * c + spot, :, :BLK]
+    query = jnp.concatenate(
+        [jnp.where(left, own, zero), jnp.where(left_half, zero, shared)], axis=0
+    ) * jnp.bfloat16(0.125)
+    g_own = g_ref[2 * c : 2 * c + 2].reshape(256, BLK)
+    g_shared = g_ref[2 * c + spot]
+    grad = jnp.concatenate(
+        [jnp.where(left, g_own, zero), jnp.where(left_half, zero, g_shared)], axis=0
+    )
+    turned = jnp.transpose(g_own.astype(jnp.float32)) * mix_ref[c]
+    delta_own = jnp.sum(turned[:64], axis=0, keepdims=True)
+    delta_pair = jnp.sum(turned[64:], axis=0, keepdims=True)
+    delta = jnp.concatenate(
+        [delta_own, jnp.where(spot == 0, delta_pair[:, :BLK], delta_pair[:, BLK:])], axis=1
+    )
+    lse = lse_ref[c]
+    q_grad = jnp.zeros((384, BLK), jnp.float32)
+    last = 2 * c + 2
+    step = 8
+    for low_block in range(0, last, step):
+        high_block = min(low_block + step, last)
+        cut = slice(low_block, high_block)
+        count = high_block - low_block
+        key = keep_ref[cut, :, BLK : 2 * BLK].reshape(count * BLK, BLK)
+        value = keep_ref[cut, :, 2 * BLK :].reshape(count * BLK, BLK)
+        scores = mask_scores(
+            dot_nt(key, query), c, spot, length, low_block * BLK, high_block == last
         )
-        key = keep_ref[: 2 * c + 2, :, BLK : 2 * BLK].reshape(keys, BLK)
-        value = keep_ref[: 2 * c + 2, :, 2 * BLK :].reshape(keys, BLK)
-        turned = jnp.transpose(g_own.astype(jnp.float32)) * mix_ref[c]
-        delta_own = jnp.sum(turned[:64], axis=0, keepdims=True)
-        delta_pair = jnp.sum(turned[64:], axis=0, keepdims=True)
-        delta = jnp.concatenate(
-            [delta_own, jnp.where(spot == 0, delta_pair[:, :BLK], delta_pair[:, BLK:])], axis=1
+        probs = jnp.exp(scores - lse)
+        score_grad = (probs * (dot_nt(value, grad) - delta)).astype(jnp.bfloat16)
+        v_part = dot_nn(probs.astype(jnp.bfloat16), grad)
+        k_part = dot_nn(score_grad, query)
+        v_sum[cut] += v_part.reshape(count, BLK, BLK)
+        k_sum[cut] += k_part.reshape(count, BLK, BLK)
+        q_grad = q_grad + lax.dot_general(
+            score_grad, key, (((0,), (0,)), ((), ())), preferred_element_type=jnp.float32
         )
-        nt = (((1,), (1,)), ((), ()))
-        scores = mask_scores(
-            lax.dot_general(key, query, nt, preferred_element_type=jnp.float32), c, spot, length
-        )
-        probs = jnp.exp(scores - lse_ref[c])
-        prob_grad = lax.dot_general(value, grad, nt, preferred_element_type=jnp.float32)
-        score_grad = (probs * (prob_grad - delta)).astype(jnp.bfloat16)
-        nn = (((1,), (0,)), ((), ()))
-        v_sum[:keys] += lax.dot_general(
-            probs.astype(jnp.bfloat16), grad, nn, preferred_element_type=jnp.float32
-        )
-        k_sum[:keys] += lax.dot_general(score_grad, query, nn, preferred_element_type=jnp.float32)
-        q_grad = lax.dot_general(
-            score_grad, key, (((0,), (0,)), ((), ())), preferred_element_type=jnp.float32
-        ) * 0.125
-        part = q_grad[256:]
-        none = jnp.zeros_like(part)
-        first = jnp.where(spot == 0, part, none)
-        second = jnp.where(spot == 0, none, part)
-        q_sum[256 * c : 256 * c + 256] = jnp.where(
-            left, q_grad[:256], jnp.concatenate([first, second], axis=0)
-        )
-    for s in range(blocks):
-        rows = pl.ds(pl.multiple_of(pair_ref[s] * BLK, BLK), BLK)
-        out_ref[s] = jnp.concatenate([q_sum[rows], k_sum[rows], v_sum[rows]], axis=1).astype(jnp.bfloat16)
+    q_grad = q_grad * 0.125
+    part = q_grad[256:]
+    none = jnp.zeros_like(part)
+    first = jnp.where(spot == 0, part, none)
+    second = jnp.where(spot == 0, none, part)
+    q_sum[2 * c : 2 * c + 2] = jnp.where(
+        left, q_grad[:256], jnp.concatenate([first, second], axis=0)
+    ).reshape(2, BLK, BLK)
 
 
 def smem():
@@ -575,31 +573,13 @@
             jax.ShapeDtypeStruct((blocks, BLK, 3 * BLK), jnp.bfloat16),
             jax.ShapeDtypeStruct((chunks, BLK, 256), jnp.float32),
             jax.ShapeDtypeStruct((chunks, 1, 384), jnp.float32),
+            jax.ShapeDtypeStruct((blocks,), jnp.int32),
         ),
         in_specs=[smem(), smem(), smem(), vmem()],
-        out_specs=(vmem(), vmem(), vmem(), vmem()),
+        out_specs=(vmem(), vmem(), vmem(), vmem(), smem()),
         compiler_params=pltpu.CompilerParams(vmem_limit_bytes=48 << 20),
         name="attend",
     )(pairing, lengths, spot, packed)
-
-
-def attend_back(pairing, lengths, spot, keep, grad, mix, lse):
-    blocks = keep.shape[0]
-    chunks = blocks // 2
-    return pl.pallas_call(
-        functools.partial(attend_back_kernel, chunks),
-        out_shape=jax.ShapeDtypeStruct((blocks, BLK, 3 * BLK), jnp.bfloat16),
-        in_specs=[smem(), smem(), smem(), vmem(), vmem(), vmem(), vmem()],
-        out_specs=vmem(),
-        scratch_shapes=[
-            pltpu.VMEM((blocks, BLK, BLK), jnp.bfloat16),
-            pltpu.VMEM((blocks * BLK, BLK), jnp.float32),
-            pltpu.VMEM((blocks * BLK, BLK), jnp.float32),
-            pltpu.VMEM((blocks * BLK, BLK), jnp.float32),
-        ],
-        compiler_params=pltpu.CompilerParams(vmem_limit_bytes=48 << 20),
-        name="attend_back",
-    )(pairing, lengths, spot, keep, grad, mix, lse)
 
 
 MESH = pl.DeviceIdType.MESH
@@ -624,12 +604,29 @@
     return [{"ctx": lax.rem(me + k, n)} for k in range(1, n)]
 
 
+def two(block):
+    return pl.ds(2 * block, 2)
+
+
 def exchange_copies(n, in_ref, out_ref, sems):
     me = lax.axis_index("ctx")
-    return [
-        remote(in_ref.at[lax.rem(me + k, n)], out_ref.at[me], sems, (k,), {"ctx": lax.rem(me + k, n)})
-        for k in range(1, n)
-    ]
+    copies = []
+    for k in range(1, n):
+        peer = lax.rem(me + k, n)
+        copies.append(
+            remote(in_ref.at[two(peer)], out_ref.at[two(me)], sems, (k,), {"ctx": peer})
+        )
+    return copies
+
+
+def own_copy(in_ref, out_ref, sem):
+    me = lax.axis_index("ctx")
+    return pltpu.make_async_copy(in_ref.at[two(me)], out_ref.at[two(me)], sem)
+
+
+def both(ref, peer):
+    value = ref[2 * peer : 2 * peer + 2]
+    return value.reshape(-1, value.shape[2])
 
 
 def join_pairs(pairs):
@@ -680,8 +677,8 @@
 
 def layer_kernel(
     n, pair_ref, len_ref, mixed_ref, tokens_ref, cot_ref, rows_ref, out_full, in_full, back_ref,
-    output_ref, grad_in_ref, left_ref, right_ref, resid_ref, sums_ref,
-    mixed_in, grad_out, active, slope, w_out, w_in, w_back, in_sem, out_sem, back_sem, own_sem,
+    output_ref, grad_ref, left_ref, right_ref, resid_ref, sums_ref,
+    mixed_in, active, slope, w_out, w_in, w_back, in_sem, back_sem, own_sem,
 ):
     low, wide = jnp.bfloat16, jnp.float32
     ctx = lax.axis_index("ctx")
@@ -708,7 +705,7 @@
     ]
     for cp in loads:
         cp.start()
-    own = pltpu.make_async_copy(mixed_ref.at[ctx], mixed_in.at[ctx], own_sem.at[0])
+    own = own_copy(mixed_ref, mixed_in, own_sem.at[0])
     own.start()
     row = lambda i: rows_ref[i : i + 1, :]
     tokens = tokens_ref[...]
@@ -724,7 +721,7 @@
     for cp in copies:
         cp.wait_recv()
 
-    attended = join_pairs(lambda peer: mixed_in[peer])
+    attended = join_pairs(lambda peer: both(mixed_in, peer))
     loads[0].wait()
     resid_one = (
         tokens.astype(wide)
@@ -779,34 +776,26 @@
     sums_ref[ROW_BO : ROW_BO + 1, :] = column_sum(grad_branch.astype(wide))
     grad_attended = dot_nt(grad_branch, w_out[...].reshape(width, width)).astype(low)
     for peer in range(n):
-        grad_out[peer] = pair_of(grad_attended, peer)
-    backs = exchange_copies(n, grad_out, grad_in_ref, out_sem)
-    for cp in backs:
-        cp.start()
-    back = pltpu.make_async_copy(grad_out.at[ctx], grad_in_ref.at[ctx], own_sem.at[1])
-    back.start()
+        grad_ref[2 * peer : 2 * peer + 2] = pair_of(grad_attended, peer).reshape(2, BLK, BLK)
     left_ref[1] = jnp.transpose(attended).reshape(4, -1, 2 * BLK)
     left_ref[2] = jnp.transpose(hidden_low).reshape(4, -1, 2 * BLK)
     for f in range(4):
         turned = jnp.transpose(active[f])
         for r in range(4):
             left_ref[3 + r, f] = turned[r * width // 4 : (r + 1) * width // 4]
-    back.wait()
     for cp in copies:
         cp.wait_send()
-    for cp in backs:
-        cp.wait()
     for cp in back_shards:
         cp.wait_send()
 
 
 def layer(pairing, lengths, mixed, tokens, cotangent, rows, out_full, in_full, w_back, name):
-    n = mixed.shape[0]
+    n = mixed.shape[0] // 2
     count, width = tokens.shape
     low, wide = jnp.bfloat16, jnp.float32
     dma = pltpu.SemaphoreType.DMA
     shape = jax.ShapeDtypeStruct
-    anywhere = pl.BlockSpec(memory_space=pl.ANY)
+    anywhere = pl.BlockSpec(memory_space=pltpu.HBM)
     return pl.pallas_call(
         functools.partial(layer_kernel, n),
         out_shape=(
@@ -821,13 +810,11 @@
         out_specs=(vmem(),) * 6,
         scratch_shapes=[
             pltpu.VMEM(mixed.shape, low),
-            pltpu.VMEM(mixed.shape, low),
             pltpu.VMEM((4, count, width), low),
             pltpu.VMEM((4, count, width), wide),
             pltpu.VMEM(out_full.shape, low),
             pltpu.VMEM((4, 4, width // 4, width), low),
             pltpu.VMEM((4,) + w_back.shape, low),
-            dma((2, n)),
             dma((2, n)),
             dma((2, 1, 3)),
             dma((8,)),
@@ -863,7 +850,6 @@
     qkv_here, small_here, send, sems, own_sem, block_sem,
 ):
     low, wide = jnp.bfloat16, jnp.float32
-    ctx = lax.axis_index("ctx")
     fsdp = lax.axis_index("fsdp")
     greet(ring_peers(n) + chip_peers())
     qkv = gather_copies(qkv_ref, qkv_here, sems, 0)
@@ -920,13 +906,14 @@
                 value = value + rows_ref[bias : bias + 1, g * half : (g + 1) * half]
             parts.append(value.astype(low))
         for spot in range(n // 2):
-            send[g * n // 2 + spot] = jnp.concatenate(
+            peer = g * n // 2 + spot
+            send[2 * peer : 2 * peer + 2] = jnp.concatenate(
                 [pair_of(value, spot) for value in parts], axis=1
-            )
+            ).reshape(2, BLK, -1)
     blocks = exchange_copies(n, send, packed_ref, block_sem)
     for cp in blocks:
         cp.start()
-    own = pltpu.make_async_copy(send.at[ctx], packed_ref.at[ctx], own_sem.at[5])
+    own = own_copy(send, packed_ref, own_sem.at[5])
     own.start()
     for cps in later:
         cps[0].wait_recv()
@@ -951,11 +938,11 @@
     dma = pltpu.SemaphoreType.DMA
     shape = jax.ShapeDtypeStruct
     count, width = tokens.shape
-    anywhere = pl.BlockSpec(memory_space=pl.ANY)
+    anywhere = pl.BlockSpec(memory_space=pltpu.HBM)
     return pl.pallas_call(
         functools.partial(project_kernel, n),
         out_shape=(
-            shape((n, count, 6 * HEAD_DIM), low),
+            shape((2 * n, BLK, 6 * HEAD_DIM), low),
             shape((16, width), wide),
             shape((4,) + w_qkv.shape, low),
             shape((4,) + w_out.shape, low),
@@ -966,7 +953,7 @@
         scratch_shapes=[
             pltpu.VMEM((4,) + w_qkv.shape, low),
             pltpu.VMEM((4,) + small.shape, wide),
-            pltpu.VMEM((n, count, 6 * HEAD_DIM), low),
+            pltpu.VMEM((2 * n, BLK, 6 * HEAD_DIM), low),
             dma((2, 4, 3)),
             dma((6,)),
             dma((2, n)),
@@ -989,29 +976,101 @@
     return left, right
 
 
-def sum_kernel(
-    n, left_ref, right_ref, sums_ref, blocks_ref, w_qkv_ref, resid_ref,
-    token_ref, qkv_out, out_out, in_out, back_out, small_out,
-    blocks_in, right_all, total_ref, pair_out, pair_in, x_out, x_in, first_sum, y_out, y_in, half_sum,
-    z_out, z_in, s_pair, s_x_out, s_x, s_y_out, s_y, s_z_out, s_z,
-    block_sem, own_sem, pair_sem, x_sem, y_sem, z_sem, spread_sem, last_sem, s_sem,
+STEPS = 30
+PLAN = {
+    "pair": {**{s: s for s in range(9)}, 17: 9, 18: 10, 19: 11},
+    "x": {**{s + 1: s for s in range(9)}, 18: 9, 19: 10, 20: 11},
+    "y": {9: 0, 10: 1, 12: 2, 13: 3, 14: 4, 15: 5, 16: 6, 18: 7, 19: 8, 22: 9, 23: 10, 24: 11},
+    "near": {10: 0, 11: 1, 13: 2, 14: 3, 15: 4, 16: 5, 18: 6, 19: 7, 20: 8, 23: 9, 24: 10, 25: 11},
+    "far": {11: 0, 12: 1, **{15 + c: c for c in range(2, 12)}},
+    "own": {12: 0, **{16 + c: c for c in range(1, 12)}},
+    "wide": {17 + c: c for c in range(12)},
+    "last": {18 + c: c for c in range(12)},
+}
+ATTEND_AT = (10, 11, 12)
+JOIN_AT = 17
+SMALL_AT = (17, 18, 20, 22, 24, 26)
+TOKEN_AT = 21
+
+
+def planned(name, step):
+    chunk = jnp.int32(-1)
+    for at, which in PLAN[name].items():
+        chunk = jnp.where(step == at, which, chunk)
+    return chunk
+
+
+def back_kernel(
+    n, pair_ref, back_ref, len_ref, grad_ref, keep_ref, mix_ref, lse_ref, left_ref, right_ref,
+    sums_ref, resid_ref, qkv_ref,
+    total_ref, token_ref, small_out,
+    grad_in, g_all, q_sum, k_sum, v_sum, blocks_out, blocks_in, w_qkv, right_all,
+    pair_out, pair_in, x_out, x_in, y_out, y_in, y_keep, near_out, near_in, near_keep,
+    far_out, far_in, far_keep, s_out, s_in,
+    grad_sem, block_sem, own_sem, pair_sem, x_sem, y_sem, near_sem, far_sem, own_z_sem, wide_sem,
+    last_sem, s_sem,
 ):
     low, wide = jnp.bfloat16, jnp.float32
     ctx = lax.axis_index("ctx")
     fsdp = lax.axis_index("fsdp")
     z, y = ctx // 2, lax.rem(ctx, 2)
+    odd, upper = lax.rem(z, 2), z // 2
     x, core = fsdp // 2, lax.rem(fsdp, 2)
     sibling = {"fsdp": 2 * x + 1 - core}
     across = {"fsdp": 2 * (1 - x) + core}
     beside = {"ctx": 2 * z + 1 - y}
-    along = [{"ctx": 2 * lax.rem(z + k, 4) + y} for k in (1, 2, 3)]
+    near = {"ctx": 2 * (2 * upper + 1 - odd) + y}
+    far = {"ctx": 2 * (2 * (1 - upper) + odd) + y}
+    mine = 2 * odd + upper
     greet(ring_peers(n) + [sibling, across])
-    blocks = exchange_copies(n, blocks_ref, blocks_in, block_sem)
-    for cp in blocks:
+    grads = exchange_copies(n, grad_ref, grad_in, grad_sem)
+    for cp in grads:
         cp.start()
-    own = pltpu.make_async_copy(blocks_ref.at[ctx], blocks_in.at[ctx], own_sem)
-    own.start()
+    own_grad = own_copy(grad_ref, grad_in, own_sem.at[0])
+    own_grad.start()
+    load = pltpu.make_async_copy(qkv_ref, w_qkv, own_sem.at[1])
+    load.start()
+    blocks = exchange_copies(n, blocks_out, blocks_in, block_sem)
+    own = own_copy(blocks_out, blocks_in, own_sem.at[2])
     right_all[3:] = right_ref[...]
+    k_sum[...] = jnp.zeros_like(k_sum)
+    v_sum[...] = jnp.zeros_like(v_sum)
+    chunks = keep_ref.shape[0] // 2
+
+    def attend_some(first, last):
+        for c in range(first, last):
+            attend_back(
+                c, len_ref[0], y, keep_ref, g_all, mix_ref, lse_ref, q_sum, k_sum, v_sum
+            )
+
+    def attend_step(t):
+        @pl.when(t == ATTEND_AT[0])
+        def _():
+            own_grad.wait()
+            for cp in grads:
+                cp.wait_recv()
+            for b in range(2 * chunks):
+                g_all[b] = grad_in[back_ref[b]]
+            attend_some(0, chunks // 2)
+
+        @pl.when(t == ATTEND_AT[1])
+        def _():
+            attend_some(chunks // 2, chunks - 2)
+
+        @pl.when(t == ATTEND_AT[2])
+        def _():
+            attend_some(chunks - 2, chunks)
+            for s in range(2 * chunks):
+                place = pair_ref[s]
+                blocks_out[s] = jnp.concatenate(
+                    [q_sum[place], k_sum[place], v_sum[place]], axis=1
+                ).astype(low)
+            for cp in blocks:
+                cp.start()
+            own.start()
+
+    def slot(c):
+        return lax.rem(c, 4)
 
     def pair_copy(c):
         return remote(pair_out.at[lax.rem(c, 2)], pair_in.at[c], pair_sem, (c,), sibling)
@@ -1020,231 +1079,293 @@
         return remote(x_out.at[c], x_in.at[c], x_sem, (c,), across)
 
     def y_copy(c):
-        return remote(y_out.at[c], y_in.at[c], y_sem, (c,), beside)
-
-    def z_copy(c, k):
-        return remote(
-            z_out.at[c, lax.rem(z + k, 4)], z_in.at[c, k - 1], z_sem, (c, k - 1), along[k - 1]
-        )
-
-    def spread_copy(c, k):
-        piece = total_ref.at[c, y, z]
-        return remote(piece, piece, spread_sem, (c, k - 1), along[k - 1])
+        return remote(y_out.at[slot(c)], y_in.at[c], y_sem, (c,), beside)
+
+    def near_copy(c):
+        return remote(near_out.at[slot(c)], near_in.at[c], near_sem, (c,), near)
+
+    def far_copy(c):
+        return remote(far_out.at[slot(c)], far_in.at[c], far_sem, (c,), far)
+
+    def own_z_copy(c):
+        piece = total_ref.at[c, y, mine]
+        return remote(piece, piece, own_z_sem, (c,), far)
+
+    def wide_copy(c):
+        piece = total_ref.at[c, y, two(odd)]
+        return remote(piece, piece, wide_sem, (c,), near)
 
     def last_copy(c):
-        return remote(total_ref.at[c, y], total_ref.at[c, y], last_sem, (c,), beside)
+        piece = total_ref.at[c, y]
+        return remote(piece, piece, last_sem, (c,), beside)
+
+    def reuse(copy, c, slots):
+        @pl.when(c >= slots)
+        def _():
+            copy(c - slots).wait_send()
 
     def partial(c, shard):
         left, right = sum_sources(c)
-        return jnp.dot(left_ref[left, shard], right_all[right], preferred_element_type=jnp.float32)
+        return dot_nn(left_ref[left, shard], right_all[right])
 
     def stage_pair(c):
-        @pl.when(c >= 2)
-        def _():
-            pair_copy(c - 2).wait_send()
-
+        reuse(pair_copy, c, 2)
         for side in range(2):
             pair_out[lax.rem(c, 2), side] = partial(c, 2 * side + 1 - core).astype(low)
         pair_copy(c).start()
 
     def stage_x(c):
         pair_copy(c).wait_recv()
-        x_out[c] = (
-            partial(c, 2 * (1 - x) + core) + pair_in[c, 1 - x].astype(jnp.float32)
-        ).astype(low)
+        x_out[c] = (partial(c, 2 * (1 - x) + core) + pair_in[c, 1 - x].astype(wide)).astype(low)
         x_copy(c).start()
-        first_sum[lax.rem(c, 2)] = partial(c, 2 * x + core) + pair_in[c, x].astype(jnp.float32)
 
     def stage_y(c):
+        mine_sum = partial(c, 2 * x + core) + pair_in[c, x].astype(wide)
         x_copy(c).wait_recv()
-        total = first_sum[lax.rem(c, 2)] + x_in[c].astype(jnp.float32)
-        here, there = total[:, :384], total[:, 384:]
-        y_out[c] = jnp.where(y == 0, there, here).astype(low)
+        total = mine_sum + x_in[c].astype(wide)
+        first, second = total[:, :384], total[:, 384:]
+        reuse(y_copy, c, 4)
+        y_out[slot(c)] = jnp.where(y == 0, second, first).astype(low)
         y_copy(c).start()
-        half_sum[lax.rem(c, 2)] = jnp.where(y == 0, here, there)
-
-    def stage_z(c):
+        y_keep[slot(c)] = jnp.where(y == 0, first, second)
+
+    def stage_near(c):
         y_copy(c).wait_recv()
-        total = half_sum[lax.rem(c, 2)] + y_in[c].astype(jnp.float32)
-        z_out[c] = total.astype(low).reshape(4, 48, 384)
-        for k in (1, 2, 3):
-            z_copy(c, k).start()
-        half_sum[lax.rem(c, 2)] = total
-
-    def stage_spread(c):
-        total = half_sum[lax.rem(c, 2), pl.ds(pl.multiple_of(48 * z, 48), 48)]
-        for k in (1, 2, 3):
-            z_copy(c, k).wait_recv()
-            total = total + z_in[c, k - 1].astype(jnp.float32)
-        total_ref[c, y, z] = total.astype(low)
-        for k in (1, 2, 3):
-            spread_copy(c, k).start()
+        total = y_keep[slot(c)] + y_in[c].astype(wide)
+        first, second = total[:96], total[96:]
+        reuse(near_copy, c, 4)
+        near_out[slot(c)] = jnp.where(odd == 0, second, first).astype(low)
+        near_copy(c).start()
+        near_keep[slot(c)] = jnp.where(odd == 0, first, second)
+
+    def stage_far(c):
+        near_copy(c).wait_recv()
+        total = near_keep[slot(c)] + near_in[c].astype(wide)
+        first, second = total[:48], total[48:]
+        reuse(far_copy, c, 4)
+        far_out[slot(c)] = jnp.where(upper == 0, second, first).astype(low)
+        far_copy(c).start()
+        far_keep[slot(c)] = jnp.where(upper == 0, first, second)
+
+    def stage_own(c):
+        far_copy(c).wait_recv()
+        total_ref[c, y, mine] = (far_keep[slot(c)] + far_in[c].astype(wide)).astype(low)
+        own_z_copy(c).start()
+
+    def stage_wide(c):
+        own_z_copy(c).wait_recv()
+        wide_copy(c).start()
 
     def stage_last(c):
-        for k in (1, 2, 3):
-            spread_copy(c, k).wait_recv()
+        wide_copy(c).wait_recv()
         last_copy(c).start()
 
-    stages = [stage_pair, stage_x, stage_y, stage_z, stage_spread, stage_last]
-    order = [0, 1, 4, 2, 3, 5]
-
     def small_step(t):
-        send_pair = remote(s_pair.at[0], s_pair.at[1], s_sem, (0,), sibling)
-        send_x = remote(s_x_out, s_x, s_sem, (1,), across)
-        send_y = remote(s_y_out, s_y, s_sem, (2,), beside)
-        send_z = [remote(s_z_out, s_z.at[k], s_sem, (3 + k,), along[k]) for k in range(3)]
-
-        @pl.when(t == 0)
+        peers = [sibling, across, beside, near, far]
+        copies = [
+            remote(s_out.at[k], s_in.at[k], s_sem, (k,), peer) for k, peer in enumerate(peers)
+        ]
+
+        @pl.when(t == JOIN_AT)
         def _():
             own.wait()
             for cp in blocks:
                 cp.wait_recv()
             for part in range(3):
                 right_all[part] = join_pairs(
-                    lambda peer: blocks_in[peer, :, part * 2 * HEAD_DIM : (part + 1) * 2 * HEAD_DIM]
+                    lambda peer: both(blocks_in, peer)[:, part * BLK : (part + 1) * BLK]
                 )
-            s_pair[0] = sums_ref[...]
-            s_pair[0, ROW_BQ : ROW_BQ + 1] = column_sum(right_all[0].astype(wide))
-            s_pair[0, ROW_BV : ROW_BV + 1] = column_sum(right_all[2].astype(wide))
-            send_pair.start()
-
-        @pl.when(t == 1)
+            s_out[0] = sums_ref[...]
+            s_out[0, ROW_BQ : ROW_BQ + 1] = column_sum(right_all[0].astype(wide))
+            s_out[0, ROW_BV : ROW_BV + 1] = column_sum(right_all[2].astype(wide))
+            copies[0].start()
+
+        for k in range(1, 5):
+
+            @pl.when(t == SMALL_AT[k])
+            def _():
+                copies[k - 1].wait()
+                s_out[k] = s_out[k - 1] + s_in[k - 1]
+                copies[k].start()
+
+        @pl.when(t == SMALL_AT[5])
         def _():
-            send_pair.wait()
-            s_x_out[...] = s_pair[0] + s_pair[1]
-            send_x.start()
-            width = resid_ref.shape[1]
-            token_ref[...] = resid_ref[...] + sum(
-                dot_nt(right_all[part], w_qkv_ref[:, part * width : (part + 1) * width])
-                for part in range(3)
-            )
-
-        @pl.when(t == 2)
-        def _():
-            send_x.wait()
-            s_y_out[...] = s_x_out[...] + s_x[...]
-            send_y.start()
-
-        @pl.when(t == 3)
-        def _():
-            send_y.wait()
-            s_z_out[...] = s_y_out[...] + s_y[...]
-            for cp in send_z:
-                cp.start()
-
-        @pl.when(t == 4)
-        def _():
-            for cp in send_z:
-                cp.wait()
-            total = jnp.zeros(s_z_out.shape, wide)
-            for spot in range(4):
-                k = lax.rem(spot - z + 4, 4)
-                other = s_z[jnp.where(k == 0, 0, 3 - k)]
-                total = total + jnp.where(k == 0, s_z_out[...], other)
+            copies[4].wait()
+            total = s_out[4] + s_in[4]
             quarter = total.shape[1] // 4
             cuts = [slice(f * quarter, (f + 1) * quarter) for f in range(4)]
             pick = lambda choices: sum(
                 jnp.where(fsdp == f, choice, 0.0) for f, choice in enumerate(choices)
             )
+            small_out[...] = jnp.zeros_like(small_out)
             small_out[:8] = pick([total[:8, cut] for cut in cuts])
             line = pick([total[ROW_BI + f : ROW_BI + f + 1] for f in range(4)])
             for j, cut in enumerate(cuts):
                 small_out[8 + j : 9 + j] = line[:, cut]
 
-    def slot(t, carry):
-        small_step(t - 9)
-        for index in order:
-            c = t - index
-
-            @pl.when((c >= 0) & (c < PARTS))
+        @pl.when(t == TOKEN_AT)
+        def _():
+            load.wait()
+            width = resid_ref.shape[1]
+            token_ref[...] = resid_ref[...] + sum(
+                dot_nt(
+                    right_all[part],
+                    w_qkv[:, :, part * width : (part + 1) * width].reshape(width, width),
+                )
+                for part in range(3)
+            )
+
+    stages = [
+        ("pair", stage_pair),
+        ("x", stage_x),
+        ("last", stage_last),
+        ("wide", stage_wide),
+        ("own", stage_own),
+        ("far", stage_far),
+        ("near", stage_near),
+        ("y", stage_y),
+    ]
+
+    def step(t, carry):
+        attend_step(t)
+        small_step(t)
+        for name, stage in stages:
+            c = planned(name, t)
+
+            @pl.when(c >= 0)
             def _():
-                stages[index](c)
+                stage(c)
 
         return carry
 
-    lax.fori_loop(0, PARTS + 5, slot, 0)
+    lax.fori_loop(0, STEPS, step, 0)
 
     def drain(c, carry):
         x_copy(c).wait_send()
-        y_copy(c).wait_send()
-        for k in (1, 2, 3):
-            z_copy(c, k).wait_send()
-            spread_copy(c, k).wait_send()
+        own_z_copy(c).wait_send()
+        wide_copy(c).wait_send()
         last_copy(c).wait()
         return carry
 
     lax.fori_loop(0, PARTS, drain, 0)
+    for c in range(PARTS - 4, PARTS):
+        y_copy(c).wait_send()
+        near_copy(c).wait_send()
+        far_copy(c).wait_send()
     for c in (PARTS - 2, PARTS - 1):
         pair_copy(c).wait_send()
-    for cp in blocks:
+    for cp in grads + blocks:
         cp.wait_send()
 
-    def panel(c, target, rows_at, cols_at):
-        for half in range(2):
-            for spot in range(4):
-                target[
-                    rows_at + 48 * spot : rows_at + 48 * spot + 48,
-                    cols_at + 384 * half : cols_at + 384 * half + 384,
-                ] = total_ref[c, half, spot]
-
-    for k in range(4):
-        panel(k, back_out, 192 * k, 0)
-        panel(4 + k, in_out, 0, 768 * k)
-    panel(8, out_out, 0, 0)
-    for k in range(3):
-        panel(9 + k, qkv_out, 0, 768 * k)
-
-
-def sum_all(left, right, sums, blocks, w_qkv, resid, name):
-    n = blocks.shape[0]
+
+def back(pairing, order, lengths, grad, keep, mix, lse, left, right, sums, resid, qkv_full, name):
+    blocks = keep.shape[0]
+    n = blocks // 2
     low, wide = jnp.bfloat16, jnp.float32
     dma = pltpu.SemaphoreType.DMA
     shape = jax.ShapeDtypeStruct
-    small = pltpu.VMEM(sums.shape, wide)
+    total = pltpu.VMEM((blocks, BLK, BLK), wide)
     return pl.pallas_call(
-        functools.partial(sum_kernel, n),
+        functools.partial(back_kernel, n),
         out_shape=(
+            shape((PARTS, 2, 4, 48, 384), low),
             shape(resid.shape, wide),
-            shape((192, 2304), low),
-            shape((192, 768), low),
-            shape((192, 3072), low),
-            shape((768, 768), low),
             shape((16, 192), wide),
         ),
-        in_specs=[vmem()] * 6,
-        out_specs=(vmem(),) * 6,
+        in_specs=[smem()] * 3 + [vmem()] * 8 + [pl.BlockSpec(memory_space=pltpu.HBM)],
+        out_specs=(vmem(),) * 3,
         scratch_shapes=[
-            pltpu.VMEM(blocks.shape, low),
+            pltpu.VMEM(grad.shape, low),
+            pltpu.VMEM(grad.shape, low),
+            total, total, total,
+            pltpu.VMEM(keep.shape, low),
+            pltpu.VMEM(keep.shape, low),
+            pltpu.VMEM(qkv_full.shape, low),
             pltpu.VMEM((9,) + right.shape[1:], low),
-            pltpu.VMEM((PARTS, 2, 4, 48, 384), low),
             pltpu.VMEM((2, 2, 192, 768), low),
             pltpu.VMEM((PARTS, 2, 192, 768), low),
             pltpu.VMEM((PARTS, 192, 768), low),
             pltpu.VMEM((PARTS, 192, 768), low),
-            pltpu.VMEM((2, 192, 768), wide),
+            pltpu.VMEM((4, 192, 384), low),
             pltpu.VMEM((PARTS, 192, 384), low),
-            pltpu.VMEM((PARTS, 192, 384), low),
-            pltpu.VMEM((2, 192, 384), wide),
-            pltpu.VMEM((PARTS, 4, 48, 384), low),
-            pltpu.VMEM((PARTS, 3, 48, 384), low),
-            pltpu.VMEM((2,) + sums.shape, wide),
-            small, small, small, small, small,
-            pltpu.VMEM((3,) + sums.shape, wide),
+            pltpu.VMEM((4, 192, 384), wide),
+            pltpu.VMEM((4, 96, 384), low),
+            pltpu.VMEM((PARTS, 96, 384), low),
+            pltpu.VMEM((4, 96, 384), wide),
+            pltpu.VMEM((4, 48, 384), low),
+            pltpu.VMEM((PARTS, 48, 384), low),
+            pltpu.VMEM((4, 48, 384), wide),
+            pltpu.VMEM((5,) + sums.shape, wide),
+            pltpu.VMEM((5,) + sums.shape, wide),
             dma((2, n)),
-            dma,
-            dma((2, PARTS)),
-            dma((2, PARTS)),
-            dma((2, PARTS)),
-            dma((2, PARTS, 3)),
-            dma((2, PARTS, 3)),
-            dma((2, PARTS)),
-            dma((2, 6)),
+            dma((2, n)),
+            dma((3,)),
+        ]
+        + [dma((2, PARTS))] * 8
+        + [dma((2, 5))],
+        compiler_params=pltpu.CompilerParams(
+            collective_id=name, has_side_effects=True, vmem_limit_bytes=61 << 20
+        ),
+        name="back",
+    )(pairing, order, lengths, grad, keep, mix, lse, left, right, sums, resid, qkv_full)
+
+
+def finish_kernel(
+    total_ref, small_ref, output_ref, token_ref,
+    output_out, token_out, qkv_out, out_out, in_out, back_out, *refs
+):
+    lines, (stage, sems) = refs[:9], refs[9:]
+    copies = [
+        pltpu.make_async_copy(output_ref, output_out, sems.at[PARTS]),
+        pltpu.make_async_copy(token_ref, token_out, sems.at[PARTS + 1]),
+    ]
+    targets = [back_out.at[192 * k : 192 * k + 192] for k in range(4)]
+    targets += [in_out.at[:, 768 * k : 768 * k + 768] for k in range(4)]
+    targets += [out_out]
+    targets += [qkv_out.at[:, 768 * k : 768 * k + 768] for k in range(3)]
+    for cp in copies:
+        cp.start()
+    for c, target in enumerate(targets):
+        for half in range(2):
+            for spot in range(4):
+                stage[c, 48 * spot : 48 * spot + 48, 384 * half : 384 * half + 384] = total_ref[
+                    c, half, spot
+                ].astype(jnp.float32)
+        copies.append(pltpu.make_async_copy(stage.at[c], target, sems.at[c]))
+        copies[-1].start()
+    for i in range(8):
+        lines[i][...] = small_ref[i]
+    for j in range(4):
+        lines[8][192 * j : 192 * j + 192] = small_ref[ROW_BI + j]
+    for cp in copies:
+        cp.wait()
+
+
+def finish(total, small, output, token):
+    shape = jax.ShapeDtypeStruct
+    wide = jnp.float32
+    hbm = pl.BlockSpec(memory_space=pltpu.HBM)
+    return pl.pallas_call(
+        finish_kernel,
+        out_shape=(
+            shape(output.shape, wide),
+            shape(token.shape, wide),
+            shape((192, 2304), wide),
+            shape((192, 768), wide),
+            shape((192, 3072), wide),
+            shape((768, 768), wide),
+        )
+        + (shape((192,), wide),) * 8
+        + (shape((768,), wide),),
+        in_specs=[vmem(), vmem(), hbm, hbm],
+        out_specs=(hbm,) * 6 + (vmem(),) * 9,
+        scratch_shapes=[
+            pltpu.VMEM((PARTS, 192, 768), wide),
+            pltpu.SemaphoreType.DMA((PARTS + 2,)),
         ],
-        compiler_params=pltpu.CompilerParams(
-            collective_id=name, has_side_effects=True, vmem_limit_bytes=60 << 20
-        ),
-        name="sum_all",
-    )(left, right, sums, blocks, w_qkv, resid)
+        compiler_params=pltpu.CompilerParams(vmem_limit_bytes=32 << 20),
+        name="finish",
+    )(total, small, output, token)
 
 
 def on_device_spread(
@@ -1272,43 +1393,30 @@
     n = pairing.shape[0] // 2
     inputs = tokens[0]
     vectors = [bias_q, bias_v, bias_out, ln1_gain, ln1_bias, bias_back, ln2_gain, ln2_bias]
-    small = jnp.concatenate([jnp.stack(vectors), bias_in.reshape(4, -1)]).astype(jnp.float32)
-    small = jnp.pad(small, ((0, 16 - small.shape[0]), (0, 0)))
+    part = width // 4
+    vectors += [bias_in[j * part : (j + 1) * part] for j in range(4)]
+    line = lax.broadcasted_iota(jnp.int32, (16, part), 0)
+    small = jnp.zeros((16, part), jnp.float32)
+    for i, vector in enumerate(vectors):
+        small = jnp.where(line == i, vector.astype(jnp.float32)[None, :], small)
     packed, lines, qkv_full, out_full, in_full = project(
         inputs, small, w_qkv, w_out, w_in, n, 0
     )
     spot = lax.rem(lax.axis_index("ctx"), 2).astype(jnp.int32).reshape(1)
-    mixed_out, keep, mix, lse = attend(
-        pairing, lengths, spot, packed.reshape(-1, half, 6 * HEAD_DIM)
-    )
-    output, grad_in, left, right, resid, sums = layer(
-        pairing, lengths, mixed_out.reshape(-1, rows, 2 * HEAD_DIM), inputs, cotangent[0],
-        lines, out_full, in_full, w_back, 1,
-    )
-    grad_blocks = attend_back(
-        pairing, lengths, spot, keep, grad_in.reshape(-1, half, 2 * HEAD_DIM), mix, lse
-    )
-    token_grad, qkv_sum, out_sum, in_sum, back_sum, small = sum_all(
-        left, right, sums, grad_blocks.reshape(-1, rows, 6 * HEAD_DIM), qkv_full.reshape(width, -1),
-        resid, 2
-    )
-    wide = lambda value: value.astype(jnp.float32)
+    mixed, keep, mix, lse, order = attend(pairing, lengths, spot, packed)
+    output, grad, left, right, resid, sums = layer(
+        pairing, lengths, mixed, inputs, cotangent[0], lines, out_full, in_full, w_back, 1
+    )
+    total, token_grad, small_sum = back(
+        pairing, order, lengths, grad, keep, mix, lse, left, right, sums, resid, qkv_full, 2
+    )
+    (
+        output, token_grad, qkv_sum, out_sum, in_sum, back_sum,
+        bq, bv, bo, g1, s1, bb, g2, s2, bi,
+    ) = finish(total, small_sum, output, token_grad)
     return (
-        output[None],
-        token_grad[None],
-        wide(qkv_sum),
-        small[ROW_BQ],
-        small[ROW_BV],
-        wide(out_sum),
-        small[ROW_BO],
-        small[ROW_G1],
-        small[ROW_S1],
-        wide(in_sum),
-        small[ROW_BI : ROW_BI + 4].reshape(-1),
-        wide(back_sum),
-        small[ROW_BB],
-        small[ROW_G2],
-        small[ROW_S2],
+        output[None], token_grad[None], qkv_sum, bq, bv, out_sum, bo, g1, s1, in_sum, bi,
+        back_sum, bb, g2, s2,
     )
 
 

time: 316 us -> 289 us (0.915)
  Pallas kernels: 283 us -> 263 us
  local copies, waits for them, and re-layouts: 24.3 us -> 17.8 us
    pallas_call x3, Pallas kernels: 221 us -> 210 us  [the longest x1 144 us: back(): pl.pallas_call(functools.partial(back_kernel, n), out_shape=(shape((PARTS...]
    pallas_call x1, Pallas kernels: 54.8 us -> 45.1 us  [layer(): pl.pallas_call(functools.partial(layer_kernel, n), out_shape=(shape((coun...]
    another operation x8 -> x0, local copies, waits for them, and re-layouts: 5.26 us -> none  [on_device_spread(): jnp.stack(vectors)]
    unnamed x38 -> x36, local copies, waits for them, and re-layouts: 15.2 us -> 17.8 us
    convert_element_type x4 -> x9, other arithmetic: 6.47 us -> 6.16 us  [on_device_spread(): small = jnp.where(line == i, vector.astype(jnp.float32)[None, :], small)]
where the time goes in v5:
time: 289 us
  Pallas kernels  263 us (91%)
  local copies, waits for them, and re-layouts  17.8 us (6%)
  other arithmetic  6.29 us (2%)
    pallas_call x1, Pallas kernels, back(): pl.pallas_call(functools.partial(back_kernel, n), out_shape=(shape((PARTS...  144 us
    pallas_call x1, Pallas kernels, project(): pl.pallas_call(functools.partial(project_kernel, n), out_shape=(shape((2...  62 us
    pallas_call x1, Pallas kernels, layer(): pl.pallas_call(functools.partial(layer_kernel, n), out_shape=(shape((coun...  45.1 us
    unnamed x36, local copies, waits for them, and re-layouts  17.8 us
    pallas_call x1, Pallas kernels, attend(): pl.pallas_call(functools.partial(attend_kernel, chunks), out_shape=(jax.S...  7.85 us
    convert_element_type x9, other arithmetic, on_device_spread(): small = jnp.where(line == i, vector.astype(jnp.float32)[None, :], small)  6.16 us

profile of v5, /device:TPU:0, one launch (start us, length us, event | category | flops | bytes accessed | tf_op | source)
XLA Modules:
  0.0 288.8 jit_solution(1784901525695870766)
XLA Ops:
  0.6 0.0 copy-start.16
  1.3 0.7 convert_element_type.47
  2.0 0.7 convert_element_type.46
  2.6 0.7 convert_element_type.45
  3.3 0.7 convert_element_type.44
  3.9 0.7 convert_element_type.43
  4.6 0.7 convert_element_type.42
  5.3 0.7 convert_element_type.41
  5.9 0.7 convert_element_type.40
  6.6 0.9 slice_convert_fusion.3
  7.5 0.1 select_select_fusion.small_ref
  7.6 0.0 copy-start.3
  7.7 1.0 copy-done.3
  8.6 0.0 copy-start.6
  8.6 1.3 copy-done.6
  9.9 0.0 copy-start.8
  9.9 1.2 copy-done.8
  11.1 0.0 copy-start.12
  11.1 1.0 copy-done.12
  12.0 62.0 %project.1 = (bf16[16,128,384]{2,1,0:T(8,128)(2,1)S(1)}, f32[16,768]{1,0:T(8,128)S(1)}, bf16[4,192,2304]{2,1,0:T(8,128)(2,1)S(1)}, bf16[4,192,768]{2,1,0:T(8,128)(2,1)S(1)}, bf16[4,192,3072]{2,1,0:T(8,128)(2,1)S(1)}) custom-call(bf16[256,768]{1,0:T(8,128)(2,1)S(1)} %bitcast.6, f32[16,192]{1,0:T(8,128)S(1)} %select_select_fusion.small_ref, ...), custom_call_target="tpu_custom_call" | custom-call | tf_op jit(solution)/shard_map/project/pallas_call | solution.py:942
  74.1 0.0 copy-start
  74.1 2.1 copy-done
  76.2 0.0 copy-start.2
  76.2 1.8 copy-done.2
  78.0 0.0 copy-start.5
  78.0 1.0 copy-done.5
  79.1 0.0 copy-start.13
  79.1 0.6 copy-done.13
  79.7 0.0 copy-done.16
  79.7 7.9 %attend.1 = (bf16[16,128,128]{2,1,0:T(8,128)(2,1)S(1)}, bf16[16,128,384]{2,1,0:T(8,128)(2,1)S(1)}, f32[8,128,256]{2,1,0:T(8,128)S(1)}, f32[8,1,384]{2,1,0:T(1,128)S(1)}, s32[16]{0:T(128)S(1)}) custom-call(s32[16]{0:T(128)S(1)} %copy-done.16, s32[1]{0:T(128)S(6)} %copy.32.len_ref, s32[1]{0:T(128)} %bitcast.spot_ref, ...), custom_call_target="tpu_custom_call" | custom-call | tf_op jit(solution)/shard_map/attend/pallas_call | solution.py:569
  87.5 0.0 copy-start.4
  87.6 1.1 copy-done.4
  88.7 0.0 copy-start.7
  88.7 1.0 copy-done.7
  89.7 0.0 copy-start.11
  89.7 0.8 copy-done.11
  90.5 0.0 copy-start.15
  90.5 0.6 copy-done.15
  91.1 0.5 copy-done.17
  91.6 45.1 %layer.1 = (f32[256,768]{1,0:T(8,128)}, bf16[16,128,128]{2,1,0:T(8,128)(2,1)}, bf16[7,4,192,256]{3,2,1,0:T(8,128)(2,1)}, bf16[6,256,768]{2,1,0:T(8,128)(2,1)}, f32[256,768]{1,0:T(8,128)}, /*index=5*/f32[16,768]{1,0:T(8,128)}) custom-call(s32[16]{0:T(128)} %pair_ref.5, s32[1]{0:T(128)S(6)} %copy.32.len_ref, bf16[16,128,128]{2,1,0:T(8,128)(2,1)} %copy-done.11, ...), custom_call_target="tpu_custom_call" | custom-call | tf_op jit(solution)/shard_map/layer/pallas_call | solution.py:799
  136.7 0.0 copy-start.9
  136.7 143.9 %back.1 = (bf16[12,2,4,48,384]{4,3,2,1,0:T(8,128)(2,1)}, f32[256,768]{1,0:T(8,128)}, f32[16,192]{1,0:T(8,128)}) custom-call(s32[16]{0:T(128)} %pair_ref.5, s32[16]{0:T(128)} %copy-done.17, s32[1]{0:T(128)S(6)} %copy.32.len_ref, bf16[16,128,128]{2,1,0:T(8,128)(2,1)} %get-tuple-element.55.grad_ref, bf16[16,128,384]{2,1,0:T(8,128)(2,1)} %copy-done.4, ...), custom_call_target="tpu_custom_call" | custom-call | tf_op jit(solution)/shard_map/back/pallas_call | solution.py:1268
  280.6 0.0 copy-done.9
  280.6 0.0 copy-start.1
  280.6 2.0 copy-done.1
  282.6 1.1 copy-done.10
  283.8 0.7 copy-done.14
  284.5 4.1 %finish.1 = (f32[256,768]{1,0:T(8,128)}, f32[256,768]{1,0:T(8,128)}, f32[192,2304]{1,0:T(8,128)}, f32[192,768]{1,0:T(8,128)}, f32[192,3072]{1,0:T(8,128)}, /*ind...) custom-call(bf16[12,2,4,48,384]{4,3,2,1,0:T(8,128)(2,1)S(1)} %copy-d, ...), custom_call_target="tpu_custom_call" | custom-call | tf_op jit(solution)/shard_map/finish/pallas_call | solution.py:1348
  (9 shorter events, 0.0 us)
Async XLA Ops:
  0.6 79.0 %copy-start.16 = (s32[16]{0:T(128)S(1)}, s32[16]{0:T(128)}, u32[]{:S(2)}) copy-start(s32[16]{0:T(128)} %pair_ref.5) | copy-start | bytes 196
  7.6 1.0 copy-start.3
  8.6 1.3 copy-start.6
  9.9 1.2 copy-start.8
  11.1 1.0 copy-start.12
  74.1 2.1 copy-start
  76.2 1.8 copy-start.2
  78.0 1.0 copy-start.5
  79.1 0.6 copy-start.13
  87.5 1.1 copy-start.4
  88.7 1.0 copy-start.7
  89.7 0.8 copy-start.11
  90.5 0.6 copy-start.15
  91.1 0.5 copy-start.17
  136.7 143.9 %copy-start.9 = (f32[256,768]{1,0:T(8,128)S(1)}, f32[256,768]{1,0:T(8,128)}, u32[]{:S(2)}) copy-start(f32[256,768]{1,0:T(8,128)} %get-tuple-element.66.output_ref) | copy-start | bytes 2359300
  280.6 2.0 copy-start.1
  282.6 1.1 copy-start.10
  283.8 0.7 copy-start.14

commit v6 on v5

--- a/solution.py
+++ b/solution.py
@@ -434,52 +434,42 @@
     return lax.broadcasted_iota(jnp.int32, shape, 1) < 64
 
 
-def attend_kernel(
-    chunks, pair_ref, len_ref, spot_ref, in_ref, out_ref, keep_ref, mix_ref, lse_ref, back_ref
-):
-    length = len_ref[0]
-    spot = spot_ref[0]
-    blocks = 2 * chunks
-    for s in range(blocks):
-        keep_ref[pair_ref[s]] = in_ref[s]
-        back_ref[pair_ref[s]] = s
+def spot_of(pair_ref, place):
+    found = jnp.int32(0)
+    for s in range(pair_ref.shape[0]):
+        found = jnp.where(pair_ref[s] == place, s, found)
+    return found
+
+
+def attend(c, length, spot, keep_ref, mix_ref, lse_ref, turned_ref):
     left = low_lanes((256, BLK))
-    left_half = left[:BLK]
-    for c in range(chunks):
-        keys = 256 * (c + 1)
-        own = keep_ref[2 * c : 2 * c + 2, :, :BLK].reshape(256, BLK)
-        shared = keep_ref[2 * c + spot, :, :BLK]
-        zero = jnp.zeros((), jnp.bfloat16)
-        query = jnp.concatenate(
-            [jnp.where(left, own, zero), jnp.where(left_half, zero, shared)], axis=0
-        ) * jnp.bfloat16(0.125)
-        key = keep_ref[: 2 * c + 2, :, BLK : 2 * BLK].reshape(keys, BLK)
-        value = keep_ref[: 2 * c + 2, :, 2 * BLK :].reshape(keys, BLK)
-        scores = mask_scores(
-            lax.dot_general(key, query, (((1,), (1,)), ((), ())), preferred_element_type=jnp.float32),
-            c, spot, length, 0, True,
-        )
-        top = jnp.max(scores, axis=0, keepdims=True)
-        probs = jnp.exp(scores - top)
-        total = jnp.sum(probs, axis=0, keepdims=True)
-        summed = lax.dot_general(
-            value, probs.astype(jnp.bfloat16), (((0,), (0,)), ((), ())),
-            preferred_element_type=jnp.float32,
-        ) / total
-        lse_ref[c] = top + jnp.log(total)
-        part = summed[64:, 256:]
-        none = jnp.zeros_like(part)
-        first = jnp.where(spot == 0, part, none)
-        second = jnp.where(spot == 0, none, part)
-        mixed = jnp.concatenate(
-            [summed[:64, :256], jnp.concatenate([first, second], axis=1)], axis=0
-        )
-        mix_ref[c] = mixed
-    for s in range(blocks):
-        place = pair_ref[s]
-        c = place // 2
-        piece = mix_ref[c, :, pl.ds(pl.multiple_of((place % 2) * BLK, BLK), BLK)]
-        out_ref[s] = jnp.transpose(piece).astype(jnp.bfloat16)
+    zero = jnp.zeros((), jnp.bfloat16)
+    keys = 256 * (c + 1)
+    own = keep_ref[2 * c : 2 * c + 2, :, :BLK].reshape(256, BLK)
+    shared = keep_ref[2 * c + spot, :, :BLK]
+    query = jnp.concatenate(
+        [jnp.where(left, own, zero), jnp.where(left[:BLK], zero, shared)], axis=0
+    ) * jnp.bfloat16(0.125)
+    key = keep_ref[: 2 * c + 2, :, BLK : 2 * BLK].reshape(keys, BLK)
+    value = keep_ref[: 2 * c + 2, :, 2 * BLK :].reshape(keys, BLK)
+    scores = mask_scores(dot_nt(key, query), c, spot, length, 0, True)
+    top = jnp.max(scores, axis=0, keepdims=True)
+    probs = jnp.exp(scores - top)
+    total = jnp.sum(probs, axis=0, keepdims=True)
+    summed = lax.dot_general(
+        value, probs.astype(jnp.bfloat16), (((0,), (0,)), ((), ())),
+        preferred_element_type=jnp.float32,
+    ) / total
+    lse_ref[c] = top + jnp.log(total)
+    part = summed[64:, 256:]
+    none = jnp.zeros_like(part)
+    first = jnp.where(spot == 0, part, none)
+    second = jnp.where(spot == 0, none, part)
+    mixed = jnp.concatenate([summed[:64, :256], jnp.concatenate([first, second], axis=1)], axis=0)
+    mix_ref[c] = mixed
+    turned_ref[2 * c : 2 * c + 2] = (
+        jnp.transpose(mixed).astype(jnp.bfloat16).reshape(2, BLK, BLK)
+    )
 
 
 def mask_scores(scores, c, spot, length, start, edged):
@@ -563,25 +553,6 @@
     return pl.BlockSpec(memory_space=pltpu.VMEM)
 
 
-def attend(pairing, lengths, spot, packed):
-    blocks = packed.shape[0]
-    chunks = blocks // 2
-    return pl.pallas_call(
-        functools.partial(attend_kernel, chunks),
-        out_shape=(
-            jax.ShapeDtypeStruct((blocks, BLK, BLK), jnp.bfloat16),
-            jax.ShapeDtypeStruct((blocks, BLK, 3 * BLK), jnp.bfloat16),
-            jax.ShapeDtypeStruct((chunks, BLK, 256), jnp.float32),
-            jax.ShapeDtypeStruct((chunks, 1, 384), jnp.float32),
-            jax.ShapeDtypeStruct((blocks,), jnp.int32),
-        ),
-        in_specs=[smem(), smem(), smem(), vmem()],
-        out_specs=(vmem(), vmem(), vmem(), vmem(), smem()),
-        compiler_params=pltpu.CompilerParams(vmem_limit_bytes=48 << 20),
-        name="attend",
-    )(pairing, lengths, spot, packed)
-
-
 MESH = pl.DeviceIdType.MESH
 
 
@@ -675,157 +646,6 @@
 (ROW_BQ, ROW_BV, ROW_BO, ROW_G1, ROW_S1, ROW_BB, ROW_G2, ROW_S2, ROW_BI) = range(9)
 
 
-def layer_kernel(
-    n, pair_ref, len_ref, mixed_ref, tokens_ref, cot_ref, rows_ref, out_full, in_full, back_ref,
-    output_ref, grad_ref, left_ref, right_ref, resid_ref, sums_ref,
-    mixed_in, active, slope, w_out, w_in, w_back, in_sem, back_sem, own_sem,
-):
-    low, wide = jnp.bfloat16, jnp.float32
-    ctx = lax.axis_index("ctx")
-    sums_ref[...] = jnp.zeros_like(sums_ref)
-    fsdp = lax.axis_index("fsdp")
-    x, core = fsdp // 2, lax.rem(fsdp, 2)
-    greet(ring_peers(n) + chip_peers())
-    copies = exchange_copies(n, mixed_ref, mixed_in, in_sem)
-    for cp in copies:
-        cp.start()
-    back_shards = gather_copies(back_ref, w_back, back_sem, 0)
-    for step in (0, 1):
-        back_shards[step].start()
-    width = tokens_ref.shape[1]
-    count = w_in.shape[0]
-    loads = [
-        pltpu.make_async_copy(out_full, w_out, own_sem.at[2]),
-        pltpu.make_async_copy(back_ref, w_back.at[fsdp], own_sem.at[3]),
-    ] + [
-        pltpu.make_async_copy(
-            in_full.at[:, :, t * width : (t + 1) * width], w_in.at[t], own_sem.at[4 + t]
-        )
-        for t in range(count)
-    ]
-    for cp in loads:
-        cp.start()
-    own = own_copy(mixed_ref, mixed_in, own_sem.at[0])
-    own.start()
-    row = lambda i: rows_ref[i : i + 1, :]
-    tokens = tokens_ref[...]
-    left_ref[0] = jnp.transpose(tokens).reshape(4, -1, 2 * BLK)
-    spots = lax.broadcasted_iota(jnp.int32, (2 * BLK, 1), 0)
-    place = jnp.where(
-        spots < BLK,
-        pair_ref[2 * ctx] * BLK + spots,
-        pair_ref[2 * ctx + 1] * BLK + spots - BLK,
-    )
-    valid = place < len_ref[0]
-    own.wait()
-    for cp in copies:
-        cp.wait_recv()
-
-    attended = join_pairs(lambda peer: both(mixed_in, peer))
-    loads[0].wait()
-    resid_one = (
-        tokens.astype(wide)
-        + dot_nn(attended, w_out[...].reshape(width, width))
-        + row(ROW_BO)
-    )
-    unit_one, scale_one = unit_of(resid_one)
-    hidden = unit_one * row(ROW_G1) + row(ROW_S1)
-    hidden_low = hidden.astype(low)
-    resid_two = hidden + row(ROW_BB)
-    for cp in loads[2:]:
-        cp.wait()
-    order = [fsdp, 2 * x + 1 - core, 2 * (1 - x) + core, 2 * (1 - x) + 1 - core]
-    for step, t in enumerate(order):
-        bias = rows_ref[pl.ds(ROW_BI + t, 1), :]
-        upper = dot_nn(hidden_low, w_in[t].reshape(width, width)) + bias
-        share = 0.5 * (1.0 + lax.erf(upper * (0.5**0.5)))
-        slope[t] = share + upper * (jnp.exp(-0.5 * upper * upper) * (2 * math.pi) ** -0.5)
-        some = (upper * share).astype(low)
-        active[t] = some
-        if step == 0:
-            loads[1].wait()
-        elif step == 1:
-            back_shards[1].wait_recv()
-        elif step == 2:
-            back_shards[0].wait_recv()
-            back_shards[2].start()
-        else:
-            back_shards[2].wait_recv()
-        resid_two = resid_two + dot_nn(some, w_back[t])
-    unit_two, scale_two = unit_of(resid_two)
-    output_ref[...] = jnp.where(valid, unit_two * row(ROW_G2) + row(ROW_S2), 0.0)
-    grad_y = jnp.where(valid, cot_ref[...].astype(wide), 0.0)
-    sums_ref[ROW_G2 : ROW_G2 + 1, :] = column_sum(grad_y * unit_two)
-    sums_ref[ROW_S2 : ROW_S2 + 1, :] = column_sum(grad_y)
-    grad_resid_two = unit_back(unit_two, scale_two, grad_y * row(ROW_G2))
-    grad_mixed = grad_resid_two.astype(low)
-    right_ref[5] = grad_mixed
-    sums_ref[ROW_BB : ROW_BB + 1, :] = column_sum(grad_mixed.astype(wide))
-    grad_hidden = grad_resid_two
-    for t in range(count):
-        grad_upper = (dot_nt(grad_mixed, w_back[t]) * slope[t]).astype(low)
-        right_ref[1 + t] = grad_upper
-        sums_ref[ROW_BI + t : ROW_BI + t + 1, :] = column_sum(grad_upper.astype(wide))
-        grad_hidden = grad_hidden + dot_nt(grad_upper, w_in[t].reshape(width, width))
-    sums_ref[ROW_G1 : ROW_G1 + 1, :] = column_sum(grad_hidden * unit_one)
-    sums_ref[ROW_S1 : ROW_S1 + 1, :] = column_sum(grad_hidden)
-    grad_resid_one = unit_back(unit_one, scale_one, grad_hidden * row(ROW_G1))
-    resid_ref[...] = grad_resid_one
-    grad_branch = grad_resid_one.astype(low)
-    right_ref[0] = grad_branch
-    sums_ref[ROW_BO : ROW_BO + 1, :] = column_sum(grad_branch.astype(wide))
-    grad_attended = dot_nt(grad_branch, w_out[...].reshape(width, width)).astype(low)
-    for peer in range(n):
-        grad_ref[2 * peer : 2 * peer + 2] = pair_of(grad_attended, peer).reshape(2, BLK, BLK)
-    left_ref[1] = jnp.transpose(attended).reshape(4, -1, 2 * BLK)
-    left_ref[2] = jnp.transpose(hidden_low).reshape(4, -1, 2 * BLK)
-    for f in range(4):
-        turned = jnp.transpose(active[f])
-        for r in range(4):
-            left_ref[3 + r, f] = turned[r * width // 4 : (r + 1) * width // 4]
-    for cp in copies:
-        cp.wait_send()
-    for cp in back_shards:
-        cp.wait_send()
-
-
-def layer(pairing, lengths, mixed, tokens, cotangent, rows, out_full, in_full, w_back, name):
-    n = mixed.shape[0] // 2
-    count, width = tokens.shape
-    low, wide = jnp.bfloat16, jnp.float32
-    dma = pltpu.SemaphoreType.DMA
-    shape = jax.ShapeDtypeStruct
-    anywhere = pl.BlockSpec(memory_space=pltpu.HBM)
-    return pl.pallas_call(
-        functools.partial(layer_kernel, n),
-        out_shape=(
-            shape((count, width), wide),
-            shape(mixed.shape, low),
-            shape((7, 4, width // 4, count), low),
-            shape((6, count, width), low),
-            shape((count, width), wide),
-            shape((16, width), wide),
-        ),
-        in_specs=[smem(), smem()] + [vmem()] * 4 + [anywhere] * 3,
-        out_specs=(vmem(),) * 6,
-        scratch_shapes=[
-            pltpu.VMEM(mixed.shape, low),
-            pltpu.VMEM((4, count, width), low),
-            pltpu.VMEM((4, count, width), wide),
-            pltpu.VMEM(out_full.shape, low),
-            pltpu.VMEM((4, 4, width // 4, width), low),
-            pltpu.VMEM((4,) + w_back.shape, low),
-            dma((2, n)),
-            dma((2, 1, 3)),
-            dma((8,)),
-        ],
-        compiler_params=pltpu.CompilerParams(
-            collective_id=name, has_side_effects=True, vmem_limit_bytes=56 << 20
-        ),
-        name="layer",
-    )(pairing, lengths, mixed, tokens, cotangent, rows, out_full, in_full, w_back)
-
-
 def gather_copies(src, full, sems, index):
     fsdp = lax.axis_index("fsdp")
     x, core = fsdp // 2, lax.rem(fsdp, 2)
@@ -844,125 +664,324 @@
     return [{"fsdp": 2 * x + 1 - core}, {"fsdp": 2 * (1 - x) + core}]
 
 
-def project_kernel(
-    n, tokens_ref, small_ref, qkv_ref, out_ref, in_ref,
-    packed_ref, rows_ref, qkv_full, out_full, in_full,
-    qkv_here, small_here, send, sems, own_sem, block_sem,
+def split_gather(src, full, sems, pieces):
+    ctx, fsdp = lax.axis_index("ctx"), lax.axis_index("fsdp")
+    z, y = ctx // 2, lax.rem(ctx, 2)
+    x, core = fsdp // 2, lax.rem(fsdp, 2)
+    sibling, across = {"fsdp": 2 * x + 1 - core}, {"fsdp": 2 * (1 - x) + core}
+    beside = {"ctx": 2 * z + 1 - y}
+    other = 2 * (1 - x) + core
+    count = src.shape[0] // (2 * pieces)
+
+    def rows(half, p):
+        return pl.ds(pl.multiple_of((half * pieces + p) * count, count), count)
+
+    cross, side, on, off = [], [], [], []
+    for p in range(pieces):
+        here, there = rows(y, p), rows(1 - y, p)
+        moved = full.at[other, here]
+        late = full.at[other, there]
+        cross.append(remote(src.at[here], full.at[fsdp, here], sems, (0, p), across))
+        side.append(remote(moved, moved, sems, (1, p), beside))
+        on.append(remote(moved, moved, sems, (2, p), sibling))
+        off.append(remote(late, late, sems, (3, p), sibling))
+    whole = remote(src, full.at[fsdp], sems, (4, 0), sibling)
+    return cross, side, on, off, whole
+
+
+def front_kernel(
+    n, pair_ref, len_ref, *refs
 ):
+    vectors, refs = refs[:9], refs[9:]
+    (
+        tokens_ref, cot_ref, qkv_src, out_src, in_src, back_src,
+        output_ref, grad_ref, left_ref, right_ref, resid_ref, sums_ref,
+        keep_ref, mix_ref, lse_ref, qkv_ref,
+        small_out, small, rows_ref, token_buf, cot, w_qkv, w_out, w_in, w_back, send, packed, keep, mix,
+        lse, turned, mixed_out, mixed_in, active, slope, output, grad_out, left, right, resid, sums,
+        small_sem, qkv_sem, gather_sem, send_sem, in_sem, own_sem, load_sem, ship_sem,
+    ) = refs
     low, wide = jnp.bfloat16, jnp.float32
-    fsdp = lax.axis_index("fsdp")
-    greet(ring_peers(n) + chip_peers())
-    qkv = gather_copies(qkv_ref, qkv_here, sems, 0)
-    small = gather_copies(small_ref, small_here, sems, 1)
-    for step in (0, 1):
-        small[step].start()
-        qkv[step].start()
-    locals_ = [
-        pltpu.make_async_copy(src, dst, own_sem.at[i])
+    ctx, fsdp = lax.axis_index("ctx"), lax.axis_index("fsdp")
+    x, core = fsdp // 2, lax.rem(fsdp, 2)
+    spot = lax.rem(ctx, 2)
+    width = token_buf.shape[1]
+    count = in_src.shape[1] // width
+    pieces = 3
+    loads = [
+        pltpu.make_async_copy(src, dst, load_sem.at[i])
         for i, (src, dst) in enumerate(
             [
-                (qkv_ref, qkv_here.at[fsdp]),
-                (small_ref, small_here.at[fsdp]),
-                (out_ref, out_full.at[fsdp]),
-                (in_ref, in_full.at[fsdp]),
+                (tokens_ref, token_buf),
+                (cot_ref, cot),
+                (qkv_src, w_qkv.at[fsdp]),
+                (out_src, w_out.at[fsdp]),
+                (in_src, w_in.at[fsdp]),
+                (back_src, w_back.at[fsdp]),
             ]
         )
     ]
-    for cp in locals_:
+    cot_load = loads[1]
+    for cp in loads[:3]:
         cp.start()
-    small[0].wait_recv()
-    small[2].start()
-    qkv[0].wait_recv()
-    qkv[2].start()
-    later = [gather_copies(out_ref, out_full, sems, 2), gather_copies(in_ref, in_full, sems, 3)]
+    part = width // 4
+    small_out[...] = jnp.zeros_like(small_out)
+    for i in range(8):
+        small_out[i : i + 1] = vectors[i][...].astype(wide).reshape(1, part)
+    inner_bias = vectors[8][...].astype(wide).reshape(1, -1)
+    for j in range(4):
+        small_out[8 + j : 9 + j] = inner_bias[:, j * part : (j + 1) * part]
+    greet(ring_peers(n) + chip_peers())
+    smalls = gather_copies(small_out, small, small_sem, 0)
+    cross, side, on, off, whole = split_gather(qkv_src, w_qkv, qkv_sem, pieces)
     for step in (0, 1):
-        for cps in later:
-            cps[step].start()
-    for cps in (small, qkv):
-        cps[1].wait_recv()
-        cps[2].wait_recv()
-    locals_[0].wait()
-    locals_[1].wait()
-    keep = pltpu.make_async_copy(qkv_here, qkv_full, own_sem.at[4])
-    keep.start()
+        smalls[step].start()
+    for cp in cross:
+        cp.start()
+    whole.start()
+    for cp in loads[3:]:
+        cp.start()
+    shards = [
+        gather_copies(src, full, gather_sem, i)
+        for i, (src, full) in enumerate([(out_src, w_out), (in_src, w_in), (back_src, w_back)])
+    ]
+    back_shards = shards[2]
+    small[fsdp] = small_out[...]
+    smalls[0].wait_recv()
+    smalls[2].start()
+    for p in range(pieces):
+        cross[p].wait_recv()
+        side[p].start()
+        on[p].start()
+    for cps in shards:
+        cps[0].start()
+    for cps in shards:
+        cps[1].start()
+    for p in range(pieces):
+        side[p].wait_recv()
+        off[p].start()
+    loads[0].wait()
+    tokens = token_buf[...]
+    left[0] = jnp.transpose(tokens).reshape(4, -1, 2 * BLK)
+    smalls[1].wait_recv()
+    smalls[2].wait_recv()
     for f in range(4):
-        width = small_here.shape[2]
-        cols = slice(f * width, (f + 1) * width)
-        rows_ref[:8, cols] = small_here[f, :8]
+        cols = slice(f * part, (f + 1) * part)
+        rows_ref[:8, cols] = small[f, :8]
         for j in range(4):
-            rows_ref[ROW_BI + f : ROW_BI + f + 1, j * width : (j + 1) * width] = small_here[
+            rows_ref[ROW_BI + f : ROW_BI + f + 1, j * part : (j + 1) * part] = small[
                 f, 8 + j : 9 + j
             ]
     rows_ref[12:] = jnp.zeros_like(rows_ref[12:])
-    tokens = tokens_ref[...]
-    width = tokens.shape[1]
+    row = lambda i: rows_ref[i : i + 1, :]
+    whole.wait_recv()
+    for p in range(pieces):
+        on[p].wait_recv()
+        off[p].wait_recv()
+    loads[2].wait()
+
     half = width // 2
     for g in range(2):
         parts = []
-        for part, bias in ((0, ROW_BQ), (1, None), (2, ROW_BV)):
-            at = part * width + g * half
-            value = dot_nn(tokens, qkv_here[:, :, at : at + half].reshape(width, half))
+        for which, bias in ((0, ROW_BQ), (1, None), (2, ROW_BV)):
+            at = which * width + g * half
+            value = dot_nn(tokens, w_qkv[:, :, at : at + half].reshape(width, half))
             if bias is not None:
                 value = value + rows_ref[bias : bias + 1, g * half : (g + 1) * half]
             parts.append(value.astype(low))
-        for spot in range(n // 2):
-            peer = g * n // 2 + spot
+        for at in range(n // 2):
+            peer = g * n // 2 + at
             send[2 * peer : 2 * peer + 2] = jnp.concatenate(
-                [pair_of(value, spot) for value in parts], axis=1
+                [pair_of(value, at) for value in parts], axis=1
             ).reshape(2, BLK, -1)
-    blocks = exchange_copies(n, send, packed_ref, block_sem)
-    for cp in blocks:
+    sends = exchange_copies(n, send, packed, send_sem)
+    for cp in sends:
         cp.start()
-    own = own_copy(send, packed_ref, own_sem.at[5])
-    own.start()
-    for cps in later:
+    own_send = own_copy(send, packed, own_sem.at[0])
+    own_send.start()
+    shipped = []
+
+    def ship(src, dst):
+        cp = pltpu.make_async_copy(src, dst, ship_sem.at[len(shipped)])
+        cp.start()
+        shipped.append(cp)
+
+    ship(w_qkv, qkv_ref)
+    spots = lax.broadcasted_iota(jnp.int32, (2 * BLK, 1), 0)
+    place = jnp.where(
+        spots < BLK,
+        pair_ref[2 * ctx] * BLK + spots,
+        pair_ref[2 * ctx + 1] * BLK + spots - BLK,
+    )
+    valid = place < len_ref[0]
+    own_send.wait()
+    for cp in sends:
+        cp.wait_recv()
+    for cps in shards[:2]:
         cps[0].wait_recv()
         cps[2].start()
-    own.wait()
-    keep.wait()
-    locals_[2].wait()
-    locals_[3].wait()
-    for cp in blocks:
+
+    for b in range(2 * n):
+        keep[b] = packed[spot_of(pair_ref, b)]
+    ship(keep, keep_ref)
+    for c in range(n):
+        attend(c, len_ref[0], spot, keep, mix, lse, turned)
+    for s in range(2 * n):
+        mixed_out[s] = turned[pair_ref[s]]
+    copies = exchange_copies(n, mixed_out, mixed_in, in_sem)
+    for cp in copies:
+        cp.start()
+    own_mixed = own_copy(mixed_out, mixed_in, own_sem.at[1])
+    own_mixed.start()
+    ship(mix, mix_ref)
+    ship(lse, lse_ref)
+    sums[...] = jnp.zeros_like(sums)
+    for cp in loads[3:]:
         cp.wait()
-    for cps in later:
-        cps[0].wait_send()
-        cps[1].wait()
-        cps[2].wait()
-    for cps in (small, qkv):
+    for cps in shards[:2]:
+        cps[1].wait_recv()
+        cps[2].wait_recv()
+    own_mixed.wait()
+    for cp in copies:
+        cp.wait_recv()
+    back_shards[0].wait_recv()
+    back_shards[2].start()
+    back_shards[1].wait_recv()
+
+    attended = join_pairs(lambda peer: both(mixed_in, peer))
+    resid_one = (
+        tokens.astype(wide)
+        + dot_nn(attended, w_out[...].reshape(width, width))
+        + row(ROW_BO)
+    )
+    unit_one, scale_one = unit_of(resid_one)
+    hidden = unit_one * row(ROW_G1) + row(ROW_S1)
+    hidden_low = hidden.astype(low)
+    resid_two = hidden + row(ROW_BB)
+    cut = lambda t: pl.ds(pl.multiple_of(t * width, width), width)
+    order = [fsdp, 2 * x + 1 - core, 2 * (1 - x) + core, 2 * (1 - x) + 1 - core]
+    for step, t in enumerate(order):
+        bias = rows_ref[pl.ds(ROW_BI + t, 1), :]
+        upper = dot_nn(hidden_low, w_in[:, :, cut(t)].reshape(width, width)) + bias
+        share = 0.5 * (1.0 + lax.erf(upper * (0.5**0.5)))
+        slope[t] = share + upper * (jnp.exp(-0.5 * upper * upper) * (2 * math.pi) ** -0.5)
+        some = (upper * share).astype(low)
+        active[t] = some
+        if step == 3:
+            back_shards[2].wait_recv()
+        resid_two = resid_two + dot_nn(some, w_back[t])
+    unit_two, scale_two = unit_of(resid_two)
+    output[...] = jnp.where(valid, unit_two * row(ROW_G2) + row(ROW_S2), 0.0)
+    cot_load.wait()
+    grad_y = jnp.where(valid, cot[...].astype(wide), 0.0)
+    sums[ROW_G2 : ROW_G2 + 1, :] = column_sum(grad_y * unit_two)
+    sums[ROW_S2 : ROW_S2 + 1, :] = column_sum(grad_y)
+    grad_resid_two = unit_back(unit_two, scale_two, grad_y * row(ROW_G2))
+    grad_mixed = grad_resid_two.astype(low)
+    right[5] = grad_mixed
+    sums[ROW_BB : ROW_BB + 1, :] = column_sum(grad_mixed.astype(wide))
+    grad_hidden = grad_resid_two
+    for t in range(count):
+        grad_upper = (dot_nt(grad_mixed, w_back[t]) * slope[t]).astype(low)
+        right[1 + t] = grad_upper
+        sums[ROW_BI + t : ROW_BI + t + 1, :] = column_sum(grad_upper.astype(wide))
+        grad_hidden = grad_hidden + dot_nt(grad_upper, w_in[:, :, cut(t)].reshape(width, width))
+    sums[ROW_G1 : ROW_G1 + 1, :] = column_sum(grad_hidden * unit_one)
+    sums[ROW_S1 : ROW_S1 + 1, :] = column_sum(grad_hidden)
+    grad_resid_one = unit_back(unit_one, scale_one, grad_hidden * row(ROW_G1))
+    resid[...] = grad_resid_one
+    grad_branch = grad_resid_one.astype(low)
+    right[0] = grad_branch
+    sums[ROW_BO : ROW_BO + 1, :] = column_sum(grad_branch.astype(wide))
+    ship(resid, resid_ref)
+    ship(right, right_ref)
+    ship(sums, sums_ref)
+    grad_attended = dot_nt(grad_branch, w_out[...].reshape(width, width)).astype(low)
+    for peer in range(n):
+        grad_out[2 * peer : 2 * peer + 2] = pair_of(grad_attended, peer).reshape(2, BLK, BLK)
+    ship(grad_out, grad_ref)
+    left[1] = jnp.transpose(attended).reshape(4, -1, 2 * BLK)
+    left[2] = jnp.transpose(hidden_low).reshape(4, -1, 2 * BLK)
+    for f in range(4):
+        turned = jnp.transpose(active[f])
+        for r in range(4):
+            left[3 + r, f] = turned[r * width // 4 : (r + 1) * width // 4]
+    ship(output, output_ref)
+    ship(left, left_ref)
+    for cps in [smalls] + shards:
         for cp in cps:
             cp.wait_send()
-
-
-def project(tokens, small, w_qkv, w_out, w_in, n, name):
+    for cp in cross + side + on + off + [whole] + sends + copies:
+        cp.wait_send()
+    for cp in shipped:
+        cp.wait()
+
+
+def front(pairing, lengths, vectors, tokens, cotangent, w_qkv, w_out, w_in, w_back, n, name):
+    count, width = tokens.shape
     low, wide = jnp.bfloat16, jnp.float32
     dma = pltpu.SemaphoreType.DMA
     shape = jax.ShapeDtypeStruct
-    count, width = tokens.shape
-    anywhere = pl.BlockSpec(memory_space=pltpu.HBM)
+    hbm = pl.BlockSpec(memory_space=pltpu.HBM)
+    vec = pltpu.VMEM((16, width // 4), wide)
+    results = [
+        ((count, width), wide),
+        ((2 * n, BLK, BLK), low),
+        ((7, 4, width // 4, count), low),
+        ((6, count, width), low),
+        ((count, width), wide),
+        ((16, width), wide),
+        ((2 * n, BLK, 3 * BLK), low),
+        ((n, BLK, 2 * BLK), wide),
+        ((n, 1, 3 * BLK), wide),
+        ((4,) + w_qkv.shape, low),
+    ]
+    output, grad, left, right, resid, sums, keep, mix, lse, qkv = [pltpu.VMEM(*r) for r in results]
     return pl.pallas_call(
-        functools.partial(project_kernel, n),
-        out_shape=(
-            shape((2 * n, BLK, 6 * HEAD_DIM), low),
-            shape((16, width), wide),
-            shape((4,) + w_qkv.shape, low),
-            shape((4,) + w_out.shape, low),
-            shape((4,) + w_in.shape, low),
-        ),
-        in_specs=[vmem(), vmem()] + [anywhere] * 3,
-        out_specs=(vmem(), vmem()) + (anywhere,) * 3,
+        functools.partial(front_kernel, n),
+        out_shape=tuple(shape(*r) for r in results),
+        in_specs=[smem(), smem()] + [vmem()] * 9 + [hbm] * 6,
+        out_specs=(hbm,) * 10,
         scratch_shapes=[
-            pltpu.VMEM((4,) + w_qkv.shape, low),
-            pltpu.VMEM((4,) + small.shape, wide),
-            pltpu.VMEM((2 * n, BLK, 6 * HEAD_DIM), low),
-            dma((2, 4, 3)),
+            vec,
+            pltpu.VMEM((4, 16, width // 4), wide),
+            pltpu.VMEM((16, width), wide),
+            pltpu.VMEM((count, width), low),
+            pltpu.VMEM((count, width), low),
+            qkv,
+            pltpu.VMEM((4,) + w_out.shape, low),
+            pltpu.VMEM((4,) + w_in.shape, low),
+            pltpu.VMEM((4,) + w_back.shape, low),
+            keep,
+            keep,
+            keep,
+            mix,
+            lse,
+            grad,
+            grad,
+            grad,
+            pltpu.VMEM((4, count, width), low),
+            pltpu.VMEM((4, count, width), wide),
+            output,
+            grad,
+            left,
+            right,
+            resid,
+            sums,
+            dma((2, 1, 3)),
+            dma((2, 5, 3)),
+            dma((2, 3, 3)),
+            dma((2, n)),
+            dma((2, n)),
+            dma((2,)),
             dma((6,)),
-            dma((2, n)),
+            dma((10,)),
         ],
         compiler_params=pltpu.CompilerParams(
-            collective_id=name, has_side_effects=True, vmem_limit_bytes=40 << 20
+            collective_id=name, has_side_effects=True, vmem_limit_bytes=62 << 20
         ),
-        name="project",
-    )(tokens, small, w_qkv, w_out, w_in)
+        name="front",
+    )(pairing, lengths, *vectors, tokens, cotangent, w_qkv, w_out, w_in, w_back)
 
 
 PARTS = 12
@@ -1001,7 +1020,7 @@
 
 
 def back_kernel(
-    n, pair_ref, back_ref, len_ref, grad_ref, keep_ref, mix_ref, lse_ref, left_ref, right_ref,
+    n, pair_ref, len_ref, grad_ref, keep_ref, mix_ref, lse_ref, left_ref, right_ref,
     sums_ref, resid_ref, qkv_ref,
     total_ref, token_ref, small_out,
     grad_in, g_all, q_sum, k_sum, v_sum, blocks_out, blocks_in, w_qkv, right_all,
@@ -1050,7 +1069,7 @@
             for cp in grads:
                 cp.wait_recv()
             for b in range(2 * chunks):
-                g_all[b] = grad_in[back_ref[b]]
+                g_all[b] = grad_in[spot_of(pair_ref, b)]
             attend_some(0, chunks // 2)
 
         @pl.when(t == ATTEND_AT[1])
@@ -1258,7 +1277,7 @@
         cp.wait_send()
 
 
-def back(pairing, order, lengths, grad, keep, mix, lse, left, right, sums, resid, qkv_full, name):
+def back(pairing, lengths, grad, keep, mix, lse, left, right, sums, resid, qkv_full, name):
     blocks = keep.shape[0]
     n = blocks // 2
     low, wide = jnp.bfloat16, jnp.float32
@@ -1272,7 +1291,7 @@
             shape(resid.shape, wide),
             shape((16, 192), wide),
         ),
-        in_specs=[smem()] * 3 + [vmem()] * 8 + [pl.BlockSpec(memory_space=pltpu.HBM)],
+        in_specs=[smem()] * 2 + [vmem()] * 8 + [pl.BlockSpec(memory_space=pltpu.HBM)],
         out_specs=(vmem(),) * 3,
         scratch_shapes=[
             pltpu.VMEM(grad.shape, low),
@@ -1307,36 +1326,49 @@
             collective_id=name, has_side_effects=True, vmem_limit_bytes=61 << 20
         ),
         name="back",
-    )(pairing, order, lengths, grad, keep, mix, lse, left, right, sums, resid, qkv_full)
+    )(pairing, lengths, grad, keep, mix, lse, left, right, sums, resid, qkv_full)
 
 
 def finish_kernel(
     total_ref, small_ref, output_ref, token_ref,
     output_out, token_out, qkv_out, out_out, in_out, back_out, *refs
 ):
-    lines, (stage, sems) = refs[:9], refs[9:]
+    lines, (total, small, through, stage, sems) = refs[:9], refs[9:]
+    arrive = [
+        pltpu.make_async_copy(total_ref.at[c], total.at[c], sems.at[PARTS + 2 + c])
+        for c in range(PARTS)
+    ] + [
+        pltpu.make_async_copy(small_ref, small, sems.at[2 * PARTS + 2]),
+        pltpu.make_async_copy(output_ref, through.at[0], sems.at[2 * PARTS + 3]),
+        pltpu.make_async_copy(token_ref, through.at[1], sems.at[2 * PARTS + 4]),
+    ]
+    for cp in arrive:
+        cp.start()
     copies = [
-        pltpu.make_async_copy(output_ref, output_out, sems.at[PARTS]),
-        pltpu.make_async_copy(token_ref, token_out, sems.at[PARTS + 1]),
+        pltpu.make_async_copy(through.at[0], output_out, sems.at[PARTS]),
+        pltpu.make_async_copy(through.at[1], token_out, sems.at[PARTS + 1]),
     ]
     targets = [back_out.at[192 * k : 192 * k + 192] for k in range(4)]
     targets += [in_out.at[:, 768 * k : 768 * k + 768] for k in range(4)]
     targets += [out_out]
     targets += [qkv_out.at[:, 768 * k : 768 * k + 768] for k in range(3)]
-    for cp in copies:
-        cp.start()
     for c, target in enumerate(targets):
+        arrive[c].wait()
         for half in range(2):
             for spot in range(4):
-                stage[c, 48 * spot : 48 * spot + 48, 384 * half : 384 * half + 384] = total_ref[
+                stage[c, 48 * spot : 48 * spot + 48, 384 * half : 384 * half + 384] = total[
                     c, half, spot
                 ].astype(jnp.float32)
         copies.append(pltpu.make_async_copy(stage.at[c], target, sems.at[c]))
         copies[-1].start()
+    for k in range(2):
+        arrive[PARTS + 1 + k].wait()
+        copies[k].start()
+    arrive[PARTS].wait()
     for i in range(8):
-        lines[i][...] = small_ref[i]
+        lines[i][...] = small[i]
     for j in range(4):
-        lines[8][192 * j : 192 * j + 192] = small_ref[ROW_BI + j]
+        lines[8][192 * j : 192 * j + 192] = small[ROW_BI + j]
     for cp in copies:
         cp.wait()
 
@@ -1357,13 +1389,16 @@
         )
         + (shape((192,), wide),) * 8
         + (shape((768,), wide),),
-        in_specs=[vmem(), vmem(), hbm, hbm],
+        in_specs=[hbm] * 4,
         out_specs=(hbm,) * 6 + (vmem(),) * 9,
         scratch_shapes=[
+            pltpu.VMEM(total.shape, total.dtype),
+            pltpu.VMEM(small.shape, wide),
+            pltpu.VMEM((2,) + token.shape, wide),
             pltpu.VMEM((PARTS, 192, 768), wide),
-            pltpu.SemaphoreType.DMA((PARTS + 2,)),
+            pltpu.SemaphoreType.DMA((2 * PARTS + 5,)),
         ],
-        compiler_params=pltpu.CompilerParams(vmem_limit_bytes=32 << 20),
+        compiler_params=pltpu.CompilerParams(vmem_limit_bytes=62 << 20),
         name="finish",
     )(total, small, output, token)
 
@@ -1387,28 +1422,15 @@
     ln2_gain,
     ln2_bias,
 ):
-    rows = tokens.shape[1]
-    half = rows // 2
-    width = tokens.shape[2]
     n = pairing.shape[0] // 2
     inputs = tokens[0]
     vectors = [bias_q, bias_v, bias_out, ln1_gain, ln1_bias, bias_back, ln2_gain, ln2_bias]
-    part = width // 4
-    vectors += [bias_in[j * part : (j + 1) * part] for j in range(4)]
-    line = lax.broadcasted_iota(jnp.int32, (16, part), 0)
-    small = jnp.zeros((16, part), jnp.float32)
-    for i, vector in enumerate(vectors):
-        small = jnp.where(line == i, vector.astype(jnp.float32)[None, :], small)
-    packed, lines, qkv_full, out_full, in_full = project(
-        inputs, small, w_qkv, w_out, w_in, n, 0
-    )
-    spot = lax.rem(lax.axis_index("ctx"), 2).astype(jnp.int32).reshape(1)
-    mixed, keep, mix, lse, order = attend(pairing, lengths, spot, packed)
-    output, grad, left, right, resid, sums = layer(
-        pairing, lengths, mixed, inputs, cotangent[0], lines, out_full, in_full, w_back, 1
+    vectors += [bias_in]
+    output, grad, left, right, resid, sums, keep, mix, lse, qkv_full = front(
+        pairing, lengths, vectors, inputs, cotangent[0], w_qkv, w_out, w_in, w_back, n, 0
     )
     total, token_grad, small_sum = back(
-        pairing, order, lengths, grad, keep, mix, lse, left, right, sums, resid, qkv_full, 2
+        pairing, lengths, grad, keep, mix, lse, left, right, sums, resid, qkv_full, 1
     )
     (
         output, token_grad, qkv_sum, out_sum, in_sum, back_sum,

time: 289 us -> 247 us (0.85)
  Pallas kernels: 263 us -> 245 us
  local copies, waits for them, and re-layouts: 17.8 us -> 0 us
  other arithmetic: 6.29 us -> 0 us
    pallas_call x3 -> x1, Pallas kernels: 115 us -> 88.7 us  [front(): pl.pallas_call(functools.partial(front_kernel, n), out_shape=tuple((shape...]
    unnamed x36 -> x0, local copies, waits for them, and re-layouts: 17.8 us -> none
    pallas_call x1, Pallas kernels: 144 us -> 151 us  [back(): pl.pallas_call(functools.partial(back_kernel, n), out_shape=(shape((PARTS...]
    convert_element_type x9 -> x0, other arithmetic: 6.16 us -> none  [on_device_spread(): small = jnp.where(line == i, vector.astype(jnp.float32)[None, :], small)]
where the time goes in v6:
time: 247 us; the launch traced here: 246 us
  Pallas kernels  245 us (99%)
    pallas_call x1, Pallas kernels, back(): pl.pallas_call(functools.partial(back_kernel, n), out_shape=(shape((PARTS...  151 us
    pallas_call x1, Pallas kernels, front(): pl.pallas_call(functools.partial(front_kernel, n), out_shape=tuple((shape...  88.7 us
    pallas_call x1, Pallas kernels, finish(): pl.pallas_call(finish_kernel, out_shape=(shape(output.shape, wide), shape...  5.53 us

profile of v6, /device:TPU:0, one launch (start us, length us, event | category | flops | bytes accessed | tf_op | source)
XLA Modules:
  0.0 246.4 jit_solution(1164524515264546747)
XLA Ops:
  1.3 88.7 %front.1 = (f32[256,768]{1,0:T(8,128)}, bf16[16,128,128]{2,1,0:T(8,128)(2,1)}, bf16[7,4,192,256]{3,2,1,0:T(8,128)(2,1)}, bf16[6,256,768]{2,1,0:T(8,128)(2,1)}, f...) custom-call(s32[16]{0:T(128)} %pair_ref.3, ...), custom_call_target="tpu_custom_call" | custom-call | tf_op jit(solution)/shard_map/front/pallas_call | solution.py:940
  90.0 150.7 %back.1 = (bf16[12,2,4,48,384]{4,3,2,1,0:T(8,128)(2,1)}, f32[256,768]{1,0:T(8,128)}, f32[16,192]{1,0:T(8,128)}) custom-call(s32[16]{0:T(128)} %pair_ref.3, s32[1]{0:T(128)S(6)} %copy.32.len_ref, bf16[16,128,128]{2,1,0:T(8,128)(2,1)} %get-tuple-element.43.grad_ref, bf16[16,128,384]{2,1,0:T(8,128)(2,1)} %get-tuple-element.44.keep_ref, ...), custom_call_target="tpu_custom_call" | custom-call | tf_op jit(solution)/shard_map/back/pallas_call | solution.py:1287
  240.7 5.5 %finish.1 = (f32[256,768]{1,0:T(8,128)}, f32[256,768]{1,0:T(8,128)}, f32[192,2304]{1,0:T(8,128)}, f32[192,768]{1,0:T(8,128)}, f32[192,3072]{1,0:T(8,128)}, /*ind...) custom-call(bf16[12,2,4,48,384]{4,3,2,1,0:T(8,128)(2,1)} %get-tuple-, ...), custom_call_target="tpu_custom_call" | custom-call | tf_op jit(solution)/shard_map/finish/pallas_call | solution.py:1380
